TPU v7x, 32 devices: a whole 2x2x4 slice. The times are simulated.
32 devices in a mesh: grid: 4 (over y, x), pair: 8 (over z, core).
Axes of the slice: x: 2, y: 2, z: 4, core: 2. Of those that a mesh axis runs over, the one named last changes fastest.
Arguments:
- amplitudes: bfloat16 [8, 1536, 1536], P('pair', 'grid'), may hold values from -6 to 6
- packed_factor: bfloat16 [512, 512], P(('grid', 'pair')), may hold values from -0.25 to 0.25
- screen: int32 [4, 4], replicated, may hold values from 0 to 11, as said below
- metric: bfloat16 [512, 512], P(None, 'grid'), may hold values from -6 to 6
- occ_energy: float32 [300], replicated, may hold values from -1.5 to -0.3
- vir_energy: float32 [1536], replicated, may hold values from 0.2 to 3
- pair_occ: int32 [8, 2], P('pair'), may hold values from 0 to 299
Outputs:
- update: float32 [8, 1536, 1536], P('pair', 'grid')
Inputs may be any that keep to these rules, and one draw needn't show every extreme that they name: `screen`: each row lists 4 different virtual tiles.
All inputs are finite; a program needn't handle non-finite values.
Results may differ from a plain program's by a relative error of at most 0.0049.
Values may be sent and summed in bfloat16 or wider, within the bound.
No kernel may reach another device: no remote copies, remote signals or barrier semaphores. Data moves between devices by JAX's collectives and lax.ppermute only.
A program may use at most 64 MiB of HBM per device.

v0:
```python
import jax
import jax.numpy as jnp
from jax import lax
from jax.sharding import PartitionSpec as P


def widened_factor(packed, screen, number_of_tiles):
    block_count, slots = screen.shape
    tile_rows = packed.shape[1] // slots
    block_rows = packed.shape[0] // block_count
    onehot = (
        screen[:, :, None] == jnp.arange(number_of_tiles, dtype=jnp.int32)[None, None, :]
    ).astype(jnp.bfloat16)
    pieces = packed.reshape(block_count, block_rows, slots, tile_rows)
    dense_factor = jnp.einsum("bst,bpse->tebp", onehot, pieces, preferred_element_type=jnp.float32)
    return dense_factor.reshape(number_of_tiles * tile_rows, block_count * block_rows).astype(
        jnp.bfloat16
    )


def local(amplitudes, packed_factor, screen, metric, occ_energy, vir_energy, pair_occ):
    gathered = lax.all_gather(packed_factor, ("grid", "pair"), axis=0, tiled=True)
    tile_rows = packed_factor.shape[1] // screen.shape[1]
    number_of_tiles = amplitudes.shape[2] // tile_rows
    factor = widened_factor(gathered, screen, number_of_tiles)
    grid_width = metric.shape[1]
    grid_index = lax.axis_index("grid")
    amp_full = lax.all_gather(amplitudes, "grid", axis=1, tiled=True)
    own_factor = lax.dynamic_slice_in_dim(factor, grid_index * grid_width, grid_width, 1)
    half_product = jnp.einsum(
        "kcd,dq->kcq", amp_full, own_factor, preferred_element_type=jnp.float32
    ).astype(jnp.bfloat16)
    mixed = jnp.einsum("cp,kcq->kpq", factor, half_product, preferred_element_type=jnp.float32)
    weighted = (metric.astype(jnp.float32)[None] * mixed).astype(jnp.bfloat16)
    ladder = jnp.einsum("ap,kpq->kaq", factor, weighted, preferred_element_type=jnp.float32).astype(
        jnp.bfloat16
    )
    result = jnp.einsum(
        "kaq,bq->kab",
        lax.all_to_all(ladder, "grid", split_axis=1, concat_axis=2, tiled=True),
        factor,
        preferred_element_type=jnp.float32,
    )
    own_count = result.shape[1]
    own_vir = lax.dynamic_slice_in_dim(vir_energy, grid_index * own_count, own_count, 0)
    occ_match = (
        pair_occ[:, :, None] == jnp.arange(occ_energy.shape[0], dtype=jnp.int32)[None, None, :]
    )
    occ_total = jnp.sum(
        jnp.where(occ_match, occ_energy[None, None, :], jnp.float32(0.0)), axis=(1, 2)
    )
    denominator = own_vir[None, :, None] + vir_energy[None, None, :] - occ_total[:, None, None]
    return result / denominator


def solution(mesh):
    in_specs = (
        P("pair", "grid", None),
        P(("grid", "pair"), None),
        P(),
        P(None, "grid"),
        P(),
        P(),
        P("pair", None),
    )
    out_specs = P("pair", "grid", None)
    return jax.shard_map(local, mesh=mesh, in_specs=in_specs, out_specs=out_specs, check_vma=False)
```

profile of v0, /device:TPU:0, one launch (start us, length us, event | category | flops | bytes accessed | tf_op | source)
XLA Modules:
  0.0 107.1 jit_solution(17418620426863104054)
XLA Ops:
  6.5 0.0 copy-start.2
  6.5 0.0 all-gather.2.cloned.1.call-start
  6.5 0.7 all-gather.2.cloned.1.call-update
  7.3 46.2 %all_gather.6 = bf16[512,512]{1,0:T(8,128)(2,1)S(1)} all-gather(bf16[16,512]{1,0:T(8,128)(2,1)} %param.8), channel_id=1, replica_groups=mesh['grid'=4,'pair'=8] {'grid','pair'}, dimensions={0}, use_global_device_ids=true | all-gather | bytes 540672 | tf_op jit(solution)/shard_map/all_gather | solution.py:22
  53.4 0.1 reshape.108
  53.5 0.0 copy-done.2
  53.6 1.1 convolution_convert_fusion.1
  54.6 0.0 copy-start
  54.6 0.4 copy.29
  55.1 0.5 copy-done
  55.5 0.1 copy.19
  55.7 15.1 %all-gather.2.cloned.1.call-done = bf16[1,1536,1536]{2,1,0:T(8,128)(2,1)} async-done(((bf16[1,384,1536]{2,1,0:T(8,128)(2,1)}), bf16[1,1536,1536]{2,1,0:T(8,128)(2,1)}) %all-gather.2.cloned.1.call-update) | async-done | bytes 4718608 | tf_op jit(solution)/shard_map/all_gather | solution.py:28
  70.8 4.5 %fusion.9 = bf16[512,128]{0,1:T(8,128)(2,1)S(1)} fusion(bf16[1536,512]{0,1:T(8,128)(2,1)S(1)} %bitcast.54, bf16[1,1536,1536]{2,1,0:T(8,128)(2,1)} %all-gather.2.cloned.1.call-done, s32[]{:T(128)S(6)} %select_n.18, bf16[512,128]{0,1:T(8,128)(2,1)S(1)} %copy.19), kind=kOutput, calls=%fused_computation.12 | convolution fusion | flops 805699584 | bytes 6946820 | tf_op jit(solution)/shard_map/cp,kcq->kpq/dot_general | solution.py:33
  75.2 0.4 fusion.6
  75.6 0.0 copy-start.3
  75.6 0.0 copy-start.1
  75.6 0.0 copy-start.4
  75.6 0.6 copy.21
  76.2 0.5 broadcast.69
  76.7 8.8 %reduce.1 = bf16[1536,128]{1,0:T(8,128)(2,1)S(1)} reduce(bf16[1536,1,128]{2,1,0:T(2,128)(2,1)S(1)} %bitcast.58, bf16[]{:T(256)} %broadcast.69), dimensions={1}, to_apply=%bitcast.45.reduce_sub_computation | reduce | bytes 786434
  85.5 0.8 reshape.115
  86.4 3.5 %all-to-all-start = ((bf16[4,2,24576]{2,1,0:T(2,128)(2,1)}), bf16[4,2,24576]{2,1,0:T(2,128)(2,1)S(1)}, u32[]{:S(2)}, u32[]{:S(2)}) async-start(bf16[4,2,24576]{2,1,0:T(2,128)(2,1)} %reshape.115), calls=%async_computation | async-start | bytes 786432 | tf_op jit(solution)/shard_map/all_to_all | solution.py:40
  89.8 0.0 copy-done.3
  89.9 0.1 dynamic_slice.7
  89.9 0.0 copy-done.1
  89.9 0.0 copy-done.4
  89.9 0.7 fusion.17
  90.6 6.1 %all-to-all-done = bf16[4,2,24576]{2,1,0:T(2,128)(2,1)S(1)} async-done(((bf16[4,2,24576]{2,1,0:T(2,128)(2,1)}), bf16[4,2,24576]{2,1,0:T(2,128)(2,1)S(1)}, u32[]{:S(2)}, u32[]{:S(2)}) %all-to-all-start) | async-done | bytes 393248 | tf_op jit(solution)/shard_map/all_to_all | solution.py:40
  96.7 0.4 reshape.116
  97.1 0.1 copy.25
  97.2 0.2 copy.22
  97.4 2.8 %fusion.2 = f32[1,384,1536]{2,1,0:T(8,128)} fusion(bf16[384,512]{0,1:T(8,128)(2,1)S(1)} %bitcast.61, bf16[1536,512]{0,1:T(8,128)(2,1)S(1)} %bitcast.56, f32[]{:T(128)} %fusion.17, f32[1536]{0:T(1024)S(1)} %copy-done.3, f32[384]{0:T(512)S(1)} %dynamic_slice.7), kind=kOutput, calls=%fused_computation.3 | convolution fusion | flops 605749248 | bytes 4333060 | tf_op jit(solution)/shard_map/kaq,bq->kab/dot_general | solution.py:38
Async XLA Ops:
  6.5 47.0 %copy-start.2 = (s32[4,4]{1,0:T(4,128)S(1)}, s32[4,4]{1,0:T(4,128)}, u32[]{:S(2)}) copy-start(s32[4,4]{1,0:T(4,128)} %param.9) | copy-start | bytes 196
  6.5 64.2 %all-gather.2.cloned.1.call-start = ((), (), s32[]{:S(2)}) async-start(), calls=%async_computation.1 | async-start | bytes 5898240 | tf_op jit(solution)/shard_map/all_gather | solution.py:28
  54.6 0.9 copy-start
  75.6 14.3 %copy-start.3 = (f32[1536]{0:T(1024)S(1)}, f32[1536]{0:T(1024)}, u32[]{:S(2)}) copy-start(f32[1536]{0:T(1024)} %param.12) | copy-start | bytes 18436
  75.6 14.3 %copy-start.1 = (f32[300]{0:T(512)S(1)}, f32[300]{0:T(512)}, u32[]{:S(2)}) copy-start(f32[300]{0:T(512)} %param.11) | copy-start | bytes 3604
  75.6 14.3 %copy-start.4 = (s32[1,2]{1,0:T(1,128)S(1)}, s32[1,2]{1,0:T(1,128)}, u32[]{:S(2)}) copy-start(s32[1,2]{1,0:T(1,128)} %param.13) | copy-start | bytes 28
  86.4 10.3 %all-to-all-start = ((bf16[4,2,24576]{2,1,0:T(2,128)(2,1)}), bf16[4,2,24576]{2,1,0:T(2,128)(2,1)S(1)}, u32[]{:S(2)}, u32[]{:S(2)}) async-start(bf16[4,2,24576]{2,1,0:T(2,128)(2,1)} %reshape.115), calls=%async_computation | async-start | bytes 786432 | tf_op jit(solution)/shard_map/all_to_all | solution.py:40
Sparse Core Ops, SparseCore 0:
  9.2 61.5 all-gather.1
where the time goes:
time: 107 us
  blocking collectives  46.2 us (43%)
  waiting for transfers between devices  21.9 us (20%)
  between operations  13.5 us (13%)
  other arithmetic  9.48 us (9%)
  matrix products  8.72 us (8%)
  local copies, waits for them, and re-layouts  3.83 us (4%)
  starting transfers between devices  3.46 us (3%)
    all_gather x1, blocking collectives, local(): lax.all_gather(packed_factor, ('grid', 'pair'), axis=0, tiled=True)  46.2 us
    all_gather x1, waiting for transfers between devices, local(): amp_full = lax.all_gather(amplitudes, 'grid', axis=1, tiled=True)  15.1 us
    unnamed x1, other arithmetic  8.8 us
    all_to_all x1, waiting for transfers between devices, local(): lax.all_to_all(ladder, 'grid', split_axis=1, concat_axis=2, tiled=True)  6.09 us
    dot_general x1, matrix products, local(): jnp.einsum('cp,kcq->kpq', factor, half_product, preferred_element_type=jn...  4.45 us
    all_to_all x1, starting transfers between devices, local(): lax.all_to_all(ladder, 'grid', split_axis=1, concat_axis=2, tiled=True)  3.46 us
    dot_general x1, matrix products, local(): jnp.einsum('kaq,bq->kab', lax.all_to_all(ladder, 'grid', split_axis=1, co...  2.83 us
    unnamed x16, local copies, waits for them, and re-layouts  2.83 us
  transfers between devices with their start and end apart: 2, of which 2 were waited for; matrix products, arithmetic and copies ran while one was open for 2% of the time, Pallas kernels for 0%

commit v1 on v0

v1 whole, which is shorter than its diff:
```python
import functools

import jax
import jax.numpy as jnp
from jax import lax
from jax.experimental import pallas as pl
from jax.experimental.pallas import tpu as pltpu
from jax.sharding import PartitionSpec as P

BF16 = jnp.bfloat16
F32 = jnp.float32
VMEM_LIMIT = 40 * 1024 * 1024


def exchange(value, axis, size, step):
    return lax.ppermute(value, axis, [(i, i ^ step) for i in range(size)])


def pack_kernel(tile, slots, count, place, screen, amplitudes, *rest):
    outs, sems = rest[:count], rest[count]
    copies = []
    for k in list(range(1, count)) + [0]:
        block = place[0] ^ k
        for s in range(slots):
            column = pl.multiple_of(screen[block, s] * tile, tile)
            copies.append(
                pltpu.make_async_copy(
                    amplitudes.at[:, pl.ds(column, tile)],
                    outs[k].at[:, pl.ds(s * tile, tile)],
                    sems.at[k * slots + s],
                )
            )
    for copy in copies:
        copy.start()
    for copy in copies:
        copy.wait()


def pack(place, screen, amplitudes, count, tile):
    rows = amplitudes.shape[0]
    slots = screen.shape[1]
    return pl.pallas_call(
        functools.partial(pack_kernel, tile, slots, count),
        out_shape=[jax.ShapeDtypeStruct((rows, slots * tile), BF16)] * count,
        in_specs=[
            pl.BlockSpec(memory_space=pltpu.SMEM),
            pl.BlockSpec(memory_space=pltpu.SMEM),
            pl.BlockSpec(memory_space=pl.ANY),
        ],
        out_specs=[pl.BlockSpec(memory_space=pl.ANY)] * count,
        scratch_shapes=[pltpu.SemaphoreType.DMA((count * slots,))],
        name="pack",
    )(place, screen, amplitudes)


def widen_kernel(tile, slots, screen, packed, dense):
    width = packed.shape[0] // screen.shape[0]
    dense[...] = jnp.zeros_like(dense)
    for b in range(screen.shape[0]):
        for s in range(slots):
            column = pl.multiple_of(screen[b, s] * tile, tile)
            dense[b * width : (b + 1) * width, pl.ds(column, tile)] = packed[
                b * width : (b + 1) * width, s * tile : (s + 1) * tile
            ]


def widen(screen, packed, virtuals, tile):
    return pl.pallas_call(
        functools.partial(widen_kernel, tile, screen.shape[1]),
        out_shape=jax.ShapeDtypeStruct((packed.shape[0], virtuals), BF16),
        in_specs=[
            pl.BlockSpec(memory_space=pltpu.SMEM),
            pl.BlockSpec(memory_space=pltpu.VMEM),
        ],
        out_specs=pl.BlockSpec(memory_space=pltpu.VMEM),
        compiler_params=pltpu.CompilerParams(vmem_limit_bytes=VMEM_LIMIT),
        name="widen",
    )(screen, packed)


def ladder_kernel(tile, slots, count, place, screen, packed, metric, *rest):
    amps, outs = rest[:count], rest[count : 2 * count]
    half, selected, total = rest[2 * count :]
    width = metric.shape[1]
    rows = amps[0].shape[0]
    me = place[0]
    own = packed[pl.ds(pl.multiple_of(me * width, width), width), :]
    for k in range(count):
        start = pl.multiple_of((me ^ k) * rows, rows)
        half[pl.ds(start, rows), :] = lax.dot_general(
            amps[k][...], own, (((1,), (1,)), ((), ())), preferred_element_type=F32
        ).astype(BF16)
    total[...] = jnp.zeros_like(total)
    for b in range(count):
        for s in range(slots):
            start = pl.multiple_of(screen[b, s] * tile, tile)
            selected[b, s * tile : (s + 1) * tile, :] = half[pl.ds(start, tile), :]
    for b in range(count):
        block = packed[b * width : (b + 1) * width, :]
        mixed = jnp.dot(block, selected[b], preferred_element_type=F32)
        weighted = (metric[b * width : (b + 1) * width, :].astype(F32) * mixed).astype(BF16)
        part = lax.dot_general(
            block, weighted, (((0,), (0,)), ((), ())), preferred_element_type=F32
        )
        for s in range(slots):
            start = pl.multiple_of(screen[b, s] * tile, tile)
            total[pl.ds(start, tile), :] += part[s * tile : (s + 1) * tile, :]
    for k in range(count):
        start = pl.multiple_of((me ^ k) * rows, rows)
        outs[k][...] = total[pl.ds(start, rows), :].astype(BF16)


def ladders(place, screen, packed, metric, amps, virtuals, tile):
    count = len(amps)
    rows = amps[0].shape[0]
    width = metric.shape[1]
    slots = screen.shape[1]
    vmem = pl.BlockSpec(memory_space=pltpu.VMEM)
    return pl.pallas_call(
        functools.partial(ladder_kernel, tile, slots, count),
        out_shape=[jax.ShapeDtypeStruct((rows, width), BF16)] * count,
        in_specs=[pl.BlockSpec(memory_space=pltpu.SMEM)] * 2 + [vmem] * (2 + count),
        out_specs=[vmem] * count,
        scratch_shapes=[
            pltpu.VMEM((virtuals, width), BF16),
            pltpu.VMEM((count, slots * tile, width), BF16),
            pltpu.VMEM((virtuals, width), F32),
        ],
        compiler_params=pltpu.CompilerParams(vmem_limit_bytes=VMEM_LIMIT),
        name="ladders",
    )(place, screen, packed, metric, *amps)


def result_kernel(count, place, pair_occ, occ_energy, own_vir, vir, dense, *rest):
    pieces, out, joined = rest[:count], rest[count], rest[count + 1]
    me = place[0]
    width = pieces[0].shape[1]
    for k in range(count):
        column = pl.multiple_of((me ^ k) * width, width)
        joined[:, pl.ds(column, width)] = pieces[k][...]
    occ_total = occ_energy[pair_occ[0, 0]] + occ_energy[pair_occ[0, 1]]
    value = jnp.dot(joined[...], dense[...], preferred_element_type=F32)
    out[...] = value / ((own_vir[...] + vir[...]) - occ_total)


def results(place, pair_occ, occ_energy, own_vir, vir, dense, pieces):
    count = len(pieces)
    rows, width = pieces[0].shape
    points, virtuals = dense.shape
    steps = 3 if rows % 48 == 0 else 1
    part = rows // steps
    smem = pl.BlockSpec(memory_space=pltpu.SMEM)
    return pl.pallas_call(
        functools.partial(result_kernel, count),
        grid=(steps,),
        out_shape=jax.ShapeDtypeStruct((rows, virtuals), F32),
        in_specs=[smem] * 3
        + [
            pl.BlockSpec((part, 1), lambda i: (i, 0)),
            pl.BlockSpec((1, virtuals), lambda i: (0, 0)),
            pl.BlockSpec((points, virtuals), lambda i: (0, 0)),
        ]
        + [pl.BlockSpec((part, width), lambda i: (i, 0))] * count,
        out_specs=pl.BlockSpec((part, virtuals), lambda i: (i, 0)),
        scratch_shapes=[pltpu.VMEM((part, points), BF16)],
        compiler_params=pltpu.CompilerParams(vmem_limit_bytes=VMEM_LIMIT),
        name="results",
    )(place, pair_occ, occ_energy, own_vir, vir, dense, *pieces)


def local(
    grids, pairs, amplitudes, packed_factor, screen, metric, occ_energy, vir_energy, pair_occ
):
    me = lax.axis_index("grid")
    pair = lax.axis_index("pair")
    layer, core = pair // 2, pair % 2
    layers = pairs // 2
    place = me.astype(jnp.int32).reshape(1)
    _, rows, virtuals = amplitudes.shape
    tile = packed_factor.shape[1] // screen.shape[1]

    packs = pack(place, screen, amplitudes[0], grids, tile)
    amps = [packs[0]] + [exchange(packs[k], "grid", grids, k) for k in range(1, grids)]

    stack = jnp.zeros((layers,) + packed_factor.shape, BF16)
    stack = lax.dynamic_update_slice(stack, packed_factor[None], (layer, 0, 0))
    for k in range(1, layers):
        piece = exchange(packed_factor, "pair", pairs, 2 * k)
        stack = lax.dynamic_update_slice(stack, piece[None], (layer ^ k, 0, 0))
    plane = jnp.zeros((grids,) + stack.shape, BF16)
    plane = lax.dynamic_update_slice(plane, stack[None], (me, 0, 0, 0))
    for k in range(1, grids):
        piece = exchange(stack, "grid", grids, k)
        plane = lax.dynamic_update_slice(plane, piece[None], (me ^ k, 0, 0, 0))
    other = exchange(plane, "pair", pairs, 1)
    packed = jnp.where(
        core == 0, jnp.stack([plane, other], 2), jnp.stack([other, plane], 2)
    ).reshape(-1, packed_factor.shape[1])
    dense = widen(screen, packed, virtuals, tile)
    own_vir = lax.dynamic_slice_in_dim(vir_energy, me * rows, rows, 0)[:, None]

    sent = ladders(place, screen, packed, metric, amps, virtuals, tile)
    pieces = [sent[0]] + [exchange(sent[k], "grid", grids, k) for k in range(1, grids)]
    update = results(
        place, pair_occ, occ_energy, own_vir, vir_energy[None, :], dense, pieces
    )
    return update[None]


def solution(mesh):
    in_specs = (
        P("pair", "grid", None),
        P(("grid", "pair"), None),
        P(),
        P(None, "grid"),
        P(),
        P(),
        P("pair", None),
    )
    return jax.shard_map(
        functools.partial(local, mesh.shape["grid"], mesh.shape["pair"]),
        mesh=mesh,
        in_specs=in_specs,
        out_specs=P("pair", "grid", None),
        check_vma=False,
    )
```

time: 107 us -> 97 us (0.907)
  Pallas kernels: 0 us -> 55.4 us
  blocking collectives: 46.2 us -> 0 us
  starting transfers between devices: 3.46 us -> 17.4 us
  between operations: 13.5 us -> 0.2 us
  other arithmetic: 9.48 us -> 0.05 us
  matrix products: 8.72 us -> 0 us
  local copies, waits for them, and re-layouts: 3.83 us -> 1.02 us
    pallas_call x0 -> x4, Pallas kernels: none -> 55.4 us  [the longest x1 49.7 us: pack(): pl.pallas_call(functools.partial(pack_kernel, tile, slots, count), out_sh...]
    all_gather x1 -> x0, blocking collectives: 46.2 us -> none  [local(): lax.all_gather(packed_factor, ('grid', 'pair'), axis=0, tiled=True)]
    ppermute x0 -> x13, waiting for transfers between devices: none -> 22.7 us  [exchange(): return lax.ppermute(value, axis, [(i, i ^ step) for i in range(size)])]
    ppermute x0 -> x13, starting transfers between devices: none -> 17.4 us  [exchange(): return lax.ppermute(value, axis, [(i, i ^ step) for i in range(size)])]
    all_gather x1 -> x0, waiting for transfers between devices: 15.1 us -> none  [local(): amp_full = lax.all_gather(amplitudes, 'grid', axis=1, tiled=True)]
    unnamed x1 -> x0, other arithmetic: 8.8 us -> none
    dot_general x4 -> x0, matrix products: 8.72 us -> none  [the longest x1 4.45 us: local(): jnp.einsum('cp,kcq->kpq', factor, half_product, preferred_element_type=jn...]
    all_to_all x1 -> x0, waiting for transfers between devices: 6.09 us -> none  [local(): lax.all_to_all(ladder, 'grid', split_axis=1, concat_axis=2, tiled=True)]
  transfers between devices with their start and end apart: 2 -> 13, of which waited for: 2 -> 6; matrix products, arithmetic and copies ran while one was open for 2% -> 1% of each run, Pallas kernels for 0% -> 52%
where the time goes in v1:
time: 97 us; the launch traced here: 96.8 us
  Pallas kernels  55.4 us (57%)
  waiting for transfers between devices  22.7 us (23%)
  starting transfers between devices  17.4 us (18%)
  local copies, waits for them, and re-layouts  1.02 us (1%)
    pallas_call x1, Pallas kernels, pack(): pl.pallas_call(functools.partial(pack_kernel, tile, slots, count), out_sh...  49.7 us
    ppermute x13, waiting for transfers between devices, exchange(): return lax.ppermute(value, axis, [(i, i ^ step) for i in range(size)])  22.7 us
    ppermute x13, starting transfers between devices, exchange(): return lax.ppermute(value, axis, [(i, i ^ step) for i in range(size)])  17.4 us
    pallas_call x1, Pallas kernels, results(): pl.pallas_call(functools.partial(result_kernel, count), grid=(steps,), ou...  3.13 us
  transfers between devices with their start and end apart: 13, of which 6 were waited for; matrix products, arithmetic and copies ran while one was open for 1% of the time, Pallas kernels for 52%

profile of v1, /device:TPU:0, one launch (start us, length us, event | category | flops | bytes accessed | tf_op | source)
XLA Modules:
  0.0 96.8 jit_solution(17370247290825011339)
XLA Ops:
  0.0 3.0 %collective-permute-start = (bf16[16,512]{1,0:T(8,128)(2,1)}, bf16[16,512]{1,0:T(8,128)(2,1)S(1)}, u32[]{:S(2)}, u32[]{:S(2)}) collective-permute-start(bf16[16,512]{1,0:T(8,128)(2,1)} %param.8), channel_id=1, source_target_pairs={{0,2},{1,3},{2,0},{3,1},{4,6},{5,7},{6,4},{7,5},{8,10},{9,11},{10,... | collective-permute-start | bytes 49160 | tf_op jit(solution)/shard_map/ppermute | solution.py:16
  3.0 2.5 %collective-permute-start.2 = (bf16[16,512]{1,0:T(8,128)(2,1)}, bf16[16,512]{1,0:T(8,128)(2,1)S(1)}, u32[]{:S(2)}, u32[]{:S(2)}) collective-permute-start(bf16[16,512]{1,0:T(8,128)(2,1)} %param.8), channel_id=1, source_target_pairs={{0,6},{1,7},{2,4},{3,5},{4,2},{5,3},{6,0},{7,1},{8,14},{9,15},{10,... | collective-permute-start | bytes 49160 | tf_op jit(solution)/shard_map/ppermute | solution.py:16
  5.5 0.1 collective-permute-start.1
  5.6 49.7 %pack.1 = (bf16[384,512]{1,0:T(8,128)(2,1)}, bf16[384,512]{1,0:T(8,128)(2,1)}, bf16[384,512]{1,0:T(8,128)(2,1)}, bf16[384,512]{1,0:T(8,128)(2,1)}) custom-call(s32[1]{0:T(128)} %bitcast.place, s32[4,4]{1,0:T(4,128)} %screen.5, bf16[384,1536]{1,0:T(8,128)(2,1)} %bitcast.24), custom_call_target="tpu_custom_call" | custom-call | tf_op jit(solution)/shard_map/pack/pallas_call | solution.py:42
  55.4 0.0 copy-start
  55.4 1.6 %collective-permute-start.7 = (bf16[384,512]{1,0:T(8,128)(2,1)}, bf16[384,512]{1,0:T(8,128)(2,1)S(1)}, u32[]{:S(2)}, u32[]{:S(2)}) collective-permute-start(bf16[384,512]{1,0:T(8,128)(2,1)} %get-tuple-element.14), channel_id=1, source_target_pairs={{0,8},{8,0},{16,24},{24,16},{1,9},{9,1},{17,25},{25,17},{2,10},{10... | collective-permute-start | bytes 1179656 | tf_op jit(solution)/shard_map/ppermute | solution.py:16
  56.9 1.5 %collective-permute-start.8 = (bf16[384,512]{1,0:T(8,128)(2,1)}, bf16[384,512]{1,0:T(8,128)(2,1)S(1)}, u32[]{:S(2)}, u32[]{:S(2)}) collective-permute-start(bf16[384,512]{1,0:T(8,128)(2,1)} %get-tuple-element.15), channel_id=1, source_target_pairs={{0,16},{8,24},{16,0},{24,8},{1,17},{9,25},{17,1},{25,9},{2,18},{10... | collective-permute-start | bytes 1179656 | tf_op jit(solution)/shard_map/ppermute | solution.py:16
  58.4 0.7 bitcast_dynamic-update-slice_fusion.7
  59.2 0.0 collective-permute-done
  59.2 0.5 collective-permute-start.9
  59.7 0.0 collective-permute-done.2
  59.7 2.5 %collective-permute-start.5 = (bf16[4,16,512]{2,1,0:T(8,128)(2,1)S(1)}, bf16[4,16,512]{2,1,0:T(8,128)(2,1)S(1)}, u32[]{:S(2)}, u32[]{:S(2)}) collective-permute-start(bf16[4,16,512]{2,1,0:T(8,128)(2,1)S(1)} %bitcast_dynamic-update-slice_fusion.4), channel_id=1, source_target_pairs={{0,24},{8,16},{16,8},{24,0},{1,25},{9,17},{17,9},{25,1},{2,26},{10... | collective-permute-start | bytes 196616 | tf_op jit(solution)/shard_map/ppermute | solution.py:16
  62.2 0.5 collective-permute-start.3
  62.8 14.4 %collective-permute-done.3 = bf16[4,16,512]{2,1,0:T(8,128)(2,1)S(1)} collective-permute-done((bf16[4,16,512]{2,1,0:T(8,128)(2,1)S(1)}, bf16[4,16,512]{2,1,0:T(8,128)(2,1)S(1)}, u32[]{:S(2)}, u32[]{:S(2)}) %collective-permute-start.3) | collective-permute-done | bytes 65568 | tf_op jit(solution)/shard_map/ppermute | solution.py:16
  77.2 1.5 %collective-permute-start.4 = (bf16[4,16,512]{2,1,0:T(8,128)(2,1)S(1)}, bf16[4,16,512]{2,1,0:T(8,128)(2,1)S(1)}, u32[]{:S(2)}, u32[]{:S(2)}) collective-permute-start(bf16[4,16,512]{2,1,0:T(8,128)(2,1)S(1)} %bitcast_dynamic-update-slice_fusion.4), channel_id=1, source_target_pairs={{0,16},{8,24},{16,0},{24,8},{1,17},{9,25},{17,1},{25,9},{2,18},{10... | collective-permute-start | bytes 196616 | tf_op jit(solution)/shard_map/ppermute | solution.py:16
  78.7 2.7 %collective-permute-done.4 = bf16[4,16,512]{2,1,0:T(8,128)(2,1)S(1)} collective-permute-done((bf16[4,16,512]{2,1,0:T(8,128)(2,1)S(1)}, bf16[4,16,512]{2,1,0:T(8,128)(2,1)S(1)}, u32[]{:S(2)}, u32[]{:S(2)}) %collective-permute-start.4) | collective-permute-done | bytes 65568 | tf_op jit(solution)/shard_map/ppermute | solution.py:16
  81.5 0.1 collective-permute-start.6
  81.6 1.5 %collective-permute-done.6 = bf16[4,4,16,512]{3,2,1,0:T(8,128)(2,1)S(1)} collective-permute-done((bf16[4,4,16,512]{3,2,1,0:T(8,128)(2,1)S(1)}, bf16[4,4,16,512]{3,2,1,0:T(8,128)(2,1)S(1)}, u32[]{:S(2)}, u32[]{:S(2)}) %collective-permute-start.6) | collective-permute-done | bytes 262176 | tf_op jit(solution)/shard_map/ppermute | solution.py:16
  83.2 0.0 collective-permute-done.8.rest_2_
  83.2 1.8 %ladders.1 = (bf16[384,128]{1,0:T(8,128)(2,1)S(1)}, bf16[384,128]{1,0:T(8,128)(2,1)S(1)}, bf16[384,128]{1,0:T(8,128)(2,1)S(1)}, bf16[384,128]{1,0:T(8,128)(2,1)S(1)}) custom-call(s32[1]{0:T(128)} %bitcast.place, s32[4,4]{1,0:T(4,128)S(1)} %copy-done.2, bf16[512,512]{1,0:T(8,128)(2,1)S(1)} %bitcast.22, bf16[512,128]{1,0:T(8,128)(2,1)S(1)} %copy-done.1, ...), custom_call_target="tpu_custom_call" | custom-call | tf_op jit(solution)/shard_map/ladders/pallas_call | solution.py:119
  85.1 0.0 copy-start.3
  85.1 0.0 copy-start.4
  85.1 1.6 %collective-permute-start.10 = (bf16[384,128]{1,0:T(8,128)(2,1)S(1)}, bf16[384,128]{1,0:T(8,128)(2,1)S(1)}, u32[]{:S(2)}, u32[]{:S(2)}) collective-permute-start(bf16[384,128]{1,0:T(8,128)(2,1)S(1)} %get-tuple-element.18), channel_id=1, source_target_pairs={{0,8},{8,0},{16,24},{24,16},{1,9},{9,1},{17,25},{25,17},{2,10},{10... | collective-permute-start | bytes 294920 | tf_op jit(solution)/shard_map/ppermute | solution.py:16
  86.6 1.5 %collective-permute-start.11 = (bf16[384,128]{1,0:T(8,128)(2,1)S(1)}, bf16[384,128]{1,0:T(8,128)(2,1)S(1)}, u32[]{:S(2)}, u32[]{:S(2)}) collective-permute-start(bf16[384,128]{1,0:T(8,128)(2,1)S(1)} %get-tuple-element.19), channel_id=1, source_target_pairs={{0,16},{8,24},{16,0},{24,8},{1,17},{9,25},{17,1},{25,9},{2,18},{10... | collective-permute-start | bytes 294920 | tf_op jit(solution)/shard_map/ppermute | solution.py:16
  88.1 0.5 collective-permute-start.12
  88.6 0.1 dynamic_slice.3
  88.7 0.1 broadcast_in_dim.52.own_vir
  88.8 0.8 widen.1.dense
  89.6 0.4 collective-permute-done.10.rest_1_
  90.0 2.4 %collective-permute-done.11.rest_2_ = bf16[384,128]{1,0:T(8,128)(2,1)S(1)} collective-permute-done((bf16[384,128]{1,0:T(8,128)(2,1)S(1)}, bf16[384,128]{1,0:T(8,128)(2,1)S(1)}, u32[]{:S(2)}, u32[]{:S(2)}) %collective-permute-start.11) | collective-permute-done | bytes 98336 | tf_op jit(solution)/shard_map/ppermute | solution.py:16
  92.4 1.2 %collective-permute-done.12.rest_3_ = bf16[384,128]{1,0:T(8,128)(2,1)S(1)} collective-permute-done((bf16[384,128]{1,0:T(8,128)(2,1)S(1)}, bf16[384,128]{1,0:T(8,128)(2,1)S(1)}, u32[]{:S(2)}, u32[]{:S(2)}) %collective-permute-start.12) | collective-permute-done | bytes 98336 | tf_op jit(solution)/shard_map/ppermute | solution.py:16
  93.6 3.1 %results.1 = f32[384,1536]{1,0:T(8,128)} custom-call(s32[1]{0:T(128)} %bitcast.place, s32[1,2]{1,0:T(1,128)S(1)} %copy-done.4, f32[300]{0:T(512)S(1)} %copy-done.3, f32[384,1]{1,0:T(8,128)S(1)} %broadcast_in_dim.52.own_vir, f32[1,1536]{1,0:T(1,128)S(1)} %broadcast_in_dim.40.vir, bf16[512,1536]{1,0:T(8,128)(2,1)S(1)} %widen.1.dense, ...), custom_call_target="tpu_custom_call" | custom-call | tf_op jit(solution)/shard_map/results/pallas_call | solution.py:153
  (24 shorter events, 0.2 us)
Async XLA Ops:
  0.0 59.2 %collective-permute-start = (bf16[16,512]{1,0:T(8,128)(2,1)}, bf16[16,512]{1,0:T(8,128)(2,1)S(1)}, u32[]{:S(2)}, u32[]{:S(2)}) collective-permute-start(bf16[16,512]{1,0:T(8,128)(2,1)} %param.8), channel_id=1, source_target_pairs={{0,2},{1,3},{2,0},{3,1},{4,6},{5,7},{6,4},{7,5},{8,10},{9,11},{10,... | collective-permute-start | bytes 49160 | tf_op jit(solution)/shard_map/ppermute | solution.py:16
  3.0 56.6 %collective-permute-start.2 = (bf16[16,512]{1,0:T(8,128)(2,1)}, bf16[16,512]{1,0:T(8,128)(2,1)S(1)}, u32[]{:S(2)}, u32[]{:S(2)}) collective-permute-start(bf16[16,512]{1,0:T(8,128)(2,1)} %param.8), channel_id=1, source_target_pairs={{0,6},{1,7},{2,4},{3,5},{4,2},{5,3},{6,0},{7,1},{8,14},{9,15},{10,... | collective-permute-start | bytes 49160 | tf_op jit(solution)/shard_map/ppermute | solution.py:16
  5.5 54.2 %collective-permute-start.1 = (bf16[16,512]{1,0:T(8,128)(2,1)}, bf16[16,512]{1,0:T(8,128)(2,1)S(1)}, u32[]{:S(2)}, u32[]{:S(2)}) collective-permute-start(bf16[16,512]{1,0:T(8,128)(2,1)} %param.8), channel_id=1, source_target_pairs={{0,4},{1,5},{2,6},{3,7},{4,0},{5,1},{6,2},{7,3},{8,12},{9,13},{10,... | collective-permute-start | bytes 49160 | tf_op jit(solution)/shard_map/ppermute | solution.py:16
  5.6 77.6 %copy-start.1 = (bf16[512,128]{1,0:T(8,128)(2,1)S(1)}, bf16[512,128]{1,0:T(8,128)(2,1)}, u32[]{:S(2)}) copy-start(bf16[512,128]{1,0:T(8,128)(2,1)} %metric.1) | copy-start | bytes 393220
  5.6 77.6 %copy-start.2 = (s32[4,4]{1,0:T(4,128)S(1)}, s32[4,4]{1,0:T(4,128)}, u32[]{:S(2)}) copy-start(s32[4,4]{1,0:T(4,128)} %screen.5) | copy-start | bytes 196
  55.4 27.9 %copy-start = (bf16[384,512]{1,0:T(8,128)(2,1)S(1)}, bf16[384,512]{1,0:T(8,128)(2,1)}, u32[]{:S(2)}) copy-start(bf16[384,512]{1,0:T(8,128)(2,1)} %get-tuple-element.13.rest_0_) | copy-start | bytes 1179652
  55.4 27.8 %collective-permute-start.7 = (bf16[384,512]{1,0:T(8,128)(2,1)}, bf16[384,512]{1,0:T(8,128)(2,1)S(1)}, u32[]{:S(2)}, u32[]{:S(2)}) collective-permute-start(bf16[384,512]{1,0:T(8,128)(2,1)} %get-tuple-element.14), channel_id=1, source_target_pairs={{0,8},{8,0},{16,24},{24,16},{1,9},{9,1},{17,25},{25,17},{2,10},{10... | collective-permute-start | bytes 1179656 | tf_op jit(solution)/shard_map/ppermute | solution.py:16
  56.9 26.3 %collective-permute-start.8 = (bf16[384,512]{1,0:T(8,128)(2,1)}, bf16[384,512]{1,0:T(8,128)(2,1)S(1)}, u32[]{:S(2)}, u32[]{:S(2)}) collective-permute-start(bf16[384,512]{1,0:T(8,128)(2,1)} %get-tuple-element.15), channel_id=1, source_target_pairs={{0,16},{8,24},{16,0},{24,8},{1,17},{9,25},{17,1},{25,9},{2,18},{10... | collective-permute-start | bytes 1179656 | tf_op jit(solution)/shard_map/ppermute | solution.py:16
  59.2 24.0 %collective-permute-start.9 = (bf16[384,512]{1,0:T(8,128)(2,1)}, bf16[384,512]{1,0:T(8,128)(2,1)S(1)}, u32[]{:S(2)}, u32[]{:S(2)}) collective-permute-start(bf16[384,512]{1,0:T(8,128)(2,1)} %get-tuple-element.16), channel_id=1, source_target_pairs={{0,24},{8,16},{16,8},{24,0},{1,25},{9,17},{17,9},{25,1},{2,26},{10... | collective-permute-start | bytes 1179656 | tf_op jit(solution)/shard_map/ppermute | solution.py:16
  59.7 21.8 %collective-permute-start.5 = (bf16[4,16,512]{2,1,0:T(8,128)(2,1)S(1)}, bf16[4,16,512]{2,1,0:T(8,128)(2,1)S(1)}, u32[]{:S(2)}, u32[]{:S(2)}) collective-permute-start(bf16[4,16,512]{2,1,0:T(8,128)(2,1)S(1)} %bitcast_dynamic-update-slice_fusion.4), channel_id=1, source_target_pairs={{0,24},{8,16},{16,8},{24,0},{1,25},{9,17},{17,9},{25,1},{2,26},{10... | collective-permute-start | bytes 196616 | tf_op jit(solution)/shard_map/ppermute | solution.py:16
  62.2 15.0 %collective-permute-start.3 = (bf16[4,16,512]{2,1,0:T(8,128)(2,1)S(1)}, bf16[4,16,512]{2,1,0:T(8,128)(2,1)S(1)}, u32[]{:S(2)}, u32[]{:S(2)}) collective-permute-start(bf16[4,16,512]{2,1,0:T(8,128)(2,1)S(1)} %bitcast_dynamic-update-slice_fusion.4), channel_id=1, source_target_pairs={{0,8},{8,0},{16,24},{24,16},{1,9},{9,1},{17,25},{25,17},{2,10},{10... | collective-permute-start | bytes 196616 | tf_op jit(solution)/shard_map/ppermute | solution.py:16
  77.2 4.3 %collective-permute-start.4 = (bf16[4,16,512]{2,1,0:T(8,128)(2,1)S(1)}, bf16[4,16,512]{2,1,0:T(8,128)(2,1)S(1)}, u32[]{:S(2)}, u32[]{:S(2)}) collective-permute-start(bf16[4,16,512]{2,1,0:T(8,128)(2,1)S(1)} %bitcast_dynamic-update-slice_fusion.4), channel_id=1, source_target_pairs={{0,16},{8,24},{16,0},{24,8},{1,17},{9,25},{17,1},{25,9},{2,18},{10... | collective-permute-start | bytes 196616 | tf_op jit(solution)/shard_map/ppermute | solution.py:16
  81.5 1.6 %collective-permute-start.6 = (bf16[4,4,16,512]{3,2,1,0:T(8,128)(2,1)S(1)}, bf16[4,4,16,512]{3,2,1,0:T(8,128)(2,1)S(1)}, u32[]{:S(2)}, u32[]{:S(2)}) collective-permute-start(bf16[4,4,16,512]{3,2,1,0:T(8,128)(2,1)S(1)} %bitcast_dynamic-update-slice_fusion), channel_id=1, source_target_pairs={{0,1},{1,0},{2,3},{3,2},{4,5},{5,4},{6,7},{7,6},{8,9},{9,8},{10,11... | collective-permute-start | bytes 786440 | tf_op jit(solution)/shard_map/ppermute | solution.py:16
  83.1 5.5 %copy-start.5 = (f32[1536]{0:T(1024)S(1)}, f32[1536]{0:T(1024)}, u32[]{:S(2)}) copy-start(f32[1536]{0:T(1024)} %param.12) | copy-start | bytes 18436
  85.1 8.6 %copy-start.3 = (f32[300]{0:T(512)S(1)}, f32[300]{0:T(512)}, u32[]{:S(2)}) copy-start(f32[300]{0:T(512)} %occ_energy.1) | copy-start | bytes 3604
  85.1 8.6 %copy-start.4 = (s32[1,2]{1,0:T(1,128)S(1)}, s32[1,2]{1,0:T(1,128)}, u32[]{:S(2)}) copy-start(s32[1,2]{1,0:T(1,128)} %pair_occ.1) | copy-start | bytes 28
  85.1 4.9 %collective-permute-start.10 = (bf16[384,128]{1,0:T(8,128)(2,1)S(1)}, bf16[384,128]{1,0:T(8,128)(2,1)S(1)}, u32[]{:S(2)}, u32[]{:S(2)}) collective-permute-start(bf16[384,128]{1,0:T(8,128)(2,1)S(1)} %get-tuple-element.18), channel_id=1, source_target_pairs={{0,8},{8,0},{16,24},{24,16},{1,9},{9,1},{17,25},{25,17},{2,10},{10... | collective-permute-start | bytes 294920 | tf_op jit(solution)/shard_map/ppermute | solution.py:16
  86.6 5.7 %collective-permute-start.11 = (bf16[384,128]{1,0:T(8,128)(2,1)S(1)}, bf16[384,128]{1,0:T(8,128)(2,1)S(1)}, u32[]{:S(2)}, u32[]{:S(2)}) collective-permute-start(bf16[384,128]{1,0:T(8,128)(2,1)S(1)} %get-tuple-element.19), channel_id=1, source_target_pairs={{0,16},{8,24},{16,0},{24,8},{1,17},{9,25},{17,1},{25,9},{2,18},{10... | collective-permute-start | bytes 294920 | tf_op jit(solution)/shard_map/ppermute | solution.py:16
  88.1 5.5 %collective-permute-start.12 = (bf16[384,128]{1,0:T(8,128)(2,1)S(1)}, bf16[384,128]{1,0:T(8,128)(2,1)S(1)}, u32[]{:S(2)}, u32[]{:S(2)}) collective-permute-start(bf16[384,128]{1,0:T(8,128)(2,1)S(1)} %get-tuple-element.20), channel_id=1, source_target_pairs={{0,24},{8,16},{16,8},{24,0},{1,25},{9,17},{17,9},{25,1},{2,26},{10... | collective-permute-start | bytes 294920 | tf_op jit(solution)/shard_map/ppermute | solution.py:16

commit v2 on v1

v2 whole, which is shorter than its diff:
```python
import functools

import jax
import jax.numpy as jnp
from jax import lax
from jax.experimental import pallas as pl
from jax.experimental.pallas import tpu as pltpu
from jax.sharding import PartitionSpec as P

BF16 = jnp.bfloat16
F32 = jnp.float32
VMEM_LIMIT = 40 * 1024 * 1024


def exchange(value, axis, size, step):
    return lax.ppermute(value, axis, [(i, i ^ step) for i in range(size)])


def pack_kernel(tile, slots, count, place, screen, amplitudes, *rest):
    outs, sems = rest[:count], rest[count]
    copies = []
    for k in list(range(1, count)) + [0]:
        block = place[0] ^ k
        for s in range(slots):
            column = pl.multiple_of(screen[block, s] * tile, tile)
            copies.append(
                pltpu.make_async_copy(
                    amplitudes.at[:, pl.ds(column, tile)],
                    outs[k].at[:, pl.ds(s * tile, tile)],
                    sems.at[k * slots + s],
                )
            )
    for copy in copies:
        copy.start()
    for copy in copies:
        copy.wait()


def pack(place, screen, amplitudes, count, tile):
    rows = amplitudes.shape[0]
    slots = screen.shape[1]
    return pl.pallas_call(
        functools.partial(pack_kernel, tile, slots, count),
        out_shape=[jax.ShapeDtypeStruct((rows, slots * tile), BF16)] * count,
        in_specs=[
            pl.BlockSpec(memory_space=pltpu.SMEM),
            pl.BlockSpec(memory_space=pltpu.SMEM),
            pl.BlockSpec(memory_space=pl.ANY),
        ],
        out_specs=[pl.BlockSpec(memory_space=pltpu.VMEM)] * count,
        scratch_shapes=[pltpu.SemaphoreType.DMA((count * slots,))],
        cost_estimate=pl.CostEstimate(
            flops=0, bytes_accessed=4 * count * rows * slots * tile, transcendentals=0
        ),
        compiler_params=pltpu.CompilerParams(vmem_limit_bytes=VMEM_LIMIT),
        name="pack",
    )(place, screen, amplitudes)


def half_kernel(listed, block, out):
    out[...] = lax.dot_general(
        listed[...], block[...], (((1,), (1,)), ((), ())), preferred_element_type=F32
    ).astype(BF16)


def half_product(listed, block):
    rows, columns = listed.shape
    width = block.shape[0]
    vmem = pl.BlockSpec(memory_space=pltpu.VMEM)
    return pl.pallas_call(
        half_kernel,
        out_shape=jax.ShapeDtypeStruct((rows, width), BF16),
        in_specs=[vmem] * 2,
        out_specs=vmem,
        cost_estimate=pl.CostEstimate(
            flops=2 * rows * columns * width, bytes_accessed=0, transcendentals=0
        ),
        compiler_params=pltpu.CompilerParams(vmem_limit_bytes=VMEM_LIMIT),
        name="half_product",
    )(listed, block)


def prepare_kernel(tile, slots, count, place, screen, pair_occ, occ_energy, own_vir, vir, *rest):
    blocks, (dense, turned, inverse) = rest[:count], rest[count:]
    width = blocks[0].shape[0]
    dense[...] = jnp.zeros_like(dense)
    for k in range(count):
        b = place[0] ^ k
        for s in range(slots):
            column = pl.multiple_of(screen[b, s] * tile, tile)
            dense[k * width : (k + 1) * width, pl.ds(column, tile)] = blocks[k][
                :, s * tile : (s + 1) * tile
            ]
        turned[k] = blocks[k][...].T
    occ_total = occ_energy[pair_occ[0, 0]] + occ_energy[pair_occ[0, 1]]
    inverse[...] = 1.0 / ((own_vir[...] + vir[...]) - occ_total)


def prepare(place, screen, pair_occ, occ_energy, own_vir, vir, blocks, tile):
    count = len(blocks)
    width, columns = blocks[0].shape
    rows, virtuals = own_vir.shape[0], vir.shape[1]
    smem = pl.BlockSpec(memory_space=pltpu.SMEM)
    vmem = pl.BlockSpec(memory_space=pltpu.VMEM)
    return pl.pallas_call(
        functools.partial(prepare_kernel, tile, screen.shape[1], count),
        out_shape=[
            jax.ShapeDtypeStruct((count * width, virtuals), BF16),
            jax.ShapeDtypeStruct((count, columns, width), BF16),
            jax.ShapeDtypeStruct((rows, virtuals), F32),
        ],
        in_specs=[smem] * 4 + [vmem] * (2 + count),
        out_specs=[vmem] * 3,
        compiler_params=pltpu.CompilerParams(vmem_limit_bytes=VMEM_LIMIT),
        name="prepare",
    )(place, screen, pair_occ, occ_energy, own_vir, vir, *blocks)


def ladder_kernel(tile, slots, count, place, screen, turned, metric, *rest):
    blocks, halves, outs = (rest[i * count : (i + 1) * count] for i in range(3))
    half, total = rest[3 * count :]
    width = metric.shape[1]
    rows = halves[0].shape[0]
    me = place[0]
    for k in range(count):
        start = pl.multiple_of((me ^ k) * rows, rows)
        half[pl.ds(start, rows), :] = halves[k][...]
    total[...] = jnp.zeros_like(total)
    for k in range(count):
        b = me ^ k
        starts = [pl.multiple_of(screen[b, s] * tile, tile) for s in range(slots)]
        listed = jnp.concatenate([half[pl.ds(start, tile), :] for start in starts], axis=0)
        mixed = jnp.dot(blocks[k][...], listed, preferred_element_type=F32)
        scale = metric[pl.ds(pl.multiple_of(b * width, width), width), :].astype(F32)
        weighted = (scale * mixed).astype(BF16)
        part = jnp.dot(turned[k], weighted, preferred_element_type=F32)
        for s, start in enumerate(starts):
            total[pl.ds(start, tile), :] += part[s * tile : (s + 1) * tile, :]
    for k in range(count):
        start = pl.multiple_of((me ^ k) * rows, rows)
        outs[k][...] = total[pl.ds(start, rows), :].astype(BF16)


def ladders(place, screen, turned, metric, blocks, halves, virtuals, tile):
    count = len(halves)
    rows, width = halves[0].shape
    slots = screen.shape[1]
    smem = pl.BlockSpec(memory_space=pltpu.SMEM)
    vmem = pl.BlockSpec(memory_space=pltpu.VMEM)
    return pl.pallas_call(
        functools.partial(ladder_kernel, tile, slots, count),
        out_shape=[jax.ShapeDtypeStruct((rows, width), BF16)] * count,
        in_specs=[smem] * 2 + [vmem] * (2 + 2 * count),
        out_specs=[vmem] * count,
        scratch_shapes=[pltpu.VMEM((virtuals, width), BF16), pltpu.VMEM((virtuals, width), F32)],
        compiler_params=pltpu.CompilerParams(vmem_limit_bytes=VMEM_LIMIT),
        name="ladders",
    )(place, screen, turned, metric, *blocks, *halves)


def result_kernel(count, chunks, dense, inverse, *rest):
    pieces, out = rest[:count], rest[count]
    joined, staged, sems = rest[count + 1 :]
    width = pieces[0].shape[1]
    part = out.shape[1] // chunks
    for k in range(count):
        joined[:, k * width : (k + 1) * width] = pieces[k][...]
    copies = []
    for j in range(chunks):
        span = slice(j * part, (j + 1) * part)
        value = jnp.dot(joined[...], dense[:, span], preferred_element_type=F32)
        staged[:, span] = value * inverse[:, span]
        copies.append(pltpu.make_async_copy(staged.at[:, span], out.at[:, span], sems.at[j]))
        copies[-1].start()
    for copy in copies:
        copy.wait()


def results(dense, inverse, pieces):
    count = len(pieces)
    rows = pieces[0].shape[0]
    points, virtuals = dense.shape
    chunks = 6 if virtuals % 768 == 0 else 1
    vmem = pl.BlockSpec(memory_space=pltpu.VMEM)
    return pl.pallas_call(
        functools.partial(result_kernel, count, chunks),
        out_shape=jax.ShapeDtypeStruct((rows, virtuals), F32),
        in_specs=[vmem] * (2 + count),
        out_specs=pl.BlockSpec(memory_space=pl.ANY),
        scratch_shapes=[
            pltpu.VMEM((rows, points), BF16),
            pltpu.VMEM((rows, virtuals), F32),
            pltpu.SemaphoreType.DMA((chunks,)),
        ],
        compiler_params=pltpu.CompilerParams(vmem_limit_bytes=VMEM_LIMIT),
        name="results",
    )(dense, inverse, *pieces)


def local(
    grids, pairs, amplitudes, packed_factor, screen, metric, occ_energy, vir_energy, pair_occ
):
    me = lax.axis_index("grid")
    pair = lax.axis_index("pair")
    place = me.astype(jnp.int32).reshape(1)
    _, rows, virtuals = amplitudes.shape
    tile = packed_factor.shape[1] // screen.shape[1]

    block = packed_factor[None]
    step = 2
    while step < pairs:
        other = exchange(block, "pair", pairs, step)
        block = jnp.where(
            pair & step == 0,
            jnp.concatenate([block, other], 0),
            jnp.concatenate([other, block], 0),
        )
        step *= 2
    other = exchange(block, "pair", pairs, 1)
    block = jnp.where(
        pair & 1 == 0, jnp.stack([block, other], 1), jnp.stack([other, block], 1)
    ).reshape(-1, packed_factor.shape[1])
    blocks = [block] + [exchange(block, "grid", grids, k) for k in range(1, grids)]

    packs = pack(place, screen, amplitudes[0], grids, tile)
    halves = [half_product(packs[0], block)]
    for k in range(1, grids):
        half = half_product(packs[k], blocks[k])
        if k + 1 < grids:
            half, blocks[k + 1] = lax.optimization_barrier((half, blocks[k + 1]))
        halves.append(exchange(half, "grid", grids, k))

    own_vir = lax.dynamic_slice_in_dim(vir_energy, me * rows, rows, 0)[:, None]
    dense, turned, inverse = prepare(
        place, screen, pair_occ, occ_energy, own_vir, vir_energy[None, :], blocks, tile
    )
    sent = ladders(place, screen, turned, metric, blocks, halves, virtuals, tile)
    pieces = [sent[0]] + [exchange(sent[k], "grid", grids, k) for k in range(1, grids)]
    return results(dense, inverse, pieces)[None]


def solution(mesh):
    in_specs = (
        P("pair", "grid", None),
        P(("grid", "pair"), None),
        P(),
        P(None, "grid"),
        P(),
        P(),
        P("pair", None),
    )
    return jax.shard_map(
        functools.partial(local, mesh.shape["grid"], mesh.shape["pair"]),
        mesh=mesh,
        in_specs=in_specs,
        out_specs=P("pair", "grid", None),
        check_vma=False,
    )
```

time: 97 us -> 41.5 us (0.43)
  Pallas kernels: 55.4 us -> 6.43 us
  waiting for transfers between devices: 22.7 us -> 13.8 us
  other arithmetic: 0.05 us -> 1.63 us
  local copies, waits for them, and re-layouts: 1.02 us -> 2.18 us
    pallas_call x1, Pallas kernels: 49.7 us -> 1.06 us  [pack(): pl.pallas_call(functools.partial(pack_kernel, tile, slots, count), out_sh...]
    ppermute x13 -> x12, waiting for transfers between devices: 22.7 us -> 13.8 us  [exchange(): return lax.ppermute(value, axis, [(i, i ^ step) for i in range(size)])]
    unnamed x12 -> x14, local copies, waits for them, and re-layouts: 0.03 us -> 1.97 us
    ppermute x13 -> x12, starting transfers between devices: 17.4 us -> 16.8 us  [exchange(): return lax.ppermute(value, axis, [(i, i ^ step) for i in range(size)])]
    pallas_call x2 -> x6, Pallas kernels: 3.89 us -> 4.12 us  [the longest x1 1.84 us: results(): pl.pallas_call(functools.partial(result_kernel, count, chunks), out_shape...]
  transfers between devices with their start and end apart: 13 -> 12, of which waited for: 6 -> 10; matrix products, arithmetic and copies ran while one was open for 1% -> 2% of each run, Pallas kernels for 52% -> 8%
where the time goes in v2:
time: 41.5 us; the launch traced here: 41 us
  starting transfers between devices  16.8 us (40%)
  waiting for transfers between devices  13.8 us (33%)
  Pallas kernels  6.43 us (15%)
  local copies, waits for them, and re-layouts  2.18 us (5%)
  other arithmetic  1.63 us (4%)
    ppermute x12, starting transfers between devices, exchange(): return lax.ppermute(value, axis, [(i, i ^ step) for i in range(size)])  16.8 us
    ppermute x12, waiting for transfers between devices, exchange(): return lax.ppermute(value, axis, [(i, i ^ step) for i in range(size)])  13.8 us
    unnamed x14, local copies, waits for them, and re-layouts  1.97 us
    pallas_call x1, Pallas kernels, results(): pl.pallas_call(functools.partial(result_kernel, count, chunks), out_shape...  1.84 us
    pallas_call x1, Pallas kernels, ladders(): pl.pallas_call(functools.partial(ladder_kernel, tile, slots, count), out_...  1.25 us
    pallas_call x1, Pallas kernels, prepare(): pl.pallas_call(functools.partial(prepare_kernel, tile, screen.shape[1], c...  1.25 us
    pallas_call x1, Pallas kernels, pack(): pl.pallas_call(functools.partial(pack_kernel, tile, slots, count), out_sh...  1.06 us
    pallas_call x4, Pallas kernels, half_product(): pl.pallas_call(half_kernel, out_shape=jax.ShapeDtypeStruct((rows, width),...  1.03 us
  transfers between devices with their start and end apart: 12, of which 10 were waited for; matrix products, arithmetic and copies ran while one was open for 2% of the time, Pallas kernels for 8%

profile of v2, /device:TPU:0, one launch (start us, length us, event | category | flops | bytes accessed | tf_op | source)
XLA Modules:
  0.0 41.0 jit_solution(1412106600138703837)
XLA Ops:
  0.0 3.0 %collective-permute-start = (bf16[1,16,512]{2,1,0:T(8,128)(2,1)}, bf16[1,16,512]{2,1,0:T(8,128)(2,1)S(1)}, u32[]{:S(2)}, u32[]{:S(2)}) collective-permute-start(bf16[1,16,512]{2,1,0:T(8,128)(2,1)} %bitcast.18), channel_id=1, source_target_pairs={{0,2},{1,3},{2,0},{3,1},{4,6},{5,7},{6,4},{7,5},{8,10},{9,11},{10,... | collective-permute-start | bytes 49160 | tf_op jit(solution)/shard_map/ppermute | solution.py:16
  3.0 1.9 %collective-permute-done = bf16[1,16,512]{2,1,0:T(8,128)(2,1)S(1)} collective-permute-done((bf16[1,16,512]{2,1,0:T(8,128)(2,1)}, bf16[1,16,512]{2,1,0:T(8,128)(2,1)S(1)}, u32[]{:S(2)}, u32[]{:S(2)}) %collective-permute-start) | collective-permute-done | bytes 16416 | tf_op jit(solution)/shard_map/ppermute | solution.py:16
  5.0 0.8 %maximum_select_fusion.3 = bf16[2,16,512]{2,1,0:T(8,128)(2,1)S(1)} fusion(bf16[1,16,512]{2,1,0:T(8,128)(2,1)S(1)} %collective-permute-done, bf16[1,16,512]{2,1,0:T(8,128)(2,1)} %bitcast.19, pred[]{:T(512)S(6)} %eq.11), kind=kLoop, calls=%fused_computation.3 | loop fusion | flops 49152 | bytes 65537 | tf_op jit(solution)/shard_map/jit(_where)/select_n | solution.py:213
  5.8 3.0 %collective-permute-start.1 = (bf16[2,16,512]{2,1,0:T(8,128)(2,1)S(1)}, bf16[2,16,512]{2,1,0:T(8,128)(2,1)S(1)}, u32[]{:S(2)}, u32[]{:S(2)}) collective-permute-start(bf16[2,16,512]{2,1,0:T(8,128)(2,1)S(1)} %maximum_select_fusion.3), channel_id=1, source_target_pairs={{0,4},{1,5},{2,6},{3,7},{4,0},{5,1},{6,2},{7,3},{8,12},{9,13},{10,... | collective-permute-start | bytes 98312 | tf_op jit(solution)/shard_map/ppermute | solution.py:16
  8.8 0.8 %fusion = bf16[2,1,16,512]{3,2,0,1:T(8,128)(2,1)S(1)} fusion(bf16[1,16,512]{2,1,0:T(8,128)(2,1)} %bitcast.20, bf16[1,16,512]{2,1,0:T(8,128)(2,1)S(1)} %collective-permute-done, pred[]{:T(512)S(6)} %eq.11), kind=kLoop, calls=%fused_computation.4 | loop fusion | flops 49152 | bytes 65537 | tf_op jit(solution)/shard_map/concatenate | solution.py:215
  9.6 1.1 %collective-permute-done.1 = bf16[2,16,512]{2,1,0:T(8,128)(2,1)S(1)} collective-permute-done((bf16[2,16,512]{2,1,0:T(8,128)(2,1)S(1)}, bf16[2,16,512]{2,1,0:T(8,128)(2,1)S(1)}, u32[]{:S(2)}, u32[]{:S(2)}) %collective-permute-start.1) | collective-permute-done | bytes 32800 | tf_op jit(solution)/shard_map/ppermute | solution.py:16
  10.8 1.2 %collective-permute-done.2 = bf16[4,16,512]{2,1,0:T(8,128)(2,1)S(1)} collective-permute-done((bf16[4,16,512]{2,1,0:T(8,128)(2,1)S(1)}, bf16[4,16,512]{2,1,0:T(8,128)(2,1)S(1)}, u32[]{:S(2)}, u32[]{:S(2)}) %collective-permute-start.2) | collective-permute-done | bytes 65568 | tf_op jit(solution)/shard_map/ppermute | solution.py:16
  12.1 1.9 %collective-permute-start.3 = (bf16[128,512]{1,0:T(8,128)(2,1)S(1)}, bf16[128,512]{1,0:T(8,128)(2,1)S(1)}, u32[]{:S(2)}, u32[]{:S(2)}) collective-permute-start(bf16[128,512]{1,0:T(8,128)(2,1)S(1)} %bitcast.9), channel_id=1, source_target_pairs={{0,8},{8,0},{16,24},{24,16},{1,9},{9,1},{17,25},{25,17},{2,10},{10... | collective-permute-start | bytes 393224 | tf_op jit(solution)/shard_map/ppermute | solution.py:16
  14.0 1.5 %collective-permute-start.4 = (bf16[128,512]{1,0:T(8,128)(2,1)S(1)}, bf16[128,512]{1,0:T(8,128)(2,1)S(1)}, u32[]{:S(2)}, u32[]{:S(2)}) collective-permute-start(bf16[128,512]{1,0:T(8,128)(2,1)S(1)} %bitcast.10), channel_id=1, source_target_pairs={{0,16},{8,24},{16,0},{24,8},{1,17},{9,25},{17,1},{25,9},{2,18},{10... | collective-permute-start | bytes 393224 | tf_op jit(solution)/shard_map/ppermute | solution.py:16
  15.5 0.1 collective-permute-start.5
  15.6 1.3 %copy-done = bf16[1,384,1536]{2,1,0:T(8,128)(2,1)S(1)} copy-done((bf16[1,384,1536]{2,1,0:T(8,128)(2,1)S(1)}, bf16[1,384,1536]{2,1,0:T(8,128)(2,1)}, u32[]{:S(2)}) %copy-start) | copy-done | bytes 1179672
  16.9 0.7 %copy-done.2 = s32[4,4]{1,0:T(4,128)S(1)} copy-done((s32[4,4]{1,0:T(4,128)S(1)}, s32[4,4]{1,0:T(4,128)}, u32[]{:S(2)}) %copy-start.2) | copy-done | bytes 88
  17.6 1.1 %pack.1 = (bf16[384,512]{1,0:T(8,128)(2,1)S(1)}, bf16[384,512]{1,0:T(8,128)(2,1)S(1)}, bf16[384,512]{1,0:T(8,128)(2,1)S(1)}, bf16[384,512]{1,0:T(8,128)(2,1)S(1)}) custom-call(s32[1]{0:T(128)} %bitcast.place, s32[4,4]{1,0:T(4,128)S(1)} %copy-done.2, bf16[384,1536]{1,0:T(8,128)(2,1)S(1)} %bitcast.15), custom_call_target="tpu_custom_call" | custom-call | bytes 3145728 | tf_op jit(solution)/shard_map/pack/pallas_call | solution.py:42
  18.6 0.3 half_product.4
  18.9 3.1 %collective-permute-done.4.block.rest_2_ = bf16[128,512]{1,0:T(8,128)(2,1)S(1)} collective-permute-done((bf16[128,512]{1,0:T(8,128)(2,1)S(1)}, bf16[128,512]{1,0:T(8,128)(2,1)S(1)}, u32[]{:S(2)}, u32[]{:S(2)}) %collective-permute-start.4) | collective-permute-done | bytes 131104 | tf_op jit(solution)/shard_map/ppermute | solution.py:16
  22.0 0.3 half_product.5
  22.3 1.6 %collective-permute-start.7 = (bf16[384,128]{1,0:T(8,128)(2,1)S(1)}, bf16[384,128]{1,0:T(8,128)(2,1)S(1)}, u32[]{:S(2)}, u32[]{:S(2)}) collective-permute-start(bf16[384,128]{1,0:T(8,128)(2,1)S(1)} %half_product.5), channel_id=1, source_target_pairs={{0,16},{8,24},{16,0},{24,8},{1,17},{9,25},{17,1},{25,9},{2,18},{10... | collective-permute-start | bytes 294920 | tf_op jit(solution)/shard_map/ppermute | solution.py:16
  23.9 0.3 half_product.7
  24.2 0.9 %collective-permute-start.8 = (bf16[384,128]{1,0:T(8,128)(2,1)S(1)}, bf16[384,128]{1,0:T(8,128)(2,1)S(1)}, u32[]{:S(2)}, u32[]{:S(2)}) collective-permute-start(bf16[384,128]{1,0:T(8,128)(2,1)S(1)} %half_product.7), channel_id=1, source_target_pairs={{0,24},{8,16},{16,8},{24,0},{1,25},{9,17},{17,9},{25,1},{2,26},{10... | collective-permute-start | bytes 294920 | tf_op jit(solution)/shard_map/ppermute | solution.py:16
  25.1 1.1 %collective-permute-start.6 = (bf16[384,128]{1,0:T(8,128)(2,1)S(1)}, bf16[384,128]{1,0:T(8,128)(2,1)S(1)}, u32[]{:S(2)}, u32[]{:S(2)}) collective-permute-start(bf16[384,128]{1,0:T(8,128)(2,1)S(1)} %half_product.4), channel_id=1, source_target_pairs={{0,8},{8,0},{16,24},{24,16},{1,9},{9,1},{17,25},{25,17},{2,10},{10... | collective-permute-start | bytes 294920 | tf_op jit(solution)/shard_map/ppermute | solution.py:16
  26.3 0.1 broadcast_in_dim.13.own_vir
  26.4 0.3 half_product.6.rest_4_
  26.7 1.2 %prepare.1 = (bf16[512,1536]{1,0:T(8,128)(2,1)S(1)}, bf16[4,512,128]{2,1,0:T(8,128)(2,1)S(1)}, f32[384,1536]{1,0:T(8,128)S(1)}) custom-call(s32[1]{0:T(128)} %bitcast.place, s32[4,4]{1,0:T(4,128)S(1)} %copy-done.3, s32[1,2]{1,0:T(1,128)S(1)} %copy-done.5, f32[300]{0:T(512)S(1)} %copy-done.4, f32[384,1]{1,0:T(8,128)S(1)} %broadcast_in_dim.13.own_vir, ...), custom_call_target="tpu_custom_call" | custom-call | tf_op jit(solution)/shard_map/prepare/pallas_call | solution.py:105
  28.1 1.7 %collective-permute-done.8.rest_7_ = bf16[384,128]{1,0:T(8,128)(2,1)S(1)} collective-permute-done((bf16[384,128]{1,0:T(8,128)(2,1)S(1)}, bf16[384,128]{1,0:T(8,128)(2,1)S(1)}, u32[]{:S(2)}, u32[]{:S(2)}) %collective-permute-start.8) | collective-permute-done | bytes 98336 | tf_op jit(solution)/shard_map/ppermute | solution.py:16
  29.8 1.3 %ladders.1 = (bf16[384,128]{1,0:T(8,128)(2,1)S(1)}, bf16[384,128]{1,0:T(8,128)(2,1)S(1)}, bf16[384,128]{1,0:T(8,128)(2,1)S(1)}, bf16[384,128]{1,0:T(8,128)(2,1)S(1)}) custom-call(s32[1]{0:T(128)} %bitcast.place, s32[4,4]{1,0:T(4,128)S(1)} %copy-done.3, bf16[4,512,128]{2,1,0:T(8,128)(2,1)S(1)} %get-tuple-element.26.turned, bf16[512,128]{1,0:T(8,128)(2,1)S(1)} %copy-done.1, ...), custom_call_target="tpu_custom_call" | custom-call | tf_op jit(solution)/shard_map/ladders/pallas_call | solution.py:150
  31.1 1.2 %collective-permute-start.9 = (bf16[384,128]{1,0:T(8,128)(2,1)S(1)}, bf16[384,128]{1,0:T(8,128)(2,1)S(1)}, u32[]{:S(2)}, u32[]{:S(2)}) collective-permute-start(bf16[384,128]{1,0:T(8,128)(2,1)S(1)} %get-tuple-element.32), channel_id=1, source_target_pairs={{0,8},{8,0},{16,24},{24,16},{1,9},{9,1},{17,25},{25,17},{2,10},{10... | collective-permute-start | bytes 294920 | tf_op jit(solution)/shard_map/ppermute | solution.py:16
  32.3 1.4 %collective-permute-start.10 = (bf16[384,128]{1,0:T(8,128)(2,1)S(1)}, bf16[384,128]{1,0:T(8,128)(2,1)S(1)}, u32[]{:S(2)}, u32[]{:S(2)}) collective-permute-start(bf16[384,128]{1,0:T(8,128)(2,1)S(1)} %get-tuple-element.33), channel_id=1, source_target_pairs={{0,16},{8,24},{16,0},{24,8},{1,17},{9,25},{17,1},{25,9},{2,18},{10... | collective-permute-start | bytes 294920 | tf_op jit(solution)/shard_map/ppermute | solution.py:16
  33.7 1.0 %collective-permute-start.11 = (bf16[384,128]{1,0:T(8,128)(2,1)S(1)}, bf16[384,128]{1,0:T(8,128)(2,1)S(1)}, u32[]{:S(2)}, u32[]{:S(2)}) collective-permute-start(bf16[384,128]{1,0:T(8,128)(2,1)S(1)} %get-tuple-element.34), channel_id=1, source_target_pairs={{0,24},{8,16},{16,8},{24,0},{1,25},{9,17},{17,9},{25,1},{2,26},{10... | collective-permute-start | bytes 294920 | tf_op jit(solution)/shard_map/ppermute | solution.py:16
  34.7 1.2 %collective-permute-done.9.rest_1_ = bf16[384,128]{1,0:T(8,128)(2,1)S(1)} collective-permute-done((bf16[384,128]{1,0:T(8,128)(2,1)S(1)}, bf16[384,128]{1,0:T(8,128)(2,1)S(1)}, u32[]{:S(2)}, u32[]{:S(2)}) %collective-permute-start.9) | collective-permute-done | bytes 98336 | tf_op jit(solution)/shard_map/ppermute | solution.py:16
  35.9 1.1 %collective-permute-done.10.rest_2_ = bf16[384,128]{1,0:T(8,128)(2,1)S(1)} collective-permute-done((bf16[384,128]{1,0:T(8,128)(2,1)S(1)}, bf16[384,128]{1,0:T(8,128)(2,1)S(1)}, u32[]{:S(2)}, u32[]{:S(2)}) %collective-permute-start.10) | collective-permute-done | bytes 98336 | tf_op jit(solution)/shard_map/ppermute | solution.py:16
  36.9 2.3 %collective-permute-done.11.rest_3_ = bf16[384,128]{1,0:T(8,128)(2,1)S(1)} collective-permute-done((bf16[384,128]{1,0:T(8,128)(2,1)S(1)}, bf16[384,128]{1,0:T(8,128)(2,1)S(1)}, u32[]{:S(2)}, u32[]{:S(2)}) %collective-permute-start.11) | collective-permute-done | bytes 98336 | tf_op jit(solution)/shard_map/ppermute | solution.py:16
  39.2 1.8 %results.1 = f32[384,1536]{1,0:T(8,128)} custom-call(bf16[512,1536]{1,0:T(8,128)(2,1)S(1)} %get-tuple-element.24.dense, f32[384,1536]{1,0:T(8,128)S(1)} %get-tuple-element.25.inverse, bf16[384,128]{1,0:T(8,128)(2,1)S(1)} %get-tuple-element.31.rest_0_, bf16[384,128]{1,0:T(8,128)(2,1)S(1)} %collective-permute-done.9.rest_1_, ...), custom_call_target="tpu_custom_call" | custom-call | tf_op jit(solution)/shard_map/results/pallas_call | solution.py:185
  (23 shorter events, 0.4 us)
Async XLA Ops:
  0.0 26.2 %copy-start.6 = (f32[1536]{0:T(1024)S(1)}, f32[1536]{0:T(1024)}, u32[]{:S(2)}) copy-start(f32[1536]{0:T(1024)} %param.12) | copy-start | bytes 18436
  0.0 5.0 %collective-permute-start = (bf16[1,16,512]{2,1,0:T(8,128)(2,1)}, bf16[1,16,512]{2,1,0:T(8,128)(2,1)S(1)}, u32[]{:S(2)}, u32[]{:S(2)}) collective-permute-start(bf16[1,16,512]{2,1,0:T(8,128)(2,1)} %bitcast.18), channel_id=1, source_target_pairs={{0,2},{1,3},{2,0},{3,1},{4,6},{5,7},{6,4},{7,5},{8,10},{9,11},{10,... | collective-permute-start | bytes 49160 | tf_op jit(solution)/shard_map/ppermute | solution.py:16
  5.8 4.9 %collective-permute-start.1 = (bf16[2,16,512]{2,1,0:T(8,128)(2,1)S(1)}, bf16[2,16,512]{2,1,0:T(8,128)(2,1)S(1)}, u32[]{:S(2)}, u32[]{:S(2)}) collective-permute-start(bf16[2,16,512]{2,1,0:T(8,128)(2,1)S(1)} %maximum_select_fusion.3), channel_id=1, source_target_pairs={{0,4},{1,5},{2,6},{3,7},{4,0},{5,1},{6,2},{7,3},{8,12},{9,13},{10,... | collective-permute-start | bytes 98312 | tf_op jit(solution)/shard_map/ppermute | solution.py:16
  9.6 17.1 %copy-start.3 = (s32[4,4]{1,0:T(4,128)S(1)}, s32[4,4]{1,0:T(4,128)}, u32[]{:S(2)}) copy-start(s32[4,4]{1,0:T(4,128)} %screen.5) | copy-start | bytes 196
  9.6 17.1 %copy-start.4 = (f32[300]{0:T(512)S(1)}, f32[300]{0:T(512)}, u32[]{:S(2)}) copy-start(f32[300]{0:T(512)} %occ_energy.1) | copy-start | bytes 3604
  9.6 17.1 %copy-start.5 = (s32[1,2]{1,0:T(1,128)S(1)}, s32[1,2]{1,0:T(1,128)}, u32[]{:S(2)}) copy-start(s32[1,2]{1,0:T(1,128)} %pair_occ.1) | copy-start | bytes 28
  10.7 1.3 %collective-permute-start.2 = (bf16[4,16,512]{2,1,0:T(8,128)(2,1)S(1)}, bf16[4,16,512]{2,1,0:T(8,128)(2,1)S(1)}, u32[]{:S(2)}, u32[]{:S(2)}) collective-permute-start(bf16[4,16,512]{2,1,0:T(8,128)(2,1)S(1)} %maximum_select_fusion.2), channel_id=1, source_target_pairs={{0,1},{1,0},{2,3},{3,2},{4,5},{5,4},{6,7},{7,6},{8,9},{9,8},{10,11... | collective-permute-start | bytes 196616 | tf_op jit(solution)/shard_map/ppermute | solution.py:16
  12.0 17.8 %copy-start.1 = (bf16[512,128]{1,0:T(8,128)(2,1)S(1)}, bf16[512,128]{1,0:T(8,128)(2,1)}, u32[]{:S(2)}) copy-start(bf16[512,128]{1,0:T(8,128)(2,1)} %metric.1) | copy-start | bytes 393220
  12.1 6.6 %collective-permute-start.3 = (bf16[128,512]{1,0:T(8,128)(2,1)S(1)}, bf16[128,512]{1,0:T(8,128)(2,1)S(1)}, u32[]{:S(2)}, u32[]{:S(2)}) collective-permute-start(bf16[128,512]{1,0:T(8,128)(2,1)S(1)} %bitcast.9), channel_id=1, source_target_pairs={{0,8},{8,0},{16,24},{24,16},{1,9},{9,1},{17,25},{25,17},{2,10},{10... | collective-permute-start | bytes 393224 | tf_op jit(solution)/shard_map/ppermute | solution.py:16
  14.0 8.1 %collective-permute-start.4 = (bf16[128,512]{1,0:T(8,128)(2,1)S(1)}, bf16[128,512]{1,0:T(8,128)(2,1)S(1)}, u32[]{:S(2)}, u32[]{:S(2)}) collective-permute-start(bf16[128,512]{1,0:T(8,128)(2,1)S(1)} %bitcast.10), channel_id=1, source_target_pairs={{0,16},{8,24},{16,0},{24,8},{1,17},{9,25},{17,1},{25,9},{2,18},{10... | collective-permute-start | bytes 393224 | tf_op jit(solution)/shard_map/ppermute | solution.py:16
  15.5 6.8 %collective-permute-start.5 = (bf16[128,512]{1,0:T(8,128)(2,1)S(1)}, bf16[128,512]{1,0:T(8,128)(2,1)S(1)}, u32[]{:S(2)}, u32[]{:S(2)}) collective-permute-start(bf16[128,512]{1,0:T(8,128)(2,1)S(1)} %bitcast.11), channel_id=1, source_target_pairs={{0,24},{8,16},{16,8},{24,0},{1,25},{9,17},{17,9},{25,1},{2,26},{10... | collective-permute-start | bytes 393224 | tf_op jit(solution)/shard_map/ppermute | solution.py:16
  15.6 1.3 %copy-start = (bf16[1,384,1536]{2,1,0:T(8,128)(2,1)S(1)}, bf16[1,384,1536]{2,1,0:T(8,128)(2,1)}, u32[]{:S(2)}) copy-start(bf16[1,384,1536]{2,1,0:T(8,128)(2,1)} %param.7) | copy-start | bytes 3538948
  16.9 0.7 %copy-start.2 = (s32[4,4]{1,0:T(4,128)S(1)}, s32[4,4]{1,0:T(4,128)}, u32[]{:S(2)}) copy-start(s32[4,4]{1,0:T(4,128)} %screen.5) | copy-start | bytes 196
  22.3 5.7 %collective-permute-start.7 = (bf16[384,128]{1,0:T(8,128)(2,1)S(1)}, bf16[384,128]{1,0:T(8,128)(2,1)S(1)}, u32[]{:S(2)}, u32[]{:S(2)}) collective-permute-start(bf16[384,128]{1,0:T(8,128)(2,1)S(1)} %half_product.5), channel_id=1, source_target_pairs={{0,16},{8,24},{16,0},{24,8},{1,17},{9,25},{17,1},{25,9},{2,18},{10... | collective-permute-start | bytes 294920 | tf_op jit(solution)/shard_map/ppermute | solution.py:16
  24.2 5.6 %collective-permute-start.8 = (bf16[384,128]{1,0:T(8,128)(2,1)S(1)}, bf16[384,128]{1,0:T(8,128)(2,1)S(1)}, u32[]{:S(2)}, u32[]{:S(2)}) collective-permute-start(bf16[384,128]{1,0:T(8,128)(2,1)S(1)} %half_product.7), channel_id=1, source_target_pairs={{0,24},{8,16},{16,8},{24,0},{1,25},{9,17},{17,9},{25,1},{2,26},{10... | collective-permute-start | bytes 294920 | tf_op jit(solution)/shard_map/ppermute | solution.py:16
  25.1 4.8 %collective-permute-start.6 = (bf16[384,128]{1,0:T(8,128)(2,1)S(1)}, bf16[384,128]{1,0:T(8,128)(2,1)S(1)}, u32[]{:S(2)}, u32[]{:S(2)}) collective-permute-start(bf16[384,128]{1,0:T(8,128)(2,1)S(1)} %half_product.4), channel_id=1, source_target_pairs={{0,8},{8,0},{16,24},{24,16},{1,9},{9,1},{17,25},{25,17},{2,10},{10... | collective-permute-start | bytes 294920 | tf_op jit(solution)/shard_map/ppermute | solution.py:16
  31.1 4.7 %collective-permute-start.9 = (bf16[384,128]{1,0:T(8,128)(2,1)S(1)}, bf16[384,128]{1,0:T(8,128)(2,1)S(1)}, u32[]{:S(2)}, u32[]{:S(2)}) collective-permute-start(bf16[384,128]{1,0:T(8,128)(2,1)S(1)} %get-tuple-element.32), channel_id=1, source_target_pairs={{0,8},{8,0},{16,24},{24,16},{1,9},{9,1},{17,25},{25,17},{2,10},{10... | collective-permute-start | bytes 294920 | tf_op jit(solution)/shard_map/ppermute | solution.py:16
  32.3 4.6 %collective-permute-start.10 = (bf16[384,128]{1,0:T(8,128)(2,1)S(1)}, bf16[384,128]{1,0:T(8,128)(2,1)S(1)}, u32[]{:S(2)}, u32[]{:S(2)}) collective-permute-start(bf16[384,128]{1,0:T(8,128)(2,1)S(1)} %get-tuple-element.33), channel_id=1, source_target_pairs={{0,16},{8,24},{16,0},{24,8},{1,17},{9,25},{17,1},{25,9},{2,18},{10... | collective-permute-start | bytes 294920 | tf_op jit(solution)/shard_map/ppermute | solution.py:16
  33.7 5.5 %collective-permute-start.11 = (bf16[384,128]{1,0:T(8,128)(2,1)S(1)}, bf16[384,128]{1,0:T(8,128)(2,1)S(1)}, u32[]{:S(2)}, u32[]{:S(2)}) collective-permute-start(bf16[384,128]{1,0:T(8,128)(2,1)S(1)} %get-tuple-element.34), channel_id=1, source_target_pairs={{0,24},{8,16},{16,8},{24,0},{1,25},{9,17},{17,9},{25,1},{2,26},{10... | collective-permute-start | bytes 294920 | tf_op jit(solution)/shard_map/ppermute | solution.py:16

commit v3 on v2

v3 whole, which is shorter than its diff:
```python
import functools

import jax
import jax.numpy as jnp
from jax import lax
from jax.experimental import pallas as pl
from jax.experimental.pallas import tpu as pltpu
from jax.sharding import PartitionSpec as P

BF16 = jnp.bfloat16
F32 = jnp.float32
VMEM_LIMIT = 40 * 1024 * 1024


def exchange(value, axis, size, step):
    return lax.ppermute(value, axis, [(i, i ^ step) for i in range(size)])


def keep_kernel(value, out):
    out[...] = value[...]


def keep(value):
    vmem = pl.BlockSpec(memory_space=pltpu.VMEM)
    return pl.pallas_call(
        keep_kernel,
        out_shape=pltpu.VMEM(value.shape, value.dtype),
        in_specs=[vmem],
        out_specs=vmem,
        name="keep",
    )(value)


def pack_kernel(tile, slots, count, place, screen, amplitudes, *rest):
    outs, sems = rest[:count], rest[count]
    copies = []
    for k in range(count):
        block = place[0] ^ k
        for s in range(slots):
            column = pl.multiple_of(screen[block, s] * tile, tile)
            copies.append(
                pltpu.make_async_copy(
                    amplitudes.at[:, pl.ds(column, tile)],
                    outs[k].at[:, pl.ds(s * tile, tile)],
                    sems.at[k * slots + s],
                )
            )
    for copy in copies:
        copy.start()
    for copy in copies:
        copy.wait()


def pack(place, screen, amplitudes, tile):
    rows = amplitudes.shape[0]
    count, slots = screen.shape
    smem = pl.BlockSpec(memory_space=pltpu.SMEM)
    hbm = pl.BlockSpec(memory_space=pltpu.HBM)
    return pl.pallas_call(
        functools.partial(pack_kernel, tile, slots, count),
        out_shape=[jax.ShapeDtypeStruct((rows, slots * tile), BF16)] * count,
        in_specs=[smem] * 2 + [hbm],
        out_specs=[pl.BlockSpec(memory_space=pltpu.VMEM)] * count,
        scratch_shapes=[pltpu.SemaphoreType.DMA((count * slots,))],
        cost_estimate=pl.CostEstimate(
            flops=0, bytes_accessed=4 * count * rows * slots * tile, transcendentals=0
        ),
        compiler_params=pltpu.CompilerParams(vmem_limit_bytes=VMEM_LIMIT),
        name="pack",
    )(place, screen, amplitudes)


def half_kernel(count, packed, *rest):
    listed, outs = rest[:count], rest[count:]
    width = packed.shape[0] // count
    for k in range(count):
        outs[k][...] = lax.dot_general(
            listed[k][...],
            packed[k * width : (k + 1) * width, :],
            (((1,), (1,)), ((), ())),
            preferred_element_type=F32,
        ).astype(BF16)


def half_products(packed, listed):
    count = len(listed)
    rows, columns = listed[0].shape
    width = packed.shape[0] // count
    vmem = pl.BlockSpec(memory_space=pltpu.VMEM)
    return pl.pallas_call(
        functools.partial(half_kernel, count),
        out_shape=[jax.ShapeDtypeStruct((rows, width), BF16)] * count,
        in_specs=[vmem] * (1 + count),
        out_specs=[vmem] * count,
        compiler_params=pltpu.CompilerParams(vmem_limit_bytes=VMEM_LIMIT),
        name="half_products",
    )(packed, *listed)


def prepare_kernel(tile, slots, count, place, screen, pair_occ, occ_energy, *rest):
    packed, metric, own_vir, vir, dense, turned, scale, inverse = rest
    width = packed.shape[0] // count
    dense[...] = jnp.zeros_like(dense)
    turned[...] = jnp.zeros_like(turned)
    for k in range(count):
        b = place[0] ^ k
        span = slice(k * width, (k + 1) * width)
        block = packed[span, :]
        other = block.T
        for s in range(slots):
            start = pl.multiple_of(screen[b, s] * tile, tile)
            dense[span, pl.ds(start, tile)] = block[:, s * tile : (s + 1) * tile]
            turned[pl.ds(start, tile), span] = other[s * tile : (s + 1) * tile, :]
        scale[:, span] = metric[pl.ds(pl.multiple_of(b * width, width), width), :].astype(F32).T
    occ_total = occ_energy[pair_occ[0, 0]] + occ_energy[pair_occ[0, 1]]
    inverse[...] = 1.0 / ((own_vir[...] + vir[...]) - occ_total)


def prepare(place, screen, pair_occ, occ_energy, packed, metric, own_vir, vir, tile):
    count, slots = screen.shape
    points = packed.shape[0]
    rows, virtuals = own_vir.shape[0], vir.shape[1]
    smem = pl.BlockSpec(memory_space=pltpu.SMEM)
    vmem = pl.BlockSpec(memory_space=pltpu.VMEM)
    return pl.pallas_call(
        functools.partial(prepare_kernel, tile, slots, count),
        out_shape=[
            jax.ShapeDtypeStruct((points, virtuals), BF16),
            jax.ShapeDtypeStruct((virtuals, points), BF16),
            jax.ShapeDtypeStruct((metric.shape[1], points), F32),
            jax.ShapeDtypeStruct((rows, virtuals), F32),
        ],
        in_specs=[smem] * 4 + [vmem] * 4,
        out_specs=[vmem] * 4,
        cost_estimate=pl.CostEstimate(
            flops=0, bytes_accessed=8 * points * virtuals, transcendentals=0
        ),
        compiler_params=pltpu.CompilerParams(vmem_limit_bytes=VMEM_LIMIT),
        name="prepare",
    )(place, screen, pair_occ, occ_energy, packed, metric, own_vir, vir)


def mixed_part(half, factor):
    return lax.dot_general(half, factor, (((0,), (0,)), ((), ())), preferred_element_type=F32)


def mixed_kernel(known, place, turned, *rest):
    halves, out = rest[:known], rest[known]
    rows = halves[0].shape[0]
    total = None
    for k in range(known):
        start = pl.multiple_of((place[0] ^ k) * rows, rows)
        part = mixed_part(halves[k][...], turned[pl.ds(start, rows), :])
        total = part if total is None else total + part
    out[...] = total


def mixed_sum(place, turned, halves):
    known = len(halves)
    width, points = halves[0].shape[1], turned.shape[1]
    vmem = pl.BlockSpec(memory_space=pltpu.VMEM)
    return pl.pallas_call(
        functools.partial(mixed_kernel, known),
        out_shape=jax.ShapeDtypeStruct((width, points), F32),
        in_specs=[pl.BlockSpec(memory_space=pltpu.SMEM)] + [vmem] * (1 + known),
        out_specs=vmem,
        cost_estimate=pl.CostEstimate(
            flops=2 * known * halves[0].size * points, bytes_accessed=0, transcendentals=0
        ),
        compiler_params=pltpu.CompilerParams(vmem_limit_bytes=VMEM_LIMIT),
        name="mixed",
    )(place, turned, *halves)


def ladder_kernel(count, turned, scale, mixed, half, *outs):
    me = lax.axis_index("grid")
    rows = half.shape[0]
    start = pl.multiple_of((me ^ (count - 1)) * rows, rows)
    total = mixed[...] + mixed_part(half[...], turned[pl.ds(start, rows), :])
    weighted = (scale[...] * total).astype(BF16)
    for k in list(range(1, count)) + [0]:
        start = pl.multiple_of((me ^ k) * rows, rows)
        outs[k][...] = lax.dot_general(
            turned[pl.ds(start, rows), :],
            weighted,
            (((1,), (1,)), ((), ())),
            preferred_element_type=F32,
        ).astype(BF16)


def ladders(turned, scale, mixed, half, count):
    rows, width = half.shape
    vmem = pl.BlockSpec(memory_space=pltpu.VMEM)
    return pl.pallas_call(
        functools.partial(ladder_kernel, count),
        out_shape=[jax.ShapeDtypeStruct((rows, width), BF16)] * count,
        in_specs=[vmem] * 4,
        out_specs=[vmem] * count,
        compiler_params=pltpu.CompilerParams(vmem_limit_bytes=VMEM_LIMIT),
        name="ladders",
    )(turned, scale, mixed, half)


def start_kernel(dense, *rest):
    pieces, out = rest[:-1], rest[-1]
    joined = jnp.concatenate([piece[...] for piece in pieces], axis=1)
    out[...] = jnp.dot(joined, dense[: joined.shape[1], :], preferred_element_type=F32)


def result_start(dense, pieces):
    rows, width = pieces[0].shape
    vmem = pl.BlockSpec(memory_space=pltpu.VMEM)
    return pl.pallas_call(
        start_kernel,
        out_shape=jax.ShapeDtypeStruct((rows, dense.shape[1]), F32),
        in_specs=[vmem] * (1 + len(pieces)),
        out_specs=vmem,
        cost_estimate=pl.CostEstimate(
            flops=2 * len(pieces) * rows * width * dense.shape[1],
            bytes_accessed=0,
            transcendentals=0,
        ),
        compiler_params=pltpu.CompilerParams(vmem_limit_bytes=VMEM_LIMIT),
        name="result_start",
    )(dense, *pieces)


def result_kernel(chunks, begun, dense, inverse, *rest):
    *pieces, out, staged, sems = rest
    joined = jnp.concatenate([piece[...] for piece in pieces], axis=1)
    first = dense.shape[0] - joined.shape[1]
    part = out.shape[1] // chunks
    copies = []
    for j in range(chunks):
        span = slice(j * part, (j + 1) * part)
        value = jnp.dot(joined, dense[first:, span], preferred_element_type=F32)
        staged[:, span] = (begun[:, span] + value) * inverse[:, span]
        copies.append(pltpu.make_async_copy(staged.at[:, span], out.at[:, span], sems.at[j]))
        copies[-1].start()
    for copy in copies:
        copy.wait()


def results(begun, dense, inverse, pieces):
    rows, virtuals = begun.shape
    chunks = 6 if virtuals % 768 == 0 else 1
    vmem = pl.BlockSpec(memory_space=pltpu.VMEM)
    return pl.pallas_call(
        functools.partial(result_kernel, chunks),
        out_shape=jax.ShapeDtypeStruct((rows, virtuals), F32),
        in_specs=[vmem] * (3 + len(pieces)),
        out_specs=pl.BlockSpec(memory_space=pl.ANY),
        scratch_shapes=[
            pltpu.VMEM((rows, virtuals), F32),
            pltpu.SemaphoreType.DMA((chunks,)),
        ],
        compiler_params=pltpu.CompilerParams(vmem_limit_bytes=VMEM_LIMIT),
        name="results",
    )(begun, dense, inverse, *pieces)


def local(
    grids, pairs, amplitudes, packed_factor, screen, metric, occ_energy, vir_energy, pair_occ
):
    me = lax.axis_index("grid")
    pair = lax.axis_index("pair")
    place = me.astype(jnp.int32).reshape(1)
    rows = amplitudes.shape[1]
    tile = packed_factor.shape[1] // screen.shape[1]

    part, sent = keep(packed_factor)[None], packed_factor[None]
    step = 2
    while step < pairs:
        other = exchange(sent, "pair", pairs, step)
        part = jnp.where(
            pair & step == 0,
            jnp.concatenate([part, other], 0),
            jnp.concatenate([other, part], 0),
        )
        sent = part
        step *= 2
    amplitudes, part = lax.optimization_barrier((amplitudes, part))
    packs = pack(place, screen, amplitudes[0], tile)
    part = jnp.stack([part] + [exchange(part, "grid", grids, k) for k in range(1, grids)], 0)
    packs, part = lax.optimization_barrier((packs, part))
    other = exchange(part, "pair", pairs, 1)
    packed = jnp.where(
        pair & 1 == 0, jnp.stack([part, other], 2), jnp.stack([other, part], 2)
    ).reshape(-1, packed_factor.shape[1])

    own_vir = lax.dynamic_slice_in_dim(vir_energy, me * rows, rows, 0)[:, None]
    halves = half_products(packed, packs)
    halves = [halves[0]] + [exchange(halves[k], "grid", grids, k) for k in range(1, grids)]
    dense, turned, scale, inverse = prepare(
        place, screen, pair_occ, occ_energy, packed, metric, own_vir, vir_energy[None, :], tile
    )
    mixed = mixed_sum(place, turned, halves[:-1])
    sent = ladders(turned, scale, mixed, halves[-1], grids)
    pieces = [sent[0]] + [exchange(sent[k], "grid", grids, k) for k in range(1, grids)]
    begun = result_start(dense, pieces[: grids // 2])
    return results(begun, dense, inverse, pieces[grids // 2 :])[None]


def solution(mesh):
    in_specs = (
        P("pair", "grid", None),
        P(("grid", "pair"), None),
        P(),
        P(None, "grid"),
        P(),
        P(),
        P("pair", None),
    )
    return jax.shard_map(
        functools.partial(local, mesh.shape["grid"], mesh.shape["pair"]),
        mesh=mesh,
        in_specs=in_specs,
        out_specs=P("pair", "grid", None),
        check_vma=False,
    )
```

time: 41.5 us -> 39.1 us (0.942)
  other arithmetic: 1.63 us -> 0.13 us
  waiting for transfers between devices: 13.8 us -> 12.3 us
  Pallas kernels: 6.43 us -> 7.18 us
    ppermute x12, waiting for transfers between devices: 13.8 us -> 12.3 us  [exchange(): return lax.ppermute(value, axis, [(i, i ^ step) for i in range(size)])]
    concatenate x1 -> x0, other arithmetic: 0.8 us -> none  [local(): jnp.concatenate([block, other], 0)]
    pallas_call x7, Pallas kernels: 5.37 us -> 6.12 us  [the longest x1 1.75 us: results(): pl.pallas_call(functools.partial(result_kernel, chunks), out_shape=jax.Sh...]
    select_n x4 -> x3, other arithmetic: 0.83 us -> 0.09 us  [the longest x1 0.08 us: local(): jnp.where(pair & 1 == 0, jnp.stack([part, other], 2), jnp.stack([other, p...]
  transfers between devices with their start and end apart: 12 -> 12, of which waited for: 10 -> 11; matrix products, arithmetic and copies ran while one was open for 2% -> 1% of each run, Pallas kernels for 8% -> 10%
where the time goes in v3:
time: 39.1 us; the launch traced here: 38.8 us
  starting transfers between devices  16.9 us (43%)
  waiting for transfers between devices  12.3 us (31%)
  Pallas kernels  7.18 us (18%)
  local copies, waits for them, and re-layouts  2.2 us (6%)
    ppermute x12, starting transfers between devices, exchange(): return lax.ppermute(value, axis, [(i, i ^ step) for i in range(size)])  16.9 us
    ppermute x12, waiting for transfers between devices, exchange(): return lax.ppermute(value, axis, [(i, i ^ step) for i in range(size)])  12.3 us
    unnamed x14, local copies, waits for them, and re-layouts  1.97 us
    pallas_call x1, Pallas kernels, results(): pl.pallas_call(functools.partial(result_kernel, chunks), out_shape=jax.Sh...  1.75 us
    pallas_call x1, Pallas kernels, prepare(): pl.pallas_call(functools.partial(prepare_kernel, tile, slots, count), out...  1.39 us
    pallas_call x1, Pallas kernels, pack(): pl.pallas_call(functools.partial(pack_kernel, tile, slots, count), out_sh...  1.06 us
    pallas_call x1, Pallas kernels, ladders(): pl.pallas_call(functools.partial(ladder_kernel, count), out_shape=[jax.Sh...  0.79 us
  transfers between devices with their start and end apart: 12, of which 11 were waited for; matrix products, arithmetic and copies ran while one was open for 1% of the time, Pallas kernels for 10%

profile of v3, /device:TPU:0, one launch (start us, length us, event | category | flops | bytes accessed | tf_op | source)
XLA Modules:
  0.0 38.8 jit_solution(12080978837529111850)
XLA Ops:
  0.0 3.0 %collective-permute-start = (bf16[1,16,512]{2,1,0:T(8,128)(2,1)}, bf16[1,16,512]{2,1,0:T(8,128)(2,1)S(1)}, u32[]{:S(2)}, u32[]{:S(2)}) collective-permute-start(bf16[1,16,512]{2,1,0:T(8,128)(2,1)} %bitcast.22), channel_id=1, source_target_pairs={{0,2},{1,3},{2,0},{3,1},{4,6},{5,7},{6,4},{7,5},{8,10},{9,11},{10,... | collective-permute-start | bytes 49160 | tf_op jit(solution)/shard_map/ppermute | solution.py:16
  3.0 0.8 %keep.1 = bf16[16,512]{1,0:T(8,128)(2,1)S(1)} custom-call(bf16[16,512]{1,0:T(8,128)(2,1)} %value.1), custom_call_target="tpu_custom_call" | custom-call | tf_op jit(solution)/shard_map/keep/pallas_call | solution.py:25
  3.8 1.2 %collective-permute-done = bf16[1,16,512]{2,1,0:T(8,128)(2,1)S(1)} collective-permute-done((bf16[1,16,512]{2,1,0:T(8,128)(2,1)}, bf16[1,16,512]{2,1,0:T(8,128)(2,1)S(1)}, u32[]{:S(2)}, u32[]{:S(2)}) %collective-permute-start) | collective-permute-done | bytes 16416 | tf_op jit(solution)/shard_map/ppermute | solution.py:16
  5.0 3.1 %collective-permute-start.1 = (bf16[2,16,512]{2,1,0:T(8,128)(2,1)S(1)}, bf16[2,16,512]{2,1,0:T(8,128)(2,1)S(1)}, u32[]{:S(2)}, u32[]{:S(2)}) collective-permute-start(bf16[2,16,512]{2,1,0:T(8,128)(2,1)S(1)} %maximum_select_fusion.2), channel_id=1, source_target_pairs={{0,4},{1,5},{2,6},{3,7},{4,0},{5,1},{6,2},{7,3},{8,12},{9,13},{10,... | collective-permute-start | bytes 98312 | tf_op jit(solution)/shard_map/ppermute | solution.py:16
  8.1 1.9 %collective-permute-done.1 = bf16[2,16,512]{2,1,0:T(8,128)(2,1)S(1)} collective-permute-done((bf16[2,16,512]{2,1,0:T(8,128)(2,1)S(1)}, bf16[2,16,512]{2,1,0:T(8,128)(2,1)S(1)}, u32[]{:S(2)}, u32[]{:S(2)}) %collective-permute-start.1) | collective-permute-done | bytes 32800 | tf_op jit(solution)/shard_map/ppermute | solution.py:16
  10.0 2.8 %collective-permute-start.4 = (bf16[4,16,512]{2,1,0:T(8,128)(2,1)S(1)}, bf16[4,16,512]{2,1,0:T(8,128)(2,1)S(1)}, u32[]{:S(2)}, u32[]{:S(2)}) collective-permute-start(bf16[4,16,512]{2,1,0:T(8,128)(2,1)S(1)} %maximum_select_fusion.1), channel_id=1, source_target_pairs={{0,24},{8,16},{16,8},{24,0},{1,25},{9,17},{17,9},{25,1},{2,26},{10... | collective-permute-start | bytes 196616 | tf_op jit(solution)/shard_map/ppermute | solution.py:16
  12.8 0.5 %collective-permute-start.3 = (bf16[4,16,512]{2,1,0:T(8,128)(2,1)S(1)}, bf16[4,16,512]{2,1,0:T(8,128)(2,1)S(1)}, u32[]{:S(2)}, u32[]{:S(2)}) collective-permute-start(bf16[4,16,512]{2,1,0:T(8,128)(2,1)S(1)} %maximum_select_fusion.1), channel_id=1, source_target_pairs={{0,16},{8,24},{16,0},{24,8},{1,17},{9,25},{17,1},{25,9},{2,18},{10... | collective-permute-start | bytes 196616 | tf_op jit(solution)/shard_map/ppermute | solution.py:16
  13.3 0.2 collective-permute-start.2
  13.5 1.3 %copy-done = bf16[1,384,1536]{2,1,0:T(8,128)(2,1)S(1)} copy-done((bf16[1,384,1536]{2,1,0:T(8,128)(2,1)S(1)}, bf16[1,384,1536]{2,1,0:T(8,128)(2,1)}, u32[]{:S(2)}) %copy-start) | copy-done | bytes 1179672
  14.8 0.7 %copy-done.2 = s32[4,4]{1,0:T(4,128)S(1)} copy-done((s32[4,4]{1,0:T(4,128)S(1)}, s32[4,4]{1,0:T(4,128)}, u32[]{:S(2)}) %copy-start.2) | copy-done | bytes 88
  15.5 1.1 %pack.1 = (bf16[384,512]{1,0:T(8,128)(2,1)S(1)}, bf16[384,512]{1,0:T(8,128)(2,1)S(1)}, bf16[384,512]{1,0:T(8,128)(2,1)S(1)}, bf16[384,512]{1,0:T(8,128)(2,1)S(1)}) custom-call(s32[1]{0:T(128)} %bitcast.place, s32[4,4]{1,0:T(4,128)S(1)} %copy-done.2, bf16[384,1536]{1,0:T(8,128)(2,1)S(1)} %bitcast.14), custom_call_target="tpu_custom_call" | custom-call | bytes 3145728 | tf_op jit(solution)/shard_map/pack/pallas_call | solution.py:59
  16.5 0.5 %collective-permute-done.3 = bf16[4,16,512]{2,1,0:T(8,128)(2,1)S(1)} collective-permute-done((bf16[4,16,512]{2,1,0:T(8,128)(2,1)S(1)}, bf16[4,16,512]{2,1,0:T(8,128)(2,1)S(1)}, u32[]{:S(2)}, u32[]{:S(2)}) %collective-permute-start.3) | collective-permute-done | bytes 65568 | tf_op jit(solution)/shard_map/ppermute | solution.py:16
  17.1 0.5 %collective-permute-done.2 = bf16[4,16,512]{2,1,0:T(8,128)(2,1)S(1)} collective-permute-done((bf16[4,16,512]{2,1,0:T(8,128)(2,1)S(1)}, bf16[4,16,512]{2,1,0:T(8,128)(2,1)S(1)}, u32[]{:S(2)}, u32[]{:S(2)}) %collective-permute-start.2) | collective-permute-done | bytes 65568 | tf_op jit(solution)/shard_map/ppermute | solution.py:16
  17.7 1.5 %collective-permute-done.5 = bf16[4,4,16,512]{3,2,1,0:T(8,128)(2,1)S(1)} collective-permute-done((bf16[4,4,16,512]{3,2,1,0:T(8,128)(2,1)S(1)}, bf16[4,4,16,512]{3,2,1,0:T(8,128)(2,1)S(1)}, u32[]{:S(2)}, u32[]{:S(2)}) %collective-permute-start.5) | collective-permute-done | bytes 262176 | tf_op jit(solution)/shard_map/ppermute | solution.py:16
  19.4 0.6 %half_products.1 = (bf16[384,128]{1,0:T(8,128)(2,1)S(1)}, bf16[384,128]{1,0:T(8,128)(2,1)S(1)}, bf16[384,128]{1,0:T(8,128)(2,1)S(1)}, bf16[384,128]{1,0:T(8,128)(2,1)S(1)}) custom-call(bf16[512,512]{1,0:T(8,128)(2,1)S(1)} %bitcast.12, bf16[384,512]{1,0:T(8,128)(2,1)S(1)} %get-tuple-element.38.rest_0_, bf16[384,512]{1,0:T(8,128)(2,1)S(1)} %get-tuple-element.39.rest_1_, ...), custom_call_target="tpu_custom_call" | custom-call | tf_op jit(solution)/shard_map/half_products/pallas_call | solution.py:90
  19.9 0.9 %collective-permute-start.6 = (bf16[384,128]{1,0:T(8,128)(2,1)S(1)}, bf16[384,128]{1,0:T(8,128)(2,1)S(1)}, u32[]{:S(2)}, u32[]{:S(2)}) collective-permute-start(bf16[384,128]{1,0:T(8,128)(2,1)S(1)} %get-tuple-element.43), channel_id=1, source_target_pairs={{0,8},{8,0},{16,24},{24,16},{1,9},{9,1},{17,25},{25,17},{2,10},{10... | collective-permute-start | bytes 294920 | tf_op jit(solution)/shard_map/ppermute | solution.py:16
  20.9 1.5 %collective-permute-start.7 = (bf16[384,128]{1,0:T(8,128)(2,1)S(1)}, bf16[384,128]{1,0:T(8,128)(2,1)S(1)}, u32[]{:S(2)}, u32[]{:S(2)}) collective-permute-start(bf16[384,128]{1,0:T(8,128)(2,1)S(1)} %get-tuple-element.44), channel_id=1, source_target_pairs={{0,16},{8,24},{16,0},{24,8},{1,17},{9,25},{17,1},{25,9},{2,18},{10... | collective-permute-start | bytes 294920 | tf_op jit(solution)/shard_map/ppermute | solution.py:16
  22.4 1.1 %collective-permute-start.8 = (bf16[384,128]{1,0:T(8,128)(2,1)S(1)}, bf16[384,128]{1,0:T(8,128)(2,1)S(1)}, u32[]{:S(2)}, u32[]{:S(2)}) collective-permute-start(bf16[384,128]{1,0:T(8,128)(2,1)S(1)} %get-tuple-element.45), channel_id=1, source_target_pairs={{0,24},{8,16},{16,8},{24,0},{1,25},{9,17},{17,9},{25,1},{2,26},{10... | collective-permute-start | bytes 294920 | tf_op jit(solution)/shard_map/ppermute | solution.py:16
  23.6 0.1 broadcast_in_dim.20.rest_2_
  23.8 1.4 %prepare.1 = (bf16[512,1536]{1,0:T(8,128)(2,1)S(1)}, bf16[1536,512]{1,0:T(8,128)(2,1)S(1)}, f32[128,512]{1,0:T(8,128)S(1)}, f32[384,1536]{1,0:T(8,128)S(1)}) custom-call(s32[1]{0:T(128)} %bitcast.place, s32[4,4]{1,0:T(4,128)S(1)} %copy-done.3, s32[1,2]{1,0:T(1,128)S(1)} %copy-done.5, f32[300]{0:T(512)S(1)} %copy-done.4, bf16[512,512]{1,0:T(8,128)(2,1)S(1)} %bitcast.13, ...), custom_call_target="tpu_custom_call" | custom-call | bytes 6291456 | tf_op jit(solution)/shard_map/prepare/pallas_call | solution.py:125
  25.2 1.4 %collective-permute-done.7.rest_2_ = bf16[384,128]{1,0:T(8,128)(2,1)S(1)} collective-permute-done((bf16[384,128]{1,0:T(8,128)(2,1)S(1)}, bf16[384,128]{1,0:T(8,128)(2,1)S(1)}, u32[]{:S(2)}, u32[]{:S(2)}) %collective-permute-start.7) | collective-permute-done | bytes 98336 | tf_op jit(solution)/shard_map/ppermute | solution.py:16
  26.6 0.4 %mixed.1 = f32[128,512]{1,0:T(8,128)S(1)} custom-call(s32[1]{0:T(128)} %bitcast.place, bf16[1536,512]{1,0:T(8,128)(2,1)S(1)} %get-tuple-element.36.turned, bf16[384,128]{1,0:T(8,128)(2,1)S(1)} %get-tuple-element.42.rest_0_, bf16[384,128]{1,0:T(8,128)(2,1)S(1)} %collective-permute-done.6.rest_1_, bf16[384,128]{1,0:T(8,128)(2,1)S(1)} %collective-permute-done.7.rest_2_), custom_call_target="tpu_custom_call" | custom-call | flops 150994944 | tf_op jit(solution)/shard_map/mixed/pallas_call | solution.py:162
  27.0 0.9 %collective-permute-done.8.half = bf16[384,128]{1,0:T(8,128)(2,1)S(1)} collective-permute-done((bf16[384,128]{1,0:T(8,128)(2,1)S(1)}, bf16[384,128]{1,0:T(8,128)(2,1)S(1)}, u32[]{:S(2)}, u32[]{:S(2)}) %collective-permute-start.8) | collective-permute-done | bytes 98336 | tf_op jit(solution)/shard_map/ppermute | solution.py:16
  27.9 0.8 %ladders.1 = (bf16[384,128]{1,0:T(8,128)(2,1)S(1)}, bf16[384,128]{1,0:T(8,128)(2,1)S(1)}, bf16[384,128]{1,0:T(8,128)(2,1)S(1)}, bf16[384,128]{1,0:T(8,128)(2,1)S(1)}) custom-call(bf16[1536,512]{1,0:T(8,128)(2,1)S(1)} %get-tuple-element.36.turned, f32[128,512]{1,0:T(8,128)S(1)} %get-tuple-element.37.scale, f32[128,512]{1,0:T(8,128)S(1)} %mixed.1, ...), custom_call_target="tpu_custom_call" | custom-call | tf_op jit(solution)/shard_map/ladders/pallas_call | solution.py:194
  28.7 1.2 %collective-permute-start.9 = (bf16[384,128]{1,0:T(8,128)(2,1)S(1)}, bf16[384,128]{1,0:T(8,128)(2,1)S(1)}, u32[]{:S(2)}, u32[]{:S(2)}) collective-permute-start(bf16[384,128]{1,0:T(8,128)(2,1)S(1)} %get-tuple-element.47), channel_id=1, source_target_pairs={{0,8},{8,0},{16,24},{24,16},{1,9},{9,1},{17,25},{25,17},{2,10},{10... | collective-permute-start | bytes 294920 | tf_op jit(solution)/shard_map/ppermute | solution.py:16
  29.9 1.6 %collective-permute-start.10 = (bf16[384,128]{1,0:T(8,128)(2,1)S(1)}, bf16[384,128]{1,0:T(8,128)(2,1)S(1)}, u32[]{:S(2)}, u32[]{:S(2)}) collective-permute-start(bf16[384,128]{1,0:T(8,128)(2,1)S(1)} %get-tuple-element.49), channel_id=1, source_target_pairs={{0,16},{8,24},{16,0},{24,8},{1,17},{9,25},{17,1},{25,9},{2,18},{10... | collective-permute-start | bytes 294920 | tf_op jit(solution)/shard_map/ppermute | solution.py:16
  31.5 0.7 %collective-permute-start.11 = (bf16[384,128]{1,0:T(8,128)(2,1)S(1)}, bf16[384,128]{1,0:T(8,128)(2,1)S(1)}, u32[]{:S(2)}, u32[]{:S(2)}) collective-permute-start(bf16[384,128]{1,0:T(8,128)(2,1)S(1)} %get-tuple-element.50), channel_id=1, source_target_pairs={{0,24},{8,16},{16,8},{24,0},{1,25},{9,17},{17,9},{25,1},{2,26},{10... | collective-permute-start | bytes 294920 | tf_op jit(solution)/shard_map/ppermute | solution.py:16
  32.3 1.7 %collective-permute-done.9.rest_1_ = bf16[384,128]{1,0:T(8,128)(2,1)S(1)} collective-permute-done((bf16[384,128]{1,0:T(8,128)(2,1)S(1)}, bf16[384,128]{1,0:T(8,128)(2,1)S(1)}, u32[]{:S(2)}, u32[]{:S(2)}) %collective-permute-start.9) | collective-permute-done | bytes 98336 | tf_op jit(solution)/shard_map/ppermute | solution.py:16
  34.0 0.5 %result_start.1.begun = f32[384,1536]{1,0:T(8,128)S(1)} custom-call(bf16[512,1536]{1,0:T(8,128)(2,1)S(1)} %get-tuple-element.35.dense, bf16[384,128]{1,0:T(8,128)(2,1)S(1)} %get-tuple-element.46.rest_0_, bf16[384,128]{1,0:T(8,128)(2,1)S(1)} %collective-permute-done.9.rest_1_), custom_call_target="tpu_custom_call" | custom-call | flops 301989888 | tf_op jit(solution)/shard_map/result_start/pallas_call | solution.py:213
  34.5 0.1 collective-permute-done.10.rest_0_
  34.5 2.5 %collective-permute-done.11.rest_1_ = bf16[384,128]{1,0:T(8,128)(2,1)S(1)} collective-permute-done((bf16[384,128]{1,0:T(8,128)(2,1)S(1)}, bf16[384,128]{1,0:T(8,128)(2,1)S(1)}, u32[]{:S(2)}, u32[]{:S(2)}) %collective-permute-start.11) | collective-permute-done | bytes 98336 | tf_op jit(solution)/shard_map/ppermute | solution.py:16
  37.1 1.8 %results.1 = f32[384,1536]{1,0:T(8,128)} custom-call(f32[384,1536]{1,0:T(8,128)S(1)} %result_start.1.begun, bf16[512,1536]{1,0:T(8,128)(2,1)S(1)} %get-tuple-element.35.dense, f32[384,1536]{1,0:T(8,128)S(1)} %get-tuple-element.48.inverse, bf16[384,128]{1,0:T(8,128)(2,1)S(1)} %collective-permute-done.10.rest_0_, ...), custom_call_target="tpu_custom_call" | custom-call | tf_op jit(solution)/shard_map/results/pallas_call | solution.py:248
  (22 shorter events, 0.4 us)
Async XLA Ops:
  0.0 5.0 %collective-permute-start = (bf16[1,16,512]{2,1,0:T(8,128)(2,1)}, bf16[1,16,512]{2,1,0:T(8,128)(2,1)S(1)}, u32[]{:S(2)}, u32[]{:S(2)}) collective-permute-start(bf16[1,16,512]{2,1,0:T(8,128)(2,1)} %bitcast.22), channel_id=1, source_target_pairs={{0,2},{1,3},{2,0},{3,1},{4,6},{5,7},{6,4},{7,5},{8,10},{9,11},{10,... | collective-permute-start | bytes 49160 | tf_op jit(solution)/shard_map/ppermute | solution.py:16
  5.0 5.0 %collective-permute-start.1 = (bf16[2,16,512]{2,1,0:T(8,128)(2,1)S(1)}, bf16[2,16,512]{2,1,0:T(8,128)(2,1)S(1)}, u32[]{:S(2)}, u32[]{:S(2)}) collective-permute-start(bf16[2,16,512]{2,1,0:T(8,128)(2,1)S(1)} %maximum_select_fusion.2), channel_id=1, source_target_pairs={{0,4},{1,5},{2,6},{3,7},{4,0},{5,1},{6,2},{7,3},{8,12},{9,13},{10,... | collective-permute-start | bytes 98312 | tf_op jit(solution)/shard_map/ppermute | solution.py:16
  10.0 6.6 %collective-permute-start.4 = (bf16[4,16,512]{2,1,0:T(8,128)(2,1)S(1)}, bf16[4,16,512]{2,1,0:T(8,128)(2,1)S(1)}, u32[]{:S(2)}, u32[]{:S(2)}) collective-permute-start(bf16[4,16,512]{2,1,0:T(8,128)(2,1)S(1)} %maximum_select_fusion.1), channel_id=1, source_target_pairs={{0,24},{8,16},{16,8},{24,0},{1,25},{9,17},{17,9},{25,1},{2,26},{10... | collective-permute-start | bytes 196616 | tf_op jit(solution)/shard_map/ppermute | solution.py:16
  12.8 4.3 %collective-permute-start.3 = (bf16[4,16,512]{2,1,0:T(8,128)(2,1)S(1)}, bf16[4,16,512]{2,1,0:T(8,128)(2,1)S(1)}, u32[]{:S(2)}, u32[]{:S(2)}) collective-permute-start(bf16[4,16,512]{2,1,0:T(8,128)(2,1)S(1)} %maximum_select_fusion.1), channel_id=1, source_target_pairs={{0,16},{8,24},{16,0},{24,8},{1,17},{9,25},{17,1},{25,9},{2,18},{10... | collective-permute-start | bytes 196616 | tf_op jit(solution)/shard_map/ppermute | solution.py:16
  13.3 4.3 %collective-permute-start.2 = (bf16[4,16,512]{2,1,0:T(8,128)(2,1)S(1)}, bf16[4,16,512]{2,1,0:T(8,128)(2,1)S(1)}, u32[]{:S(2)}, u32[]{:S(2)}) collective-permute-start(bf16[4,16,512]{2,1,0:T(8,128)(2,1)S(1)} %maximum_select_fusion.1), channel_id=1, source_target_pairs={{0,8},{8,0},{16,24},{24,16},{1,9},{9,1},{17,25},{25,17},{2,10},{10... | collective-permute-start | bytes 196616 | tf_op jit(solution)/shard_map/ppermute | solution.py:16
  13.5 1.3 %copy-start = (bf16[1,384,1536]{2,1,0:T(8,128)(2,1)S(1)}, bf16[1,384,1536]{2,1,0:T(8,128)(2,1)}, u32[]{:S(2)}) copy-start(bf16[1,384,1536]{2,1,0:T(8,128)(2,1)} %param.7) | copy-start | bytes 3538948
  14.8 0.7 %copy-start.2 = (s32[4,4]{1,0:T(4,128)S(1)}, s32[4,4]{1,0:T(4,128)}, u32[]{:S(2)}) copy-start(s32[4,4]{1,0:T(4,128)} %screen.3) | copy-start | bytes 196
  17.6 5.9 %copy-start.6 = (f32[1536]{0:T(1024)S(1)}, f32[1536]{0:T(1024)}, u32[]{:S(2)}) copy-start(f32[1536]{0:T(1024)} %param.12) | copy-start | bytes 18436
  17.6 6.1 %copy-start.1 = (bf16[512,128]{1,0:T(8,128)(2,1)S(1)}, bf16[512,128]{1,0:T(8,128)(2,1)}, u32[]{:S(2)}) copy-start(bf16[512,128]{1,0:T(8,128)(2,1)} %rest_1_.1) | copy-start | bytes 393220
  17.6 6.1 %copy-start.3 = (s32[4,4]{1,0:T(4,128)S(1)}, s32[4,4]{1,0:T(4,128)}, u32[]{:S(2)}) copy-start(s32[4,4]{1,0:T(4,128)} %screen.3) | copy-start | bytes 196
  17.6 6.1 %copy-start.4 = (f32[300]{0:T(512)S(1)}, f32[300]{0:T(512)}, u32[]{:S(2)}) copy-start(f32[300]{0:T(512)} %occ_energy.1) | copy-start | bytes 3604
  17.6 6.2 %copy-start.5 = (s32[1,2]{1,0:T(1,128)S(1)}, s32[1,2]{1,0:T(1,128)}, u32[]{:S(2)}) copy-start(s32[1,2]{1,0:T(1,128)} %pair_occ.1) | copy-start | bytes 28
  17.6 1.6 %collective-permute-start.5 = (bf16[4,4,16,512]{3,2,1,0:T(8,128)(2,1)S(1)}, bf16[4,4,16,512]{3,2,1,0:T(8,128)(2,1)S(1)}, u32[]{:S(2)}, u32[]{:S(2)}) collective-permute-start(bf16[4,4,16,512]{3,2,1,0:T(8,128)(2,1)S(1)} %pad_maximum_fusion), channel_id=1, source_target_pairs={{0,1},{1,0},{2,3},{3,2},{4,5},{5,4},{6,7},{7,6},{8,9},{9,8},{10,11... | collective-permute-start | bytes 786440 | tf_op jit(solution)/shard_map/ppermute | solution.py:16
  19.9 5.3 %collective-permute-start.6 = (bf16[384,128]{1,0:T(8,128)(2,1)S(1)}, bf16[384,128]{1,0:T(8,128)(2,1)S(1)}, u32[]{:S(2)}, u32[]{:S(2)}) collective-permute-start(bf16[384,128]{1,0:T(8,128)(2,1)S(1)} %get-tuple-element.43), channel_id=1, source_target_pairs={{0,8},{8,0},{16,24},{24,16},{1,9},{9,1},{17,25},{25,17},{2,10},{10... | collective-permute-start | bytes 294920 | tf_op jit(solution)/shard_map/ppermute | solution.py:16
  20.9 5.8 %collective-permute-start.7 = (bf16[384,128]{1,0:T(8,128)(2,1)S(1)}, bf16[384,128]{1,0:T(8,128)(2,1)S(1)}, u32[]{:S(2)}, u32[]{:S(2)}) collective-permute-start(bf16[384,128]{1,0:T(8,128)(2,1)S(1)} %get-tuple-element.44), channel_id=1, source_target_pairs={{0,16},{8,24},{16,0},{24,8},{1,17},{9,25},{17,1},{25,9},{2,18},{10... | collective-permute-start | bytes 294920 | tf_op jit(solution)/shard_map/ppermute | solution.py:16
  22.4 5.5 %collective-permute-start.8 = (bf16[384,128]{1,0:T(8,128)(2,1)S(1)}, bf16[384,128]{1,0:T(8,128)(2,1)S(1)}, u32[]{:S(2)}, u32[]{:S(2)}) collective-permute-start(bf16[384,128]{1,0:T(8,128)(2,1)S(1)} %get-tuple-element.45), channel_id=1, source_target_pairs={{0,24},{8,16},{16,8},{24,0},{1,25},{9,17},{17,9},{25,1},{2,26},{10... | collective-permute-start | bytes 294920 | tf_op jit(solution)/shard_map/ppermute | solution.py:16
  28.7 5.3 %collective-permute-start.9 = (bf16[384,128]{1,0:T(8,128)(2,1)S(1)}, bf16[384,128]{1,0:T(8,128)(2,1)S(1)}, u32[]{:S(2)}, u32[]{:S(2)}) collective-permute-start(bf16[384,128]{1,0:T(8,128)(2,1)S(1)} %get-tuple-element.47), channel_id=1, source_target_pairs={{0,8},{8,0},{16,24},{24,16},{1,9},{9,1},{17,25},{25,17},{2,10},{10... | collective-permute-start | bytes 294920 | tf_op jit(solution)/shard_map/ppermute | solution.py:16
  29.9 4.6 %collective-permute-start.10 = (bf16[384,128]{1,0:T(8,128)(2,1)S(1)}, bf16[384,128]{1,0:T(8,128)(2,1)S(1)}, u32[]{:S(2)}, u32[]{:S(2)}) collective-permute-start(bf16[384,128]{1,0:T(8,128)(2,1)S(1)} %get-tuple-element.49), channel_id=1, source_target_pairs={{0,16},{8,24},{16,0},{24,8},{1,17},{9,25},{17,1},{25,9},{2,18},{10... | collective-permute-start | bytes 294920 | tf_op jit(solution)/shard_map/ppermute | solution.py:16
  31.5 5.5 %collective-permute-start.11 = (bf16[384,128]{1,0:T(8,128)(2,1)S(1)}, bf16[384,128]{1,0:T(8,128)(2,1)S(1)}, u32[]{:S(2)}, u32[]{:S(2)}) collective-permute-start(bf16[384,128]{1,0:T(8,128)(2,1)S(1)} %get-tuple-element.50), channel_id=1, source_target_pairs={{0,24},{8,16},{16,8},{24,0},{1,25},{9,17},{17,9},{25,1},{2,26},{10... | collective-permute-start | bytes 294920 | tf_op jit(solution)/shard_map/ppermute | solution.py:16

commit v4 on v3

--- a/solution.py
+++ b/solution.py
@@ -70,42 +70,44 @@
     )(place, screen, amplitudes)
 
 
-def half_kernel(count, packed, *rest):
-    listed, outs = rest[:count], rest[count:]
-    width = packed.shape[0] // count
+def half_kernel(count, *refs):
     for k in range(count):
-        outs[k][...] = lax.dot_general(
-            listed[k][...],
-            packed[k * width : (k + 1) * width, :],
+        refs[2 * count + k][...] = lax.dot_general(
+            refs[k][...],
+            refs[count + k][...],
             (((1,), (1,)), ((), ())),
             preferred_element_type=F32,
         ).astype(BF16)
 
 
-def half_products(packed, listed):
+def half_products(listed, blocks):
     count = len(listed)
     rows, columns = listed[0].shape
-    width = packed.shape[0] // count
+    width = blocks[0].shape[0]
     vmem = pl.BlockSpec(memory_space=pltpu.VMEM)
     return pl.pallas_call(
         functools.partial(half_kernel, count),
         out_shape=[jax.ShapeDtypeStruct((rows, width), BF16)] * count,
-        in_specs=[vmem] * (1 + count),
+        in_specs=[vmem] * (2 * count),
         out_specs=[vmem] * count,
+        cost_estimate=pl.CostEstimate(
+            flops=2 * count * rows * columns * width, bytes_accessed=0, transcendentals=0
+        ),
         compiler_params=pltpu.CompilerParams(vmem_limit_bytes=VMEM_LIMIT),
         name="half_products",
-    )(packed, *listed)
+    )(*listed, *blocks)
 
 
 def prepare_kernel(tile, slots, count, place, screen, pair_occ, occ_energy, *rest):
-    packed, metric, own_vir, vir, dense, turned, scale, inverse = rest
-    width = packed.shape[0] // count
+    blocks = rest[:count]
+    metric, own_vir, vir, dense, turned, scale, inverse = rest[count:]
+    width = blocks[0].shape[0]
     dense[...] = jnp.zeros_like(dense)
     turned[...] = jnp.zeros_like(turned)
     for k in range(count):
         b = place[0] ^ k
         span = slice(k * width, (k + 1) * width)
-        block = packed[span, :]
+        block = blocks[k][...]
         other = block.T
         for s in range(slots):
             start = pl.multiple_of(screen[b, s] * tile, tile)
@@ -116,9 +118,9 @@
     inverse[...] = 1.0 / ((own_vir[...] + vir[...]) - occ_total)
 
 
-def prepare(place, screen, pair_occ, occ_energy, packed, metric, own_vir, vir, tile):
+def prepare(place, screen, pair_occ, occ_energy, blocks, metric, own_vir, vir, tile):
     count, slots = screen.shape
-    points = packed.shape[0]
+    points = count * blocks[0].shape[0]
     rows, virtuals = own_vir.shape[0], vir.shape[1]
     smem = pl.BlockSpec(memory_space=pltpu.SMEM)
     vmem = pl.BlockSpec(memory_space=pltpu.VMEM)
@@ -130,37 +132,37 @@
             jax.ShapeDtypeStruct((metric.shape[1], points), F32),
             jax.ShapeDtypeStruct((rows, virtuals), F32),
         ],
-        in_specs=[smem] * 4 + [vmem] * 4,
+        in_specs=[smem] * 4 + [vmem] * (3 + count),
         out_specs=[vmem] * 4,
         cost_estimate=pl.CostEstimate(
             flops=0, bytes_accessed=8 * points * virtuals, transcendentals=0
         ),
         compiler_params=pltpu.CompilerParams(vmem_limit_bytes=VMEM_LIMIT),
         name="prepare",
-    )(place, screen, pair_occ, occ_energy, packed, metric, own_vir, vir)
+    )(place, screen, pair_occ, occ_energy, *blocks, metric, own_vir, vir)
 
 
 def mixed_part(half, factor):
     return lax.dot_general(half, factor, (((0,), (0,)), ((), ())), preferred_element_type=F32)
 
 
-def mixed_kernel(known, place, turned, *rest):
-    halves, out = rest[:known], rest[known]
+def mixed_kernel(order, place, turned, *rest):
+    halves, out = rest[:-1], rest[-1]
     rows = halves[0].shape[0]
     total = None
-    for k in range(known):
+    for k, half in zip(order, halves):
         start = pl.multiple_of((place[0] ^ k) * rows, rows)
-        part = mixed_part(halves[k][...], turned[pl.ds(start, rows), :])
+        part = mixed_part(half[...], turned[pl.ds(start, rows), :])
         total = part if total is None else total + part
     out[...] = total
 
 
-def mixed_sum(place, turned, halves):
+def mixed_sum(order, place, turned, halves):
     known = len(halves)
     width, points = halves[0].shape[1], turned.shape[1]
     vmem = pl.BlockSpec(memory_space=pltpu.VMEM)
     return pl.pallas_call(
-        functools.partial(mixed_kernel, known),
+        functools.partial(mixed_kernel, order),
         out_shape=jax.ShapeDtypeStruct((width, points), F32),
         in_specs=[pl.BlockSpec(memory_space=pltpu.SMEM)] + [vmem] * (1 + known),
         out_specs=vmem,
@@ -172,46 +174,56 @@
     )(place, turned, *halves)
 
 
-def ladder_kernel(count, turned, scale, mixed, half, *outs):
+def ladder_kernel(order, late, turned, scale, mixed, *rest):
+    halves, outs = rest[: len(late)], rest[len(late) :]
     me = lax.axis_index("grid")
-    rows = half.shape[0]
-    start = pl.multiple_of((me ^ (count - 1)) * rows, rows)
-    total = mixed[...] + mixed_part(half[...], turned[pl.ds(start, rows), :])
+    rows = halves[0].shape[0]
+
+    def own_rows(k):
+        return turned[pl.ds(pl.multiple_of((me ^ k) * rows, rows), rows), :]
+
+    total = mixed[...]
+    for k, half in zip(late, halves):
+        total = total + mixed_part(half[...], own_rows(k))
     weighted = (scale[...] * total).astype(BF16)
-    for k in list(range(1, count)) + [0]:
-        start = pl.multiple_of((me ^ k) * rows, rows)
+    for k in order:
         outs[k][...] = lax.dot_general(
-            turned[pl.ds(start, rows), :],
-            weighted,
-            (((1,), (1,)), ((), ())),
-            preferred_element_type=F32,
+            own_rows(k), weighted, (((1,), (1,)), ((), ())), preferred_element_type=F32
         ).astype(BF16)
 
 
-def ladders(turned, scale, mixed, half, count):
-    rows, width = half.shape
-    vmem = pl.BlockSpec(memory_space=pltpu.VMEM)
-    return pl.pallas_call(
-        functools.partial(ladder_kernel, count),
-        out_shape=[jax.ShapeDtypeStruct((rows, width), BF16)] * count,
-        in_specs=[vmem] * 4,
-        out_specs=[vmem] * count,
+def ladders(order, late, turned, scale, mixed, halves):
+    rows, width = halves[0].shape
+    vmem = pl.BlockSpec(memory_space=pltpu.VMEM)
+    return pl.pallas_call(
+        functools.partial(ladder_kernel, order, late),
+        out_shape=[jax.ShapeDtypeStruct((rows, width), BF16)] * len(order),
+        in_specs=[vmem] * (3 + len(halves)),
+        out_specs=[vmem] * len(order),
         compiler_params=pltpu.CompilerParams(vmem_limit_bytes=VMEM_LIMIT),
         name="ladders",
-    )(turned, scale, mixed, half)
-
-
-def start_kernel(dense, *rest):
+    )(turned, scale, mixed, *halves)
+
+
+def joined(order, width, pieces, dense, span):
+    total = None
+    for k, piece in zip(order, pieces):
+        block = dense[k * width : (k + 1) * width, span]
+        part = jnp.dot(piece[...], block, preferred_element_type=F32)
+        total = part if total is None else total + part
+    return total
+
+
+def start_kernel(order, dense, *rest):
     pieces, out = rest[:-1], rest[-1]
-    joined = jnp.concatenate([piece[...] for piece in pieces], axis=1)
-    out[...] = jnp.dot(joined, dense[: joined.shape[1], :], preferred_element_type=F32)
-
-
-def result_start(dense, pieces):
+    out[...] = joined(order, pieces[0].shape[1], pieces, dense, slice(None))
+
+
+def result_start(order, dense, pieces):
     rows, width = pieces[0].shape
     vmem = pl.BlockSpec(memory_space=pltpu.VMEM)
     return pl.pallas_call(
-        start_kernel,
+        functools.partial(start_kernel, order),
         out_shape=jax.ShapeDtypeStruct((rows, dense.shape[1]), F32),
         in_specs=[vmem] * (1 + len(pieces)),
         out_specs=vmem,
@@ -225,15 +237,14 @@
     )(dense, *pieces)
 
 
-def result_kernel(chunks, begun, dense, inverse, *rest):
+def result_kernel(order, chunks, begun, dense, inverse, *rest):
     *pieces, out, staged, sems = rest
-    joined = jnp.concatenate([piece[...] for piece in pieces], axis=1)
-    first = dense.shape[0] - joined.shape[1]
+    width = pieces[0].shape[1]
     part = out.shape[1] // chunks
     copies = []
     for j in range(chunks):
         span = slice(j * part, (j + 1) * part)
-        value = jnp.dot(joined, dense[first:, span], preferred_element_type=F32)
+        value = joined(order, width, pieces, dense, span)
         staged[:, span] = (begun[:, span] + value) * inverse[:, span]
         copies.append(pltpu.make_async_copy(staged.at[:, span], out.at[:, span], sems.at[j]))
         copies[-1].start()
@@ -241,12 +252,12 @@
         copy.wait()
 
 
-def results(begun, dense, inverse, pieces):
+def results(order, begun, dense, inverse, pieces):
     rows, virtuals = begun.shape
     chunks = 6 if virtuals % 768 == 0 else 1
     vmem = pl.BlockSpec(memory_space=pltpu.VMEM)
     return pl.pallas_call(
-        functools.partial(result_kernel, chunks),
+        functools.partial(result_kernel, order, chunks),
         out_shape=jax.ShapeDtypeStruct((rows, virtuals), F32),
         in_specs=[vmem] * (3 + len(pieces)),
         out_specs=pl.BlockSpec(memory_space=pl.ANY),
@@ -265,6 +276,7 @@
     me = lax.axis_index("grid")
     pair = lax.axis_index("pair")
     place = me.astype(jnp.int32).reshape(1)
+    order = [0] + list(range(grids - 1, 0, -1))
     rows = amplitudes.shape[1]
     tile = packed_factor.shape[1] // screen.shape[1]
 
@@ -279,26 +291,34 @@
         )
         sent = part
         step *= 2
-    amplitudes, part = lax.optimization_barrier((amplitudes, part))
+        amplitudes, part = lax.optimization_barrier((amplitudes, part))
+    parts = [exchange(part, "grid", grids, k) if k else part for k in range(grids)]
     packs = pack(place, screen, amplitudes[0], tile)
-    part = jnp.stack([part] + [exchange(part, "grid", grids, k) for k in range(1, grids)], 0)
-    packs, part = lax.optimization_barrier((packs, part))
-    other = exchange(part, "pair", pairs, 1)
-    packed = jnp.where(
-        pair & 1 == 0, jnp.stack([part, other], 2), jnp.stack([other, part], 2)
-    ).reshape(-1, packed_factor.shape[1])
-
+    packs = list(packs)
+    blocks = []
+    for k, part in enumerate(parts):
+        part, packs[k] = lax.optimization_barrier((part, packs[k]))
+        other = exchange(part, "pair", pairs, 1)
+        both = jnp.where(
+            pair & 1 == 0, jnp.stack([part, other], 1), jnp.stack([other, part], 1)
+        )
+        blocks.append(both.reshape(-1, packed_factor.shape[1]))
+
+    halves = []
+    for ks in ([0], order[1:2], order[2:]):
+        group = half_products([packs[k] for k in ks], [blocks[k] for k in ks])
+        halves += [exchange(half, "grid", grids, k) if k else half for k, half in zip(ks, group)]
+    vir_energy, halves[0] = lax.optimization_barrier((vir_energy, halves[0]))
     own_vir = lax.dynamic_slice_in_dim(vir_energy, me * rows, rows, 0)[:, None]
-    halves = half_products(packed, packs)
-    halves = [halves[0]] + [exchange(halves[k], "grid", grids, k) for k in range(1, grids)]
     dense, turned, scale, inverse = prepare(
-        place, screen, pair_occ, occ_energy, packed, metric, own_vir, vir_energy[None, :], tile
+        place, screen, pair_occ, occ_energy, blocks, metric, own_vir, vir_energy[None, :], tile
     )
-    mixed = mixed_sum(place, turned, halves[:-1])
-    sent = ladders(turned, scale, mixed, halves[-1], grids)
-    pieces = [sent[0]] + [exchange(sent[k], "grid", grids, k) for k in range(1, grids)]
-    begun = result_start(dense, pieces[: grids // 2])
-    return results(begun, dense, inverse, pieces[grids // 2 :])[None]
+    early = grids // 2
+    mixed = mixed_sum(order[:early], place, turned, halves[:early])
+    sent = ladders(order, order[early:], turned, scale, mixed, halves[early:])
+    pieces = [exchange(sent[k], "grid", grids, k) if k else sent[k] for k in order]
+    begun = result_start(order[:early], dense, pieces[:early])
+    return results(order[early:], begun, dense, inverse, pieces[early:])[None]
 
 
 def solution(mesh):

time: 39.1 us -> 38.2 us (0.977)
  waiting for transfers between devices: 12.3 us -> 9.75 us
  starting transfers between devices: 16.9 us -> 17.9 us
  Pallas kernels: 7.18 us -> 7.86 us
    ppermute x12 -> x15, waiting for transfers between devices: 12.3 us -> 9.75 us  [exchange(): return lax.ppermute(value, axis, [(i, i ^ step) for i in range(size)])]
    ppermute x12 -> x15, starting transfers between devices: 16.9 us -> 17.9 us  [exchange(): return lax.ppermute(value, axis, [(i, i ^ step) for i in range(size)])]
    pallas_call x1 -> x3, Pallas kernels: 0.57 us -> 0.88 us  [half_products(): pl.pallas_call(functools.partial(half_kernel, count), out_shape=[jax.Shap...]
  transfers between devices with their start and end apart: 12 -> 15, of which waited for: 11 -> 12; matrix products, arithmetic and copies ran while one was open for 1% -> 1% of each run, Pallas kernels for 10% -> 13%
where the time goes in v4:
time: 38.2 us; the launch traced here: 38 us
  starting transfers between devices  17.9 us (47%)
  waiting for transfers between devices  9.75 us (26%)
  Pallas kernels  7.86 us (21%)
  local copies, waits for them, and re-layouts  2.22 us (6%)
    ppermute x15, starting transfers between devices, exchange(): return lax.ppermute(value, axis, [(i, i ^ step) for i in range(size)])  17.9 us
    ppermute x15, waiting for transfers between devices, exchange(): return lax.ppermute(value, axis, [(i, i ^ step) for i in range(size)])  9.75 us
    unnamed x14, local copies, waits for them, and re-layouts  1.98 us
    pallas_call x1, Pallas kernels, results(): pl.pallas_call(functools.partial(result_kernel, order, chunks), out_shape...  1.86 us
    pallas_call x1, Pallas kernels, prepare(): pl.pallas_call(functools.partial(prepare_kernel, tile, slots, count), out...  1.39 us
    pallas_call x1, Pallas kernels, pack(): pl.pallas_call(functools.partial(pack_kernel, tile, slots, count), out_sh...  1.06 us
    pallas_call x3, Pallas kernels, half_products(): pl.pallas_call(functools.partial(half_kernel, count), out_shape=[jax.Shap...  0.88 us
    pallas_call x1, Pallas kernels, ladders(): pl.pallas_call(functools.partial(ladder_kernel, order, late), out_shape=[...  0.86 us
  transfers between devices with their start and end apart: 15, of which 12 were waited for; matrix products, arithmetic and copies ran while one was open for 1% of the time, Pallas kernels for 13%

profile of v4, /device:TPU:0, one launch (start us, length us, event | category | flops | bytes accessed | tf_op | source)
XLA Modules:
  0.0 38.0 jit_solution(14347525612276900935)
XLA Ops:
  0.0 3.0 %collective-permute-start = (bf16[1,16,512]{2,1,0:T(8,128)(2,1)}, bf16[1,16,512]{2,1,0:T(8,128)(2,1)S(1)}, u32[]{:S(2)}, u32[]{:S(2)}) collective-permute-start(bf16[1,16,512]{2,1,0:T(8,128)(2,1)} %bitcast.35), channel_id=1, source_target_pairs={{0,2},{1,3},{2,0},{3,1},{4,6},{5,7},{6,4},{7,5},{8,10},{9,11},{10,... | collective-permute-start | bytes 49160 | tf_op jit(solution)/shard_map/ppermute | solution.py:16
  3.0 0.8 %keep.1 = bf16[16,512]{1,0:T(8,128)(2,1)S(1)} custom-call(bf16[16,512]{1,0:T(8,128)(2,1)} %value.1), custom_call_target="tpu_custom_call" | custom-call | tf_op jit(solution)/shard_map/keep/pallas_call | solution.py:25
  3.8 1.2 %collective-permute-done = bf16[1,16,512]{2,1,0:T(8,128)(2,1)S(1)} collective-permute-done((bf16[1,16,512]{2,1,0:T(8,128)(2,1)}, bf16[1,16,512]{2,1,0:T(8,128)(2,1)S(1)}, u32[]{:S(2)}, u32[]{:S(2)}) %collective-permute-start) | collective-permute-done | bytes 16416 | tf_op jit(solution)/shard_map/ppermute | solution.py:16
  5.0 3.1 %collective-permute-start.1 = (bf16[2,16,512]{2,1,0:T(8,128)(2,1)S(1)}, bf16[2,16,512]{2,1,0:T(8,128)(2,1)S(1)}, u32[]{:S(2)}, u32[]{:S(2)}) collective-permute-start(bf16[2,16,512]{2,1,0:T(8,128)(2,1)S(1)} %maximum_select_fusion.5), channel_id=1, source_target_pairs={{0,4},{1,5},{2,6},{3,7},{4,0},{5,1},{6,2},{7,3},{8,12},{9,13},{10,... | collective-permute-start | bytes 98312 | tf_op jit(solution)/shard_map/ppermute | solution.py:16
  8.1 1.9 %collective-permute-done.1 = bf16[2,16,512]{2,1,0:T(8,128)(2,1)S(1)} collective-permute-done((bf16[2,16,512]{2,1,0:T(8,128)(2,1)S(1)}, bf16[2,16,512]{2,1,0:T(8,128)(2,1)S(1)}, u32[]{:S(2)}, u32[]{:S(2)}) %collective-permute-start.1) | collective-permute-done | bytes 32800 | tf_op jit(solution)/shard_map/ppermute | solution.py:16
  10.0 1.9 %collective-permute-start.5 = (bf16[4,16,512]{2,1,0:T(8,128)(2,1)S(1)}, bf16[4,16,512]{2,1,0:T(8,128)(2,1)S(1)}, u32[]{:S(2)}, u32[]{:S(2)}) collective-permute-start(bf16[4,16,512]{2,1,0:T(8,128)(2,1)S(1)} %maximum_select_fusion.4), channel_id=1, source_target_pairs={{0,16},{8,24},{16,0},{24,8},{1,17},{9,25},{17,1},{25,9},{2,18},{10... | collective-permute-start | bytes 196616 | tf_op jit(solution)/shard_map/ppermute | solution.py:16
  11.9 1.4 %collective-permute-start.7 = (bf16[4,16,512]{2,1,0:T(8,128)(2,1)S(1)}, bf16[4,16,512]{2,1,0:T(8,128)(2,1)S(1)}, u32[]{:S(2)}, u32[]{:S(2)}) collective-permute-start(bf16[4,16,512]{2,1,0:T(8,128)(2,1)S(1)} %maximum_select_fusion.4), channel_id=1, source_target_pairs={{0,24},{8,16},{16,8},{24,0},{1,25},{9,17},{17,9},{25,1},{2,26},{10... | collective-permute-start | bytes 196616 | tf_op jit(solution)/shard_map/ppermute | solution.py:16
  13.5 1.3 %copy-done = bf16[1,384,1536]{2,1,0:T(8,128)(2,1)S(1)} copy-done((bf16[1,384,1536]{2,1,0:T(8,128)(2,1)S(1)}, bf16[1,384,1536]{2,1,0:T(8,128)(2,1)}, u32[]{:S(2)}) %copy-start) | copy-done | bytes 1179672
  14.8 0.7 %copy-done.2 = s32[4,4]{1,0:T(4,128)S(1)} copy-done((s32[4,4]{1,0:T(4,128)S(1)}, s32[4,4]{1,0:T(4,128)}, u32[]{:S(2)}) %copy-start.2) | copy-done | bytes 88
  15.5 1.1 %pack.1 = (bf16[384,512]{1,0:T(8,128)(2,1)S(1)}, bf16[384,512]{1,0:T(8,128)(2,1)S(1)}, bf16[384,512]{1,0:T(8,128)(2,1)S(1)}, bf16[384,512]{1,0:T(8,128)(2,1)S(1)}) custom-call(s32[1]{0:T(128)} %bitcast.place, s32[4,4]{1,0:T(4,128)S(1)} %copy-done.2, bf16[384,1536]{1,0:T(8,128)(2,1)S(1)} %bitcast.17), custom_call_target="tpu_custom_call" | custom-call | bytes 3145728 | tf_op jit(solution)/shard_map/pack/pallas_call | solution.py:59
  16.6 0.4 %collective-permute-done.7 = bf16[4,16,512]{2,1,0:T(8,128)(2,1)S(1)} collective-permute-done((bf16[4,16,512]{2,1,0:T(8,128)(2,1)S(1)}, bf16[4,16,512]{2,1,0:T(8,128)(2,1)S(1)}, u32[]{:S(2)}, u32[]{:S(2)}) %collective-permute-start.7) | collective-permute-done | bytes 65568 | tf_op jit(solution)/shard_map/ppermute | solution.py:16
  17.0 0.5 %collective-permute-start.6 = (bf16[4,16,512]{2,1,0:T(8,128)(2,1)S(1)}, bf16[4,16,512]{2,1,0:T(8,128)(2,1)S(1)}, u32[]{:S(2)}, u32[]{:S(2)}) collective-permute-start(bf16[4,16,512]{2,1,0:T(8,128)(2,1)S(1)} %collective-permute-done.5), channel_id=1, source_target_pairs={{0,1},{1,0},{2,3},{3,2},{4,5},{5,4},{6,7},{7,6},{8,9},{9,8},{10,11... | collective-permute-start | bytes 196616 | tf_op jit(solution)/shard_map/ppermute | solution.py:16
  17.6 0.5 %collective-permute-start.4 = (bf16[4,16,512]{2,1,0:T(8,128)(2,1)S(1)}, bf16[4,16,512]{2,1,0:T(8,128)(2,1)S(1)}, u32[]{:S(2)}, u32[]{:S(2)}) collective-permute-start(bf16[4,16,512]{2,1,0:T(8,128)(2,1)S(1)} %collective-permute-done.3), channel_id=1, source_target_pairs={{0,1},{1,0},{2,3},{3,2},{4,5},{5,4},{6,7},{7,6},{8,9},{9,8},{10,11... | collective-permute-start | bytes 196616 | tf_op jit(solution)/shard_map/ppermute | solution.py:16
  18.5 0.3 collective-permute-done.2
  19.0 0.3 half_products.4
  19.3 2.5 %collective-permute-start.9 = (bf16[384,128]{1,0:T(8,128)(2,1)S(1)}, bf16[384,128]{1,0:T(8,128)(2,1)S(1)}, u32[]{:S(2)}, u32[]{:S(2)}) collective-permute-start(bf16[384,128]{1,0:T(8,128)(2,1)S(1)} %half_products.4), channel_id=1, source_target_pairs={{0,24},{8,16},{16,8},{24,0},{1,25},{9,17},{17,9},{25,1},{2,26},{10... | collective-permute-start | bytes 294920 | tf_op jit(solution)/shard_map/ppermute | solution.py:16
  21.8 0.4 half_products.5
  22.2 0.6 %collective-permute-start.10 = (bf16[384,128]{1,0:T(8,128)(2,1)S(1)}, bf16[384,128]{1,0:T(8,128)(2,1)S(1)}, u32[]{:S(2)}, u32[]{:S(2)}) collective-permute-start(bf16[384,128]{1,0:T(8,128)(2,1)S(1)} %get-tuple-element.54), channel_id=1, source_target_pairs={{0,16},{8,24},{16,0},{24,8},{1,17},{9,25},{17,1},{25,9},{2,18},{10... | collective-permute-start | bytes 294920 | tf_op jit(solution)/shard_map/ppermute | solution.py:16
  22.8 0.5 %collective-permute-start.11 = (bf16[384,128]{1,0:T(8,128)(2,1)S(1)}, bf16[384,128]{1,0:T(8,128)(2,1)S(1)}, u32[]{:S(2)}, u32[]{:S(2)}) collective-permute-start(bf16[384,128]{1,0:T(8,128)(2,1)S(1)} %get-tuple-element.55), channel_id=1, source_target_pairs={{0,8},{8,0},{16,24},{24,16},{1,9},{9,1},{17,25},{25,17},{2,10},{10... | collective-permute-start | bytes 294920 | tf_op jit(solution)/shard_map/ppermute | solution.py:16
  23.3 0.3 half_products.3.rest_0_
  23.8 1.4 %prepare.1 = (bf16[512,1536]{1,0:T(8,128)(2,1)S(1)}, bf16[1536,512]{1,0:T(8,128)(2,1)S(1)}, f32[128,512]{1,0:T(8,128)S(1)}, f32[384,1536]{1,0:T(8,128)S(1)}) custom-call(s32[1]{0:T(128)} %bitcast.place, s32[4,4]{1,0:T(4,128)S(1)} %copy-done.3, s32[1,2]{1,0:T(1,128)S(1)} %copy-done.5, f32[300]{0:T(512)S(1)} %copy-done.4, bf16[128,512]{1,0:T(8,128)(2,1)S(1)} %bitcast.21, ...), custom_call_target="tpu_custom_call" | custom-call | bytes 6291456 | tf_op jit(solution)/shard_map/prepare/pallas_call | solution.py:127
  25.4 0.3 mixed.1
  25.7 1.7 %collective-permute-done.10.rest_0_ = bf16[384,128]{1,0:T(8,128)(2,1)S(1)} collective-permute-done((bf16[384,128]{1,0:T(8,128)(2,1)S(1)}, bf16[384,128]{1,0:T(8,128)(2,1)S(1)}, u32[]{:S(2)}, u32[]{:S(2)}) %collective-permute-start.10) | collective-permute-done | bytes 98336 | tf_op jit(solution)/shard_map/ppermute | solution.py:16
  27.4 0.9 %ladders.1 = (bf16[384,128]{1,0:T(8,128)(2,1)S(1)}, bf16[384,128]{1,0:T(8,128)(2,1)S(1)}, bf16[384,128]{1,0:T(8,128)(2,1)S(1)}, bf16[384,128]{1,0:T(8,128)(2,1)S(1)}) custom-call(bf16[1536,512]{1,0:T(8,128)(2,1)S(1)} %get-tuple-element.48.turned, f32[128,512]{1,0:T(8,128)S(1)} %get-tuple-element.49.scale, f32[128,512]{1,0:T(8,128)S(1)} %mixed.1, ...), custom_call_target="tpu_custom_call" | custom-call | tf_op jit(solution)/shard_map/ladders/pallas_call | solution.py:198
  28.3 2.2 %collective-permute-start.12 = (bf16[384,128]{1,0:T(8,128)(2,1)S(1)}, bf16[384,128]{1,0:T(8,128)(2,1)S(1)}, u32[]{:S(2)}, u32[]{:S(2)}) collective-permute-start(bf16[384,128]{1,0:T(8,128)(2,1)S(1)} %get-tuple-element.57), channel_id=1, source_target_pairs={{0,24},{8,16},{16,8},{24,0},{1,25},{9,17},{17,9},{25,1},{2,26},{10... | collective-permute-start | bytes 294920 | tf_op jit(solution)/shard_map/ppermute | solution.py:16
  30.5 0.8 %collective-permute-start.13 = (bf16[384,128]{1,0:T(8,128)(2,1)S(1)}, bf16[384,128]{1,0:T(8,128)(2,1)S(1)}, u32[]{:S(2)}, u32[]{:S(2)}) collective-permute-start(bf16[384,128]{1,0:T(8,128)(2,1)S(1)} %get-tuple-element.59), channel_id=1, source_target_pairs={{0,16},{8,24},{16,0},{24,8},{1,17},{9,25},{17,1},{25,9},{2,18},{10... | collective-permute-start | bytes 294920 | tf_op jit(solution)/shard_map/ppermute | solution.py:16
  31.4 0.5 %collective-permute-start.14 = (bf16[384,128]{1,0:T(8,128)(2,1)S(1)}, bf16[384,128]{1,0:T(8,128)(2,1)S(1)}, u32[]{:S(2)}, u32[]{:S(2)}) collective-permute-start(bf16[384,128]{1,0:T(8,128)(2,1)S(1)} %get-tuple-element.60), channel_id=1, source_target_pairs={{0,8},{8,0},{16,24},{24,16},{1,9},{9,1},{17,25},{25,17},{2,10},{10... | collective-permute-start | bytes 294920 | tf_op jit(solution)/shard_map/ppermute | solution.py:16
  31.9 2.2 %collective-permute-done.12.rest_1_ = bf16[384,128]{1,0:T(8,128)(2,1)S(1)} collective-permute-done((bf16[384,128]{1,0:T(8,128)(2,1)S(1)}, bf16[384,128]{1,0:T(8,128)(2,1)S(1)}, u32[]{:S(2)}, u32[]{:S(2)}) %collective-permute-start.12) | collective-permute-done | bytes 98336 | tf_op jit(solution)/shard_map/ppermute | solution.py:16
  34.0 0.8 %result_start.1.begun = f32[384,1536]{1,0:T(8,128)S(1)} custom-call(bf16[512,1536]{1,0:T(8,128)(2,1)S(1)} %get-tuple-element.47.dense, bf16[384,128]{1,0:T(8,128)(2,1)S(1)} %get-tuple-element.56.rest_0_, bf16[384,128]{1,0:T(8,128)(2,1)S(1)} %collective-permute-done.12.rest_1_), custom_call_target="tpu_custom_call" | custom-call | flops 301989888 | tf_op jit(solution)/shard_map/result_start/pallas_call | solution.py:225
  34.8 1.0 %collective-permute-done.13.rest_0_ = bf16[384,128]{1,0:T(8,128)(2,1)S(1)} collective-permute-done((bf16[384,128]{1,0:T(8,128)(2,1)S(1)}, bf16[384,128]{1,0:T(8,128)(2,1)S(1)}, u32[]{:S(2)}, u32[]{:S(2)}) %collective-permute-start.13) | collective-permute-done | bytes 98336 | tf_op jit(solution)/shard_map/ppermute | solution.py:16
  35.8 0.3 collective-permute-done.14.rest_1_
  36.1 1.9 %results.1 = f32[384,1536]{1,0:T(8,128)} custom-call(f32[384,1536]{1,0:T(8,128)S(1)} %result_start.1.begun, bf16[512,1536]{1,0:T(8,128)(2,1)S(1)} %get-tuple-element.47.dense, f32[384,1536]{1,0:T(8,128)S(1)} %get-tuple-element.58.inverse, bf16[384,128]{1,0:T(8,128)(2,1)S(1)} %collective-permute-done.13.rest_0_, ...), custom_call_target="tpu_custom_call" | custom-call | tf_op jit(solution)/shard_map/results/pallas_call | solution.py:259
  (33 shorter events, 1.3 us)
Async XLA Ops:
  0.0 5.0 %collective-permute-start = (bf16[1,16,512]{2,1,0:T(8,128)(2,1)}, bf16[1,16,512]{2,1,0:T(8,128)(2,1)S(1)}, u32[]{:S(2)}, u32[]{:S(2)}) collective-permute-start(bf16[1,16,512]{2,1,0:T(8,128)(2,1)} %bitcast.35), channel_id=1, source_target_pairs={{0,2},{1,3},{2,0},{3,1},{4,6},{5,7},{6,4},{7,5},{8,10},{9,11},{10,... | collective-permute-start | bytes 49160 | tf_op jit(solution)/shard_map/ppermute | solution.py:16
  5.0 5.0 %collective-permute-start.1 = (bf16[2,16,512]{2,1,0:T(8,128)(2,1)S(1)}, bf16[2,16,512]{2,1,0:T(8,128)(2,1)S(1)}, u32[]{:S(2)}, u32[]{:S(2)}) collective-permute-start(bf16[2,16,512]{2,1,0:T(8,128)(2,1)S(1)} %maximum_select_fusion.5), channel_id=1, source_target_pairs={{0,4},{1,5},{2,6},{3,7},{4,0},{5,1},{6,2},{7,3},{8,12},{9,13},{10,... | collective-permute-start | bytes 98312 | tf_op jit(solution)/shard_map/ppermute | solution.py:16
  10.0 6.6 %collective-permute-start.5 = (bf16[4,16,512]{2,1,0:T(8,128)(2,1)S(1)}, bf16[4,16,512]{2,1,0:T(8,128)(2,1)S(1)}, u32[]{:S(2)}, u32[]{:S(2)}) collective-permute-start(bf16[4,16,512]{2,1,0:T(8,128)(2,1)S(1)} %maximum_select_fusion.4), channel_id=1, source_target_pairs={{0,16},{8,24},{16,0},{24,8},{1,17},{9,25},{17,1},{25,9},{2,18},{10... | collective-permute-start | bytes 196616 | tf_op jit(solution)/shard_map/ppermute | solution.py:16
  11.9 5.2 %collective-permute-start.7 = (bf16[4,16,512]{2,1,0:T(8,128)(2,1)S(1)}, bf16[4,16,512]{2,1,0:T(8,128)(2,1)S(1)}, u32[]{:S(2)}, u32[]{:S(2)}) collective-permute-start(bf16[4,16,512]{2,1,0:T(8,128)(2,1)S(1)} %maximum_select_fusion.4), channel_id=1, source_target_pairs={{0,24},{8,16},{16,8},{24,0},{1,25},{9,17},{17,9},{25,1},{2,26},{10... | collective-permute-start | bytes 196616 | tf_op jit(solution)/shard_map/ppermute | solution.py:16
  13.3 4.3 %collective-permute-start.3 = (bf16[4,16,512]{2,1,0:T(8,128)(2,1)S(1)}, bf16[4,16,512]{2,1,0:T(8,128)(2,1)S(1)}, u32[]{:S(2)}, u32[]{:S(2)}) collective-permute-start(bf16[4,16,512]{2,1,0:T(8,128)(2,1)S(1)} %maximum_select_fusion.4), channel_id=1, source_target_pairs={{0,8},{8,0},{16,24},{24,16},{1,9},{9,1},{17,25},{25,17},{2,10},{10... | collective-permute-start | bytes 196616 | tf_op jit(solution)/shard_map/ppermute | solution.py:16
  13.5 1.3 %copy-start = (bf16[1,384,1536]{2,1,0:T(8,128)(2,1)S(1)}, bf16[1,384,1536]{2,1,0:T(8,128)(2,1)}, u32[]{:S(2)}) copy-start(bf16[1,384,1536]{2,1,0:T(8,128)(2,1)} %param.7) | copy-start | bytes 3538948
  14.8 0.7 %copy-start.2 = (s32[4,4]{1,0:T(4,128)S(1)}, s32[4,4]{1,0:T(4,128)}, u32[]{:S(2)}) copy-start(s32[4,4]{1,0:T(4,128)} %screen.3) | copy-start | bytes 196
  16.5 7.0 %copy-start.6 = (f32[1536]{0:T(1024)S(1)}, f32[1536]{0:T(1024)}, u32[]{:S(2)}) copy-start(f32[1536]{0:T(1024)} %param.12) | copy-start | bytes 18436
  16.5 7.3 %copy-start.1 = (bf16[512,128]{1,0:T(8,128)(2,1)S(1)}, bf16[512,128]{1,0:T(8,128)(2,1)}, u32[]{:S(2)}) copy-start(bf16[512,128]{1,0:T(8,128)(2,1)} %rest_4_.1) | copy-start | bytes 393220
  16.6 7.3 %copy-start.3 = (s32[4,4]{1,0:T(4,128)S(1)}, s32[4,4]{1,0:T(4,128)}, u32[]{:S(2)}) copy-start(s32[4,4]{1,0:T(4,128)} %screen.3) | copy-start | bytes 196
  16.6 7.3 %copy-start.4 = (f32[300]{0:T(512)S(1)}, f32[300]{0:T(512)}, u32[]{:S(2)}) copy-start(f32[300]{0:T(512)} %occ_energy.1) | copy-start | bytes 3604
  16.6 7.3 %copy-start.5 = (s32[1,2]{1,0:T(1,128)S(1)}, s32[1,2]{1,0:T(1,128)}, u32[]{:S(2)}) copy-start(s32[1,2]{1,0:T(1,128)} %pair_occ.1) | copy-start | bytes 28
  17.0 1.3 %collective-permute-start.8 = (bf16[4,16,512]{2,1,0:T(8,128)(2,1)S(1)}, bf16[4,16,512]{2,1,0:T(8,128)(2,1)S(1)}, u32[]{:S(2)}, u32[]{:S(2)}) collective-permute-start(bf16[4,16,512]{2,1,0:T(8,128)(2,1)S(1)} %collective-permute-done.7), channel_id=1, source_target_pairs={{0,1},{1,0},{2,3},{3,2},{4,5},{5,4},{6,7},{7,6},{8,9},{9,8},{10,11... | collective-permute-start | bytes 196616 | tf_op jit(solution)/shard_map/ppermute | solution.py:16
  17.0 1.4 %collective-permute-start.6 = (bf16[4,16,512]{2,1,0:T(8,128)(2,1)S(1)}, bf16[4,16,512]{2,1,0:T(8,128)(2,1)S(1)}, u32[]{:S(2)}, u32[]{:S(2)}) collective-permute-start(bf16[4,16,512]{2,1,0:T(8,128)(2,1)S(1)} %collective-permute-done.5), channel_id=1, source_target_pairs={{0,1},{1,0},{2,3},{3,2},{4,5},{5,4},{6,7},{7,6},{8,9},{9,8},{10,11... | collective-permute-start | bytes 196616 | tf_op jit(solution)/shard_map/ppermute | solution.py:16
  17.6 1.3 %collective-permute-start.2 = (bf16[4,16,512]{2,1,0:T(8,128)(2,1)S(1)}, bf16[4,16,512]{2,1,0:T(8,128)(2,1)S(1)}, u32[]{:S(2)}, u32[]{:S(2)}) collective-permute-start(bf16[4,16,512]{2,1,0:T(8,128)(2,1)S(1)} %maximum_select_fusion.4), channel_id=1, source_target_pairs={{0,1},{1,0},{2,3},{3,2},{4,5},{5,4},{6,7},{7,6},{8,9},{9,8},{10,11... | collective-permute-start | bytes 196616 | tf_op jit(solution)/shard_map/ppermute | solution.py:16
  17.6 1.4 %collective-permute-start.4 = (bf16[4,16,512]{2,1,0:T(8,128)(2,1)S(1)}, bf16[4,16,512]{2,1,0:T(8,128)(2,1)S(1)}, u32[]{:S(2)}, u32[]{:S(2)}) collective-permute-start(bf16[4,16,512]{2,1,0:T(8,128)(2,1)S(1)} %collective-permute-done.3), channel_id=1, source_target_pairs={{0,1},{1,0},{2,3},{3,2},{4,5},{5,4},{6,7},{7,6},{8,9},{9,8},{10,11... | collective-permute-start | bytes 196616 | tf_op jit(solution)/shard_map/ppermute | solution.py:16
  19.3 6.1 %collective-permute-start.9 = (bf16[384,128]{1,0:T(8,128)(2,1)S(1)}, bf16[384,128]{1,0:T(8,128)(2,1)S(1)}, u32[]{:S(2)}, u32[]{:S(2)}) collective-permute-start(bf16[384,128]{1,0:T(8,128)(2,1)S(1)} %half_products.4), channel_id=1, source_target_pairs={{0,24},{8,16},{16,8},{24,0},{1,25},{9,17},{17,9},{25,1},{2,26},{10... | collective-permute-start | bytes 294920 | tf_op jit(solution)/shard_map/ppermute | solution.py:16
  22.2 5.3 %collective-permute-start.10 = (bf16[384,128]{1,0:T(8,128)(2,1)S(1)}, bf16[384,128]{1,0:T(8,128)(2,1)S(1)}, u32[]{:S(2)}, u32[]{:S(2)}) collective-permute-start(bf16[384,128]{1,0:T(8,128)(2,1)S(1)} %get-tuple-element.54), channel_id=1, source_target_pairs={{0,16},{8,24},{16,0},{24,8},{1,17},{9,25},{17,1},{25,9},{2,18},{10... | collective-permute-start | bytes 294920 | tf_op jit(solution)/shard_map/ppermute | solution.py:16
  22.8 4.7 %collective-permute-start.11 = (bf16[384,128]{1,0:T(8,128)(2,1)S(1)}, bf16[384,128]{1,0:T(8,128)(2,1)S(1)}, u32[]{:S(2)}, u32[]{:S(2)}) collective-permute-start(bf16[384,128]{1,0:T(8,128)(2,1)S(1)} %get-tuple-element.55), channel_id=1, source_target_pairs={{0,8},{8,0},{16,24},{24,16},{1,9},{9,1},{17,25},{25,17},{2,10},{10... | collective-permute-start | bytes 294920 | tf_op jit(solution)/shard_map/ppermute | solution.py:16
  28.3 5.7 %collective-permute-start.12 = (bf16[384,128]{1,0:T(8,128)(2,1)S(1)}, bf16[384,128]{1,0:T(8,128)(2,1)S(1)}, u32[]{:S(2)}, u32[]{:S(2)}) collective-permute-start(bf16[384,128]{1,0:T(8,128)(2,1)S(1)} %get-tuple-element.57), channel_id=1, source_target_pairs={{0,24},{8,16},{16,8},{24,0},{1,25},{9,17},{17,9},{25,1},{2,26},{10... | collective-permute-start | bytes 294920 | tf_op jit(solution)/shard_map/ppermute | solution.py:16
  30.5 5.3 %collective-permute-start.13 = (bf16[384,128]{1,0:T(8,128)(2,1)S(1)}, bf16[384,128]{1,0:T(8,128)(2,1)S(1)}, u32[]{:S(2)}, u32[]{:S(2)}) collective-permute-start(bf16[384,128]{1,0:T(8,128)(2,1)S(1)} %get-tuple-element.59), channel_id=1, source_target_pairs={{0,16},{8,24},{16,0},{24,8},{1,17},{9,25},{17,1},{25,9},{2,18},{10... | collective-permute-start | bytes 294920 | tf_op jit(solution)/shard_map/ppermute | solution.py:16
  31.4 4.7 %collective-permute-start.14 = (bf16[384,128]{1,0:T(8,128)(2,1)S(1)}, bf16[384,128]{1,0:T(8,128)(2,1)S(1)}, u32[]{:S(2)}, u32[]{:S(2)}) collective-permute-start(bf16[384,128]{1,0:T(8,128)(2,1)S(1)} %get-tuple-element.60), channel_id=1, source_target_pairs={{0,8},{8,0},{16,24},{24,16},{1,9},{9,1},{17,25},{25,17},{2,10},{10... | collective-permute-start | bytes 294920 | tf_op jit(solution)/shard_map/ppermute | solution.py:16

commit v5 on v4

--- a/solution.py
+++ b/solution.py
@@ -291,23 +291,29 @@
         )
         sent = part
         step *= 2
-        amplitudes, part = lax.optimization_barrier((amplitudes, part))
+        ready, part = lax.optimization_barrier((place, part))
     parts = [exchange(part, "grid", grids, k) if k else part for k in range(grids)]
-    packs = pack(place, screen, amplitudes[0], tile)
-    packs = list(packs)
-    blocks = []
-    for k, part in enumerate(parts):
-        part, packs[k] = lax.optimization_barrier((part, packs[k]))
+    packs = pack(ready, screen, amplitudes[0], tile)
+    def swapped(part):
         other = exchange(part, "pair", pairs, 1)
         both = jnp.where(
             pair & 1 == 0, jnp.stack([part, other], 1), jnp.stack([other, part], 1)
         )
-        blocks.append(both.reshape(-1, packed_factor.shape[1]))
-
+        return both.reshape(-1, packed_factor.shape[1])
+
+    packs = list(packs)
+    blocks = [None] * grids
+    for k in order[1:]:
+        part, packs[k] = lax.optimization_barrier((parts[k], packs[k]))
+        blocks[k] = swapped(part)
     halves = []
-    for ks in ([0], order[1:2], order[2:]):
+    for ks in (order[1:2], order[2:]):
         group = half_products([packs[k] for k in ks], [blocks[k] for k in ks])
-        halves += [exchange(half, "grid", grids, k) if k else half for k, half in zip(ks, group)]
+        if not halves:
+            parts[0], group = lax.optimization_barrier((parts[0], group))
+        halves += [exchange(half, "grid", grids, k) for k, half in zip(ks, group)]
+    blocks[0] = swapped(parts[0])
+    halves = list(half_products([packs[0]], [blocks[0]])) + halves
     vir_energy, halves[0] = lax.optimization_barrier((vir_energy, halves[0]))
     own_vir = lax.dynamic_slice_in_dim(vir_energy, me * rows, rows, 0)[:, None]
     dense, turned, scale, inverse = prepare(

time: 38.2 us -> 38 us (level)
  transfers between devices with their start and end apart: 15 -> 15, of which waited for: 12 -> 10; matrix products, arithmetic and copies ran while one was open for 1% -> 1% of each run, Pallas kernels for 13% -> 14%
where the time goes in v5:
time: 38 us; the launch traced here: 37.8 us
  starting transfers between devices  17.8 us (47%)
  waiting for transfers between devices  9.59 us (25%)
  Pallas kernels  7.87 us (21%)
  local copies, waits for them, and re-layouts  2.22 us (6%)
    ppermute x15, starting transfers between devices, exchange(): return lax.ppermute(value, axis, [(i, i ^ step) for i in range(size)])  17.8 us
    ppermute x15, waiting for transfers between devices, exchange(): return lax.ppermute(value, axis, [(i, i ^ step) for i in range(size)])  9.59 us
    unnamed x14, local copies, waits for them, and re-layouts  1.98 us
    pallas_call x1, Pallas kernels, results(): pl.pallas_call(functools.partial(result_kernel, order, chunks), out_shape...  1.86 us
    pallas_call x1, Pallas kernels, prepare(): pl.pallas_call(functools.partial(prepare_kernel, tile, slots, count), out...  1.39 us
    pallas_call x1, Pallas kernels, pack(): pl.pallas_call(functools.partial(pack_kernel, tile, slots, count), out_sh...  1.06 us
    pallas_call x3, Pallas kernels, half_products(): pl.pallas_call(functools.partial(half_kernel, count), out_shape=[jax.Shap...  0.87 us
    pallas_call x1, Pallas kernels, ladders(): pl.pallas_call(functools.partial(ladder_kernel, order, late), out_shape=[...  0.86 us
  transfers between devices with their start and end apart: 15, of which 10 were waited for; matrix products, arithmetic and copies ran while one was open for 1% of the time, Pallas kernels for 14%

profile of v5, /device:TPU:0, one launch (start us, length us, event | category | flops | bytes accessed | tf_op | source)
XLA Modules:
  0.0 37.8 jit_solution(18150671032064397029)
XLA Ops:
  0.0 3.0 %collective-permute-start = (bf16[1,16,512]{2,1,0:T(8,128)(2,1)}, bf16[1,16,512]{2,1,0:T(8,128)(2,1)S(1)}, u32[]{:S(2)}, u32[]{:S(2)}) collective-permute-start(bf16[1,16,512]{2,1,0:T(8,128)(2,1)} %bitcast.35), channel_id=1, source_target_pairs={{0,2},{1,3},{2,0},{3,1},{4,6},{5,7},{6,4},{7,5},{8,10},{9,11},{10,... | collective-permute-start | bytes 49160 | tf_op jit(solution)/shard_map/ppermute | solution.py:16
  3.0 0.8 %keep.1 = bf16[16,512]{1,0:T(8,128)(2,1)S(1)} custom-call(bf16[16,512]{1,0:T(8,128)(2,1)} %value.1), custom_call_target="tpu_custom_call" | custom-call | tf_op jit(solution)/shard_map/keep/pallas_call | solution.py:25
  3.8 1.2 %collective-permute-done = bf16[1,16,512]{2,1,0:T(8,128)(2,1)S(1)} collective-permute-done((bf16[1,16,512]{2,1,0:T(8,128)(2,1)}, bf16[1,16,512]{2,1,0:T(8,128)(2,1)S(1)}, u32[]{:S(2)}, u32[]{:S(2)}) %collective-permute-start) | collective-permute-done | bytes 16416 | tf_op jit(solution)/shard_map/ppermute | solution.py:16
  5.0 3.1 %collective-permute-start.1 = (bf16[2,16,512]{2,1,0:T(8,128)(2,1)S(1)}, bf16[2,16,512]{2,1,0:T(8,128)(2,1)S(1)}, u32[]{:S(2)}, u32[]{:S(2)}) collective-permute-start(bf16[2,16,512]{2,1,0:T(8,128)(2,1)S(1)} %maximum_select_fusion.5), channel_id=1, source_target_pairs={{0,4},{1,5},{2,6},{3,7},{4,0},{5,1},{6,2},{7,3},{8,12},{9,13},{10,... | collective-permute-start | bytes 98312 | tf_op jit(solution)/shard_map/ppermute | solution.py:16
  8.1 1.9 %collective-permute-done.1 = bf16[2,16,512]{2,1,0:T(8,128)(2,1)S(1)} collective-permute-done((bf16[2,16,512]{2,1,0:T(8,128)(2,1)S(1)}, bf16[2,16,512]{2,1,0:T(8,128)(2,1)S(1)}, u32[]{:S(2)}, u32[]{:S(2)}) %collective-permute-start.1) | collective-permute-done | bytes 32800 | tf_op jit(solution)/shard_map/ppermute | solution.py:16
  10.0 2.8 %collective-permute-start.2 = (bf16[4,16,512]{2,1,0:T(8,128)(2,1)S(1)}, bf16[4,16,512]{2,1,0:T(8,128)(2,1)S(1)}, u32[]{:S(2)}, u32[]{:S(2)}) collective-permute-start(bf16[4,16,512]{2,1,0:T(8,128)(2,1)S(1)} %maximum_select_fusion.4), channel_id=1, source_target_pairs={{0,24},{8,16},{16,8},{24,0},{1,25},{9,17},{17,9},{25,1},{2,26},{10... | collective-permute-start | bytes 196616 | tf_op jit(solution)/shard_map/ppermute | solution.py:16
  12.8 0.5 %collective-permute-start.5 = (bf16[4,16,512]{2,1,0:T(8,128)(2,1)S(1)}, bf16[4,16,512]{2,1,0:T(8,128)(2,1)S(1)}, u32[]{:S(2)}, u32[]{:S(2)}) collective-permute-start(bf16[4,16,512]{2,1,0:T(8,128)(2,1)S(1)} %maximum_select_fusion.4), channel_id=1, source_target_pairs={{0,8},{8,0},{16,24},{24,16},{1,9},{9,1},{17,25},{25,17},{2,10},{10... | collective-permute-start | bytes 196616 | tf_op jit(solution)/shard_map/ppermute | solution.py:16
  13.5 1.3 %copy-done = bf16[1,384,1536]{2,1,0:T(8,128)(2,1)S(1)} copy-done((bf16[1,384,1536]{2,1,0:T(8,128)(2,1)S(1)}, bf16[1,384,1536]{2,1,0:T(8,128)(2,1)}, u32[]{:S(2)}) %copy-start) | copy-done | bytes 1179672
  14.8 0.7 %copy-done.2 = s32[4,4]{1,0:T(4,128)S(1)} copy-done((s32[4,4]{1,0:T(4,128)S(1)}, s32[4,4]{1,0:T(4,128)}, u32[]{:S(2)}) %copy-start.2) | copy-done | bytes 88
  15.5 1.1 %pack.1 = (bf16[384,512]{1,0:T(8,128)(2,1)S(1)}, bf16[384,512]{1,0:T(8,128)(2,1)S(1)}, bf16[384,512]{1,0:T(8,128)(2,1)S(1)}, bf16[384,512]{1,0:T(8,128)(2,1)S(1)}) custom-call(s32[1]{0:T(128)} %bitcast.place, s32[4,4]{1,0:T(4,128)S(1)} %copy-done.2, bf16[384,1536]{1,0:T(8,128)(2,1)S(1)} %bitcast.17), custom_call_target="tpu_custom_call" | custom-call | bytes 3145728 | tf_op jit(solution)/shard_map/pack/pallas_call | solution.py:59
  16.6 0.5 %collective-permute-done.5 = bf16[4,16,512]{2,1,0:T(8,128)(2,1)S(1)} collective-permute-done((bf16[4,16,512]{2,1,0:T(8,128)(2,1)S(1)}, bf16[4,16,512]{2,1,0:T(8,128)(2,1)S(1)}, u32[]{:S(2)}, u32[]{:S(2)}) %collective-permute-start.5) | collective-permute-done | bytes 65568 | tf_op jit(solution)/shard_map/ppermute | solution.py:16
  17.1 0.5 %collective-permute-start.3 = (bf16[4,16,512]{2,1,0:T(8,128)(2,1)S(1)}, bf16[4,16,512]{2,1,0:T(8,128)(2,1)S(1)}, u32[]{:S(2)}, u32[]{:S(2)}) collective-permute-start(bf16[4,16,512]{2,1,0:T(8,128)(2,1)S(1)} %collective-permute-done.2), channel_id=1, source_target_pairs={{0,1},{1,0},{2,3},{3,2},{4,5},{5,4},{6,7},{7,6},{8,9},{9,8},{10,11... | collective-permute-start | bytes 196616 | tf_op jit(solution)/shard_map/ppermute | solution.py:16
  17.6 0.7 %collective-permute-done.6 = bf16[4,16,512]{2,1,0:T(8,128)(2,1)S(1)} collective-permute-done((bf16[4,16,512]{2,1,0:T(8,128)(2,1)S(1)}, bf16[4,16,512]{2,1,0:T(8,128)(2,1)S(1)}, u32[]{:S(2)}, u32[]{:S(2)}) %collective-permute-start.6) | collective-permute-done | bytes 65568 | tf_op jit(solution)/shard_map/ppermute | solution.py:16
  18.5 0.3 half_products.3
  18.8 0.4 %collective-permute-start.4 = (bf16[4,16,512]{2,1,0:T(8,128)(2,1)S(1)}, bf16[4,16,512]{2,1,0:T(8,128)(2,1)S(1)}, u32[]{:S(2)}, u32[]{:S(2)}) collective-permute-start(bf16[4,16,512]{2,1,0:T(8,128)(2,1)S(1)} %maximum_select_fusion.4), channel_id=1, source_target_pairs={{0,1},{1,0},{2,3},{3,2},{4,5},{5,4},{6,7},{7,6},{8,9},{9,8},{10,11... | collective-permute-start | bytes 196616 | tf_op jit(solution)/shard_map/ppermute | solution.py:16
  19.3 2.5 %collective-permute-start.9 = (bf16[384,128]{1,0:T(8,128)(2,1)S(1)}, bf16[384,128]{1,0:T(8,128)(2,1)S(1)}, u32[]{:S(2)}, u32[]{:S(2)}) collective-permute-start(bf16[384,128]{1,0:T(8,128)(2,1)S(1)} %half_products.3), channel_id=1, source_target_pairs={{0,24},{8,16},{16,8},{24,0},{1,25},{9,17},{17,9},{25,1},{2,26},{10... | collective-permute-start | bytes 294920 | tf_op jit(solution)/shard_map/ppermute | solution.py:16
  21.7 0.4 half_products.5
  22.1 0.6 %collective-permute-start.10 = (bf16[384,128]{1,0:T(8,128)(2,1)S(1)}, bf16[384,128]{1,0:T(8,128)(2,1)S(1)}, u32[]{:S(2)}, u32[]{:S(2)}) collective-permute-start(bf16[384,128]{1,0:T(8,128)(2,1)S(1)} %get-tuple-element.52), channel_id=1, source_target_pairs={{0,16},{8,24},{16,0},{24,8},{1,17},{9,25},{17,1},{25,9},{2,18},{10... | collective-permute-start | bytes 294920 | tf_op jit(solution)/shard_map/ppermute | solution.py:16
  22.7 0.6 %collective-permute-start.11 = (bf16[384,128]{1,0:T(8,128)(2,1)S(1)}, bf16[384,128]{1,0:T(8,128)(2,1)S(1)}, u32[]{:S(2)}, u32[]{:S(2)}) collective-permute-start(bf16[384,128]{1,0:T(8,128)(2,1)S(1)} %get-tuple-element.53), channel_id=1, source_target_pairs={{0,8},{8,0},{16,24},{24,16},{1,9},{9,1},{17,25},{25,17},{2,10},{10... | collective-permute-start | bytes 294920 | tf_op jit(solution)/shard_map/ppermute | solution.py:16
  23.3 0.3 half_products.4.rest_0_
  23.8 1.4 %prepare.1 = (bf16[512,1536]{1,0:T(8,128)(2,1)S(1)}, bf16[1536,512]{1,0:T(8,128)(2,1)S(1)}, f32[128,512]{1,0:T(8,128)S(1)}, f32[384,1536]{1,0:T(8,128)S(1)}) custom-call(s32[1]{0:T(128)} %bitcast.place, s32[4,4]{1,0:T(4,128)S(1)} %copy-done.3, s32[1,2]{1,0:T(1,128)S(1)} %copy-done.5, f32[300]{0:T(512)S(1)} %copy-done.4, bf16[128,512]{1,0:T(8,128)(2,1)S(1)} %bitcast.21, ...), custom_call_target="tpu_custom_call" | custom-call | bytes 6291456 | tf_op jit(solution)/shard_map/prepare/pallas_call | solution.py:127
  25.2 0.3 mixed.1
  25.6 1.6 %collective-permute-done.10.rest_0_ = bf16[384,128]{1,0:T(8,128)(2,1)S(1)} collective-permute-done((bf16[384,128]{1,0:T(8,128)(2,1)S(1)}, bf16[384,128]{1,0:T(8,128)(2,1)S(1)}, u32[]{:S(2)}, u32[]{:S(2)}) %collective-permute-start.10) | collective-permute-done | bytes 98336 | tf_op jit(solution)/shard_map/ppermute | solution.py:16
  27.3 0.9 %ladders.1 = (bf16[384,128]{1,0:T(8,128)(2,1)S(1)}, bf16[384,128]{1,0:T(8,128)(2,1)S(1)}, bf16[384,128]{1,0:T(8,128)(2,1)S(1)}, bf16[384,128]{1,0:T(8,128)(2,1)S(1)}) custom-call(bf16[1536,512]{1,0:T(8,128)(2,1)S(1)} %get-tuple-element.46.turned, f32[128,512]{1,0:T(8,128)S(1)} %get-tuple-element.47.scale, f32[128,512]{1,0:T(8,128)S(1)} %mixed.1, ...), custom_call_target="tpu_custom_call" | custom-call | tf_op jit(solution)/shard_map/ladders/pallas_call | solution.py:198
  28.2 2.2 %collective-permute-start.12 = (bf16[384,128]{1,0:T(8,128)(2,1)S(1)}, bf16[384,128]{1,0:T(8,128)(2,1)S(1)}, u32[]{:S(2)}, u32[]{:S(2)}) collective-permute-start(bf16[384,128]{1,0:T(8,128)(2,1)S(1)} %get-tuple-element.55), channel_id=1, source_target_pairs={{0,24},{8,16},{16,8},{24,0},{1,25},{9,17},{17,9},{25,1},{2,26},{10... | collective-permute-start | bytes 294920 | tf_op jit(solution)/shard_map/ppermute | solution.py:16
  30.3 0.8 %collective-permute-start.13 = (bf16[384,128]{1,0:T(8,128)(2,1)S(1)}, bf16[384,128]{1,0:T(8,128)(2,1)S(1)}, u32[]{:S(2)}, u32[]{:S(2)}) collective-permute-start(bf16[384,128]{1,0:T(8,128)(2,1)S(1)} %get-tuple-element.57), channel_id=1, source_target_pairs={{0,16},{8,24},{16,0},{24,8},{1,17},{9,25},{17,1},{25,9},{2,18},{10... | collective-permute-start | bytes 294920 | tf_op jit(solution)/shard_map/ppermute | solution.py:16
  31.1 0.6 %collective-permute-start.14 = (bf16[384,128]{1,0:T(8,128)(2,1)S(1)}, bf16[384,128]{1,0:T(8,128)(2,1)S(1)}, u32[]{:S(2)}, u32[]{:S(2)}) collective-permute-start(bf16[384,128]{1,0:T(8,128)(2,1)S(1)} %get-tuple-element.58), channel_id=1, source_target_pairs={{0,8},{8,0},{16,24},{24,16},{1,9},{9,1},{17,25},{25,17},{2,10},{10... | collective-permute-start | bytes 294920 | tf_op jit(solution)/shard_map/ppermute | solution.py:16
  31.7 2.2 %collective-permute-done.12.rest_1_ = bf16[384,128]{1,0:T(8,128)(2,1)S(1)} collective-permute-done((bf16[384,128]{1,0:T(8,128)(2,1)S(1)}, bf16[384,128]{1,0:T(8,128)(2,1)S(1)}, u32[]{:S(2)}, u32[]{:S(2)}) %collective-permute-start.12) | collective-permute-done | bytes 98336 | tf_op jit(solution)/shard_map/ppermute | solution.py:16
  33.9 0.8 %result_start.1.begun = f32[384,1536]{1,0:T(8,128)S(1)} custom-call(bf16[512,1536]{1,0:T(8,128)(2,1)S(1)} %get-tuple-element.45.dense, bf16[384,128]{1,0:T(8,128)(2,1)S(1)} %get-tuple-element.54.rest_0_, bf16[384,128]{1,0:T(8,128)(2,1)S(1)} %collective-permute-done.12.rest_1_), custom_call_target="tpu_custom_call" | custom-call | flops 301989888 | tf_op jit(solution)/shard_map/result_start/pallas_call | solution.py:225
  34.6 1.0 %collective-permute-done.13.rest_0_ = bf16[384,128]{1,0:T(8,128)(2,1)S(1)} collective-permute-done((bf16[384,128]{1,0:T(8,128)(2,1)S(1)}, bf16[384,128]{1,0:T(8,128)(2,1)S(1)}, u32[]{:S(2)}, u32[]{:S(2)}) %collective-permute-start.13) | collective-permute-done | bytes 98336 | tf_op jit(solution)/shard_map/ppermute | solution.py:16
  35.6 0.3 collective-permute-done.14.rest_1_
  35.9 1.9 %results.1 = f32[384,1536]{1,0:T(8,128)} custom-call(f32[384,1536]{1,0:T(8,128)S(1)} %result_start.1.begun, bf16[512,1536]{1,0:T(8,128)(2,1)S(1)} %get-tuple-element.45.dense, f32[384,1536]{1,0:T(8,128)S(1)} %get-tuple-element.56.inverse, bf16[384,128]{1,0:T(8,128)(2,1)S(1)} %collective-permute-done.13.rest_0_, ...), custom_call_target="tpu_custom_call" | custom-call | tf_op jit(solution)/shard_map/results/pallas_call | solution.py:259
  (34 shorter events, 0.8 us)
Async XLA Ops:
  0.0 5.0 %collective-permute-start = (bf16[1,16,512]{2,1,0:T(8,128)(2,1)}, bf16[1,16,512]{2,1,0:T(8,128)(2,1)S(1)}, u32[]{:S(2)}, u32[]{:S(2)}) collective-permute-start(bf16[1,16,512]{2,1,0:T(8,128)(2,1)} %bitcast.35), channel_id=1, source_target_pairs={{0,2},{1,3},{2,0},{3,1},{4,6},{5,7},{6,4},{7,5},{8,10},{9,11},{10,... | collective-permute-start | bytes 49160 | tf_op jit(solution)/shard_map/ppermute | solution.py:16
  5.0 5.0 %collective-permute-start.1 = (bf16[2,16,512]{2,1,0:T(8,128)(2,1)S(1)}, bf16[2,16,512]{2,1,0:T(8,128)(2,1)S(1)}, u32[]{:S(2)}, u32[]{:S(2)}) collective-permute-start(bf16[2,16,512]{2,1,0:T(8,128)(2,1)S(1)} %maximum_select_fusion.5), channel_id=1, source_target_pairs={{0,4},{1,5},{2,6},{3,7},{4,0},{5,1},{6,2},{7,3},{8,12},{9,13},{10,... | collective-permute-start | bytes 98312 | tf_op jit(solution)/shard_map/ppermute | solution.py:16
  10.0 6.6 %collective-permute-start.2 = (bf16[4,16,512]{2,1,0:T(8,128)(2,1)S(1)}, bf16[4,16,512]{2,1,0:T(8,128)(2,1)S(1)}, u32[]{:S(2)}, u32[]{:S(2)}) collective-permute-start(bf16[4,16,512]{2,1,0:T(8,128)(2,1)S(1)} %maximum_select_fusion.4), channel_id=1, source_target_pairs={{0,24},{8,16},{16,8},{24,0},{1,25},{9,17},{17,9},{25,1},{2,26},{10... | collective-permute-start | bytes 196616 | tf_op jit(solution)/shard_map/ppermute | solution.py:16
  12.8 4.3 %collective-permute-start.5 = (bf16[4,16,512]{2,1,0:T(8,128)(2,1)S(1)}, bf16[4,16,512]{2,1,0:T(8,128)(2,1)S(1)}, u32[]{:S(2)}, u32[]{:S(2)}) collective-permute-start(bf16[4,16,512]{2,1,0:T(8,128)(2,1)S(1)} %maximum_select_fusion.4), channel_id=1, source_target_pairs={{0,8},{8,0},{16,24},{24,16},{1,9},{9,1},{17,25},{25,17},{2,10},{10... | collective-permute-start | bytes 196616 | tf_op jit(solution)/shard_map/ppermute | solution.py:16
  13.3 4.3 %collective-permute-start.7 = (bf16[4,16,512]{2,1,0:T(8,128)(2,1)S(1)}, bf16[4,16,512]{2,1,0:T(8,128)(2,1)S(1)}, u32[]{:S(2)}, u32[]{:S(2)}) collective-permute-start(bf16[4,16,512]{2,1,0:T(8,128)(2,1)S(1)} %maximum_select_fusion.4), channel_id=1, source_target_pairs={{0,16},{8,24},{16,0},{24,8},{1,17},{9,25},{17,1},{25,9},{2,18},{10... | collective-permute-start | bytes 196616 | tf_op jit(solution)/shard_map/ppermute | solution.py:16
  13.5 1.3 %copy-start = (bf16[1,384,1536]{2,1,0:T(8,128)(2,1)S(1)}, bf16[1,384,1536]{2,1,0:T(8,128)(2,1)}, u32[]{:S(2)}) copy-start(bf16[1,384,1536]{2,1,0:T(8,128)(2,1)} %param.7) | copy-start | bytes 3538948
  14.8 0.7 %copy-start.2 = (s32[4,4]{1,0:T(4,128)S(1)}, s32[4,4]{1,0:T(4,128)}, u32[]{:S(2)}) copy-start(s32[4,4]{1,0:T(4,128)} %screen.3) | copy-start | bytes 196
  16.5 7.0 %copy-start.6 = (f32[1536]{0:T(1024)S(1)}, f32[1536]{0:T(1024)}, u32[]{:S(2)}) copy-start(f32[1536]{0:T(1024)} %param.12) | copy-start | bytes 18436
  16.5 7.2 %copy-start.1 = (bf16[512,128]{1,0:T(8,128)(2,1)S(1)}, bf16[512,128]{1,0:T(8,128)(2,1)}, u32[]{:S(2)}) copy-start(bf16[512,128]{1,0:T(8,128)(2,1)} %rest_4_.1) | copy-start | bytes 393220
  16.6 7.2 %copy-start.3 = (s32[4,4]{1,0:T(4,128)S(1)}, s32[4,4]{1,0:T(4,128)}, u32[]{:S(2)}) copy-start(s32[4,4]{1,0:T(4,128)} %screen.3) | copy-start | bytes 196
  16.6 7.2 %copy-start.4 = (f32[300]{0:T(512)S(1)}, f32[300]{0:T(512)}, u32[]{:S(2)}) copy-start(f32[300]{0:T(512)} %occ_energy.1) | copy-start | bytes 3604
  16.6 7.2 %copy-start.5 = (s32[1,2]{1,0:T(1,128)S(1)}, s32[1,2]{1,0:T(1,128)}, u32[]{:S(2)}) copy-start(s32[1,2]{1,0:T(1,128)} %pair_occ.1) | copy-start | bytes 28
  17.1 1.3 %collective-permute-start.6 = (bf16[4,16,512]{2,1,0:T(8,128)(2,1)S(1)}, bf16[4,16,512]{2,1,0:T(8,128)(2,1)S(1)}, u32[]{:S(2)}, u32[]{:S(2)}) collective-permute-start(bf16[4,16,512]{2,1,0:T(8,128)(2,1)S(1)} %collective-permute-done.5), channel_id=1, source_target_pairs={{0,1},{1,0},{2,3},{3,2},{4,5},{5,4},{6,7},{7,6},{8,9},{9,8},{10,11... | collective-permute-start | bytes 196616 | tf_op jit(solution)/shard_map/ppermute | solution.py:16
  17.1 1.4 %collective-permute-start.3 = (bf16[4,16,512]{2,1,0:T(8,128)(2,1)S(1)}, bf16[4,16,512]{2,1,0:T(8,128)(2,1)S(1)}, u32[]{:S(2)}, u32[]{:S(2)}) collective-permute-start(bf16[4,16,512]{2,1,0:T(8,128)(2,1)S(1)} %collective-permute-done.2), channel_id=1, source_target_pairs={{0,1},{1,0},{2,3},{3,2},{4,5},{5,4},{6,7},{7,6},{8,9},{9,8},{10,11... | collective-permute-start | bytes 196616 | tf_op jit(solution)/shard_map/ppermute | solution.py:16
  17.6 1.6 %collective-permute-start.8 = (bf16[4,16,512]{2,1,0:T(8,128)(2,1)S(1)}, bf16[4,16,512]{2,1,0:T(8,128)(2,1)S(1)}, u32[]{:S(2)}, u32[]{:S(2)}) collective-permute-start(bf16[4,16,512]{2,1,0:T(8,128)(2,1)S(1)} %collective-permute-done.7), channel_id=1, source_target_pairs={{0,1},{1,0},{2,3},{3,2},{4,5},{5,4},{6,7},{7,6},{8,9},{9,8},{10,11... | collective-permute-start | bytes 196616 | tf_op jit(solution)/shard_map/ppermute | solution.py:16
  18.8 4.5 %collective-permute-start.4 = (bf16[4,16,512]{2,1,0:T(8,128)(2,1)S(1)}, bf16[4,16,512]{2,1,0:T(8,128)(2,1)S(1)}, u32[]{:S(2)}, u32[]{:S(2)}) collective-permute-start(bf16[4,16,512]{2,1,0:T(8,128)(2,1)S(1)} %maximum_select_fusion.4), channel_id=1, source_target_pairs={{0,1},{1,0},{2,3},{3,2},{4,5},{5,4},{6,7},{7,6},{8,9},{9,8},{10,11... | collective-permute-start | bytes 196616 | tf_op jit(solution)/shard_map/ppermute | solution.py:16
  19.3 6.0 %collective-permute-start.9 = (bf16[384,128]{1,0:T(8,128)(2,1)S(1)}, bf16[384,128]{1,0:T(8,128)(2,1)S(1)}, u32[]{:S(2)}, u32[]{:S(2)}) collective-permute-start(bf16[384,128]{1,0:T(8,128)(2,1)S(1)} %half_products.3), channel_id=1, source_target_pairs={{0,24},{8,16},{16,8},{24,0},{1,25},{9,17},{17,9},{25,1},{2,26},{10... | collective-permute-start | bytes 294920 | tf_op jit(solution)/shard_map/ppermute | solution.py:16
  22.1 5.1 %collective-permute-start.10 = (bf16[384,128]{1,0:T(8,128)(2,1)S(1)}, bf16[384,128]{1,0:T(8,128)(2,1)S(1)}, u32[]{:S(2)}, u32[]{:S(2)}) collective-permute-start(bf16[384,128]{1,0:T(8,128)(2,1)S(1)} %get-tuple-element.52), channel_id=1, source_target_pairs={{0,16},{8,24},{16,0},{24,8},{1,17},{9,25},{17,1},{25,9},{2,18},{10... | collective-permute-start | bytes 294920 | tf_op jit(solution)/shard_map/ppermute | solution.py:16
  22.7 4.6 %collective-permute-start.11 = (bf16[384,128]{1,0:T(8,128)(2,1)S(1)}, bf16[384,128]{1,0:T(8,128)(2,1)S(1)}, u32[]{:S(2)}, u32[]{:S(2)}) collective-permute-start(bf16[384,128]{1,0:T(8,128)(2,1)S(1)} %get-tuple-element.53), channel_id=1, source_target_pairs={{0,8},{8,0},{16,24},{24,16},{1,9},{9,1},{17,25},{25,17},{2,10},{10... | collective-permute-start | bytes 294920 | tf_op jit(solution)/shard_map/ppermute | solution.py:16
  28.2 5.7 %collective-permute-start.12 = (bf16[384,128]{1,0:T(8,128)(2,1)S(1)}, bf16[384,128]{1,0:T(8,128)(2,1)S(1)}, u32[]{:S(2)}, u32[]{:S(2)}) collective-permute-start(bf16[384,128]{1,0:T(8,128)(2,1)S(1)} %get-tuple-element.55), channel_id=1, source_target_pairs={{0,24},{8,16},{16,8},{24,0},{1,25},{9,17},{17,9},{25,1},{2,26},{10... | collective-permute-start | bytes 294920 | tf_op jit(solution)/shard_map/ppermute | solution.py:16
  30.3 5.3 %collective-permute-start.13 = (bf16[384,128]{1,0:T(8,128)(2,1)S(1)}, bf16[384,128]{1,0:T(8,128)(2,1)S(1)}, u32[]{:S(2)}, u32[]{:S(2)}) collective-permute-start(bf16[384,128]{1,0:T(8,128)(2,1)S(1)} %get-tuple-element.57), channel_id=1, source_target_pairs={{0,16},{8,24},{16,0},{24,8},{1,17},{9,25},{17,1},{25,9},{2,18},{10... | collective-permute-start | bytes 294920 | tf_op jit(solution)/shard_map/ppermute | solution.py:16
  31.1 4.8 %collective-permute-start.14 = (bf16[384,128]{1,0:T(8,128)(2,1)S(1)}, bf16[384,128]{1,0:T(8,128)(2,1)S(1)}, u32[]{:S(2)}, u32[]{:S(2)}) collective-permute-start(bf16[384,128]{1,0:T(8,128)(2,1)S(1)} %get-tuple-element.58), channel_id=1, source_target_pairs={{0,8},{8,0},{16,24},{24,16},{1,9},{9,1},{17,25},{25,17},{2,10},{10... | collective-permute-start | bytes 294920 | tf_op jit(solution)/shard_map/ppermute | solution.py:16

commit v6 on v5

--- a/solution.py
+++ b/solution.py
@@ -174,35 +174,60 @@
     )(place, turned, *halves)
 
 
-def ladder_kernel(order, late, turned, scale, mixed, *rest):
-    halves, outs = rest[: len(late)], rest[len(late) :]
-    me = lax.axis_index("grid")
+def own_rows(turned, k, rows):
+    start = (lax.axis_index("grid") ^ k) * rows
+    return turned[pl.ds(pl.multiple_of(start, rows), rows), :]
+
+
+def ladder_piece(turned, k, weighted, rows):
+    return lax.dot_general(
+        own_rows(turned, k, rows), weighted, (((1,), (1,)), ((), ())), preferred_element_type=F32
+    ).astype(BF16)
+
+
+def weighted_kernel(first, late, turned, scale, mixed, *rest):
+    halves, (weighted, out) = rest[: len(late)], rest[len(late) :]
     rows = halves[0].shape[0]
-
-    def own_rows(k):
-        return turned[pl.ds(pl.multiple_of((me ^ k) * rows, rows), rows), :]
-
     total = mixed[...]
     for k, half in zip(late, halves):
-        total = total + mixed_part(half[...], own_rows(k))
-    weighted = (scale[...] * total).astype(BF16)
-    for k in order:
-        outs[k][...] = lax.dot_general(
-            own_rows(k), weighted, (((1,), (1,)), ((), ())), preferred_element_type=F32
-        ).astype(BF16)
+        total = total + mixed_part(half[...], own_rows(turned, k, rows))
+    weighted[...] = (scale[...] * total).astype(BF16)
+    out[...] = ladder_piece(turned, first, weighted[...], rows)
+
+
+def ladder_kernel(ks, turned, weighted, *outs):
+    for k, out in zip(ks, outs):
+        out[...] = ladder_piece(turned, k, weighted[...], out.shape[0])
 
 
 def ladders(order, late, turned, scale, mixed, halves):
     rows, width = halves[0].shape
     vmem = pl.BlockSpec(memory_space=pltpu.VMEM)
-    return pl.pallas_call(
-        functools.partial(ladder_kernel, order, late),
-        out_shape=[jax.ShapeDtypeStruct((rows, width), BF16)] * len(order),
+    piece = jax.ShapeDtypeStruct((rows, width), BF16)
+    limit = pltpu.CompilerParams(vmem_limit_bytes=VMEM_LIMIT)
+    pieces = {}
+    weighted, pieces[order[1]] = pl.pallas_call(
+        functools.partial(weighted_kernel, order[1], late),
+        out_shape=[jax.ShapeDtypeStruct(scale.shape, BF16), piece],
         in_specs=[vmem] * (3 + len(halves)),
-        out_specs=[vmem] * len(order),
-        compiler_params=pltpu.CompilerParams(vmem_limit_bytes=VMEM_LIMIT),
-        name="ladders",
+        out_specs=[vmem] * 2,
+        compiler_params=limit,
+        name="weighted",
     )(turned, scale, mixed, *halves)
+    for ks in (order[2:], order[:1]):
+        outs = pl.pallas_call(
+            functools.partial(ladder_kernel, ks),
+            out_shape=[piece] * len(ks),
+            in_specs=[vmem] * 2,
+            out_specs=[vmem] * len(ks),
+            cost_estimate=pl.CostEstimate(
+                flops=2 * len(ks) * rows * weighted.size, bytes_accessed=0, transcendentals=0
+            ),
+            compiler_params=limit,
+            name="ladders",
+        )(turned, weighted)
+        pieces.update(zip(ks, outs))
+    return [pieces[k] for k in range(len(order))]
 
 
 def joined(order, width, pieces, dense, span):

time: 38 us -> 38 us (level)
  waiting for transfers between devices: 9.59 us -> 9.16 us
    ppermute x15, waiting for transfers between devices: 9.59 us -> 9.16 us  [exchange(): return lax.ppermute(value, axis, [(i, i ^ step) for i in range(size)])]
    pallas_call x1 -> x3, Pallas kernels: 0.86 us -> 1.17 us  [the longest x2 0.61 us: ladders(): pl.pallas_call(functools.partial(ladder_kernel, ks), out_shape=[piece] *...]
  transfers between devices with their start and end apart: 15 -> 15, of which waited for: 10 -> 10; matrix products, arithmetic and copies ran while one was open for 1% -> 1% of each run, Pallas kernels for 14% -> 15%
where the time goes in v6:
time: 38 us; the launch traced here: 37.7 us
  starting transfers between devices  17.8 us (47%)
  waiting for transfers between devices  9.16 us (24%)
  Pallas kernels  8.18 us (22%)
  local copies, waits for them, and re-layouts  2.22 us (6%)
    ppermute x15, starting transfers between devices, exchange(): return lax.ppermute(value, axis, [(i, i ^ step) for i in range(size)])  17.8 us
    ppermute x15, waiting for transfers between devices, exchange(): return lax.ppermute(value, axis, [(i, i ^ step) for i in range(size)])  9.16 us
    unnamed x14, local copies, waits for them, and re-layouts  1.98 us
    pallas_call x1, Pallas kernels, results(): pl.pallas_call(functools.partial(result_kernel, order, chunks), out_shape...  1.86 us
    pallas_call x1, Pallas kernels, prepare(): pl.pallas_call(functools.partial(prepare_kernel, tile, slots, count), out...  1.39 us
    pallas_call x1, Pallas kernels, pack(): pl.pallas_call(functools.partial(pack_kernel, tile, slots, count), out_sh...  1.06 us
    pallas_call x3, Pallas kernels, half_products(): pl.pallas_call(functools.partial(half_kernel, count), out_shape=[jax.Shap...  0.87 us
  transfers between devices with their start and end apart: 15, of which 10 were waited for; matrix products, arithmetic and copies ran while one was open for 1% of the time, Pallas kernels for 15%

profile of v6, /device:TPU:0, one launch (start us, length us, event | category | flops | bytes accessed | tf_op | source)
XLA Modules:
  0.0 37.7 jit_solution(17801585124894588164)
XLA Ops:
  0.0 3.0 %collective-permute-start = (bf16[1,16,512]{2,1,0:T(8,128)(2,1)}, bf16[1,16,512]{2,1,0:T(8,128)(2,1)S(1)}, u32[]{:S(2)}, u32[]{:S(2)}) collective-permute-start(bf16[1,16,512]{2,1,0:T(8,128)(2,1)} %bitcast.35), channel_id=1, source_target_pairs={{0,2},{1,3},{2,0},{3,1},{4,6},{5,7},{6,4},{7,5},{8,10},{9,11},{10,... | collective-permute-start | bytes 49160 | tf_op jit(solution)/shard_map/ppermute | solution.py:16
  3.0 0.8 %keep.1 = bf16[16,512]{1,0:T(8,128)(2,1)S(1)} custom-call(bf16[16,512]{1,0:T(8,128)(2,1)} %value.1), custom_call_target="tpu_custom_call" | custom-call | tf_op jit(solution)/shard_map/keep/pallas_call | solution.py:25
  3.8 1.2 %collective-permute-done = bf16[1,16,512]{2,1,0:T(8,128)(2,1)S(1)} collective-permute-done((bf16[1,16,512]{2,1,0:T(8,128)(2,1)}, bf16[1,16,512]{2,1,0:T(8,128)(2,1)S(1)}, u32[]{:S(2)}, u32[]{:S(2)}) %collective-permute-start) | collective-permute-done | bytes 16416 | tf_op jit(solution)/shard_map/ppermute | solution.py:16
  5.0 3.1 %collective-permute-start.1 = (bf16[2,16,512]{2,1,0:T(8,128)(2,1)S(1)}, bf16[2,16,512]{2,1,0:T(8,128)(2,1)S(1)}, u32[]{:S(2)}, u32[]{:S(2)}) collective-permute-start(bf16[2,16,512]{2,1,0:T(8,128)(2,1)S(1)} %maximum_select_fusion.5), channel_id=1, source_target_pairs={{0,4},{1,5},{2,6},{3,7},{4,0},{5,1},{6,2},{7,3},{8,12},{9,13},{10,... | collective-permute-start | bytes 98312 | tf_op jit(solution)/shard_map/ppermute | solution.py:16
  8.1 1.9 %collective-permute-done.1 = bf16[2,16,512]{2,1,0:T(8,128)(2,1)S(1)} collective-permute-done((bf16[2,16,512]{2,1,0:T(8,128)(2,1)S(1)}, bf16[2,16,512]{2,1,0:T(8,128)(2,1)S(1)}, u32[]{:S(2)}, u32[]{:S(2)}) %collective-permute-start.1) | collective-permute-done | bytes 32800 | tf_op jit(solution)/shard_map/ppermute | solution.py:16
  10.0 2.8 %collective-permute-start.2 = (bf16[4,16,512]{2,1,0:T(8,128)(2,1)S(1)}, bf16[4,16,512]{2,1,0:T(8,128)(2,1)S(1)}, u32[]{:S(2)}, u32[]{:S(2)}) collective-permute-start(bf16[4,16,512]{2,1,0:T(8,128)(2,1)S(1)} %maximum_select_fusion.4), channel_id=1, source_target_pairs={{0,24},{8,16},{16,8},{24,0},{1,25},{9,17},{17,9},{25,1},{2,26},{10... | collective-permute-start | bytes 196616 | tf_op jit(solution)/shard_map/ppermute | solution.py:16
  12.8 0.5 %collective-permute-start.5 = (bf16[4,16,512]{2,1,0:T(8,128)(2,1)S(1)}, bf16[4,16,512]{2,1,0:T(8,128)(2,1)S(1)}, u32[]{:S(2)}, u32[]{:S(2)}) collective-permute-start(bf16[4,16,512]{2,1,0:T(8,128)(2,1)S(1)} %maximum_select_fusion.4), channel_id=1, source_target_pairs={{0,8},{8,0},{16,24},{24,16},{1,9},{9,1},{17,25},{25,17},{2,10},{10... | collective-permute-start | bytes 196616 | tf_op jit(solution)/shard_map/ppermute | solution.py:16
  13.5 1.3 %copy-done = bf16[1,384,1536]{2,1,0:T(8,128)(2,1)S(1)} copy-done((bf16[1,384,1536]{2,1,0:T(8,128)(2,1)S(1)}, bf16[1,384,1536]{2,1,0:T(8,128)(2,1)}, u32[]{:S(2)}) %copy-start) | copy-done | bytes 1179672
  14.8 0.7 %copy-done.2 = s32[4,4]{1,0:T(4,128)S(1)} copy-done((s32[4,4]{1,0:T(4,128)S(1)}, s32[4,4]{1,0:T(4,128)}, u32[]{:S(2)}) %copy-start.2) | copy-done | bytes 88
  15.5 1.1 %pack.1 = (bf16[384,512]{1,0:T(8,128)(2,1)S(1)}, bf16[384,512]{1,0:T(8,128)(2,1)S(1)}, bf16[384,512]{1,0:T(8,128)(2,1)S(1)}, bf16[384,512]{1,0:T(8,128)(2,1)S(1)}) custom-call(s32[1]{0:T(128)} %bitcast.place, s32[4,4]{1,0:T(4,128)S(1)} %copy-done.2, bf16[384,1536]{1,0:T(8,128)(2,1)S(1)} %bitcast.17), custom_call_target="tpu_custom_call" | custom-call | bytes 3145728 | tf_op jit(solution)/shard_map/pack/pallas_call | solution.py:59
  16.6 0.5 %collective-permute-done.5 = bf16[4,16,512]{2,1,0:T(8,128)(2,1)S(1)} collective-permute-done((bf16[4,16,512]{2,1,0:T(8,128)(2,1)S(1)}, bf16[4,16,512]{2,1,0:T(8,128)(2,1)S(1)}, u32[]{:S(2)}, u32[]{:S(2)}) %collective-permute-start.5) | collective-permute-done | bytes 65568 | tf_op jit(solution)/shard_map/ppermute | solution.py:16
  17.1 0.5 %collective-permute-start.3 = (bf16[4,16,512]{2,1,0:T(8,128)(2,1)S(1)}, bf16[4,16,512]{2,1,0:T(8,128)(2,1)S(1)}, u32[]{:S(2)}, u32[]{:S(2)}) collective-permute-start(bf16[4,16,512]{2,1,0:T(8,128)(2,1)S(1)} %collective-permute-done.2), channel_id=1, source_target_pairs={{0,1},{1,0},{2,3},{3,2},{4,5},{5,4},{6,7},{7,6},{8,9},{9,8},{10,11... | collective-permute-start | bytes 196616 | tf_op jit(solution)/shard_map/ppermute | solution.py:16
  17.6 0.7 %collective-permute-done.6 = bf16[4,16,512]{2,1,0:T(8,128)(2,1)S(1)} collective-permute-done((bf16[4,16,512]{2,1,0:T(8,128)(2,1)S(1)}, bf16[4,16,512]{2,1,0:T(8,128)(2,1)S(1)}, u32[]{:S(2)}, u32[]{:S(2)}) %collective-permute-start.6) | collective-permute-done | bytes 65568 | tf_op jit(solution)/shard_map/ppermute | solution.py:16
  18.8 0.4 %collective-permute-start.4 = (bf16[4,16,512]{2,1,0:T(8,128)(2,1)S(1)}, bf16[4,16,512]{2,1,0:T(8,128)(2,1)S(1)}, u32[]{:S(2)}, u32[]{:S(2)}) collective-permute-start(bf16[4,16,512]{2,1,0:T(8,128)(2,1)S(1)} %maximum_select_fusion.4), channel_id=1, source_target_pairs={{0,1},{1,0},{2,3},{3,2},{4,5},{5,4},{6,7},{7,6},{8,9},{9,8},{10,11... | collective-permute-start | bytes 196616 | tf_op jit(solution)/shard_map/ppermute | solution.py:16
  19.3 2.5 %collective-permute-start.9 = (bf16[384,128]{1,0:T(8,128)(2,1)S(1)}, bf16[384,128]{1,0:T(8,128)(2,1)S(1)}, u32[]{:S(2)}, u32[]{:S(2)}) collective-permute-start(bf16[384,128]{1,0:T(8,128)(2,1)S(1)} %half_products.3), channel_id=1, source_target_pairs={{0,24},{8,16},{16,8},{24,0},{1,25},{9,17},{17,9},{25,1},{2,26},{10... | collective-permute-start | bytes 294920 | tf_op jit(solution)/shard_map/ppermute | solution.py:16
  21.7 0.4 half_products.5
  22.1 0.6 %collective-permute-start.10 = (bf16[384,128]{1,0:T(8,128)(2,1)S(1)}, bf16[384,128]{1,0:T(8,128)(2,1)S(1)}, u32[]{:S(2)}, u32[]{:S(2)}) collective-permute-start(bf16[384,128]{1,0:T(8,128)(2,1)S(1)} %get-tuple-element.52), channel_id=1, source_target_pairs={{0,16},{8,24},{16,0},{24,8},{1,17},{9,25},{17,1},{25,9},{2,18},{10... | collective-permute-start | bytes 294920 | tf_op jit(solution)/shard_map/ppermute | solution.py:16
  22.7 0.6 %collective-permute-start.11 = (bf16[384,128]{1,0:T(8,128)(2,1)S(1)}, bf16[384,128]{1,0:T(8,128)(2,1)S(1)}, u32[]{:S(2)}, u32[]{:S(2)}) collective-permute-start(bf16[384,128]{1,0:T(8,128)(2,1)S(1)} %get-tuple-element.53), channel_id=1, source_target_pairs={{0,8},{8,0},{16,24},{24,16},{1,9},{9,1},{17,25},{25,17},{2,10},{10... | collective-permute-start | bytes 294920 | tf_op jit(solution)/shard_map/ppermute | solution.py:16
  23.8 1.4 %prepare.1 = (bf16[512,1536]{1,0:T(8,128)(2,1)S(1)}, bf16[1536,512]{1,0:T(8,128)(2,1)S(1)}, f32[128,512]{1,0:T(8,128)S(1)}, f32[384,1536]{1,0:T(8,128)S(1)}) custom-call(s32[1]{0:T(128)} %bitcast.place, s32[4,4]{1,0:T(4,128)S(1)} %copy-done.3, s32[1,2]{1,0:T(1,128)S(1)} %copy-done.5, f32[300]{0:T(512)S(1)} %copy-done.4, bf16[128,512]{1,0:T(8,128)(2,1)S(1)} %bitcast.21, ...), custom_call_target="tpu_custom_call" | custom-call | bytes 6291456 | tf_op jit(solution)/shard_map/prepare/pallas_call | solution.py:127
  25.2 0.3 mixed.1
  25.6 1.6 %collective-permute-done.10.rest_0_ = bf16[384,128]{1,0:T(8,128)(2,1)S(1)} collective-permute-done((bf16[384,128]{1,0:T(8,128)(2,1)S(1)}, bf16[384,128]{1,0:T(8,128)(2,1)S(1)}, u32[]{:S(2)}, u32[]{:S(2)}) %collective-permute-start.10) | collective-permute-done | bytes 98336 | tf_op jit(solution)/shard_map/ppermute | solution.py:16
  27.3 0.6 %weighted.1 = (bf16[128,512]{1,0:T(8,128)(2,1)S(1)}, bf16[384,128]{1,0:T(8,128)(2,1)S(1)}) custom-call(bf16[1536,512]{1,0:T(8,128)(2,1)S(1)} %get-tuple-element.46.turned, f32[128,512]{1,0:T(8,128)S(1)} %get-tuple-element.47.scale, f32[128,512]{1,0:T(8,128)S(1)} %mixed.1, bf16[384,128]{1,0:T(8,128)(2,1)S(1)} %collective-permute-done.10.rest_0_, ...), custom_call_target="tpu_custom_call" | custom-call | tf_op jit(solution)/shard_map/weighted/pallas_call | solution.py:209
  27.9 2.2 %collective-permute-start.12 = (bf16[384,128]{1,0:T(8,128)(2,1)S(1)}, bf16[384,128]{1,0:T(8,128)(2,1)S(1)}, u32[]{:S(2)}, u32[]{:S(2)}) collective-permute-start(bf16[384,128]{1,0:T(8,128)(2,1)S(1)} %get-tuple-element.55), channel_id=1, source_target_pairs={{0,24},{8,16},{16,8},{24,0},{1,25},{9,17},{17,9},{25,1},{2,26},{10... | collective-permute-start | bytes 294920 | tf_op jit(solution)/shard_map/ppermute | solution.py:16
  30.0 0.4 ladders.3
  30.4 0.9 %collective-permute-start.13 = (bf16[384,128]{1,0:T(8,128)(2,1)S(1)}, bf16[384,128]{1,0:T(8,128)(2,1)S(1)}, u32[]{:S(2)}, u32[]{:S(2)}) collective-permute-start(bf16[384,128]{1,0:T(8,128)(2,1)S(1)} %get-tuple-element.57), channel_id=1, source_target_pairs={{0,16},{8,24},{16,0},{24,8},{1,17},{9,25},{17,1},{25,9},{2,18},{10... | collective-permute-start | bytes 294920 | tf_op jit(solution)/shard_map/ppermute | solution.py:16
  31.2 0.6 %collective-permute-start.14 = (bf16[384,128]{1,0:T(8,128)(2,1)S(1)}, bf16[384,128]{1,0:T(8,128)(2,1)S(1)}, u32[]{:S(2)}, u32[]{:S(2)}) collective-permute-start(bf16[384,128]{1,0:T(8,128)(2,1)S(1)} %get-tuple-element.58), channel_id=1, source_target_pairs={{0,8},{8,0},{16,24},{24,16},{1,9},{9,1},{17,25},{25,17},{2,10},{10... | collective-permute-start | bytes 294920 | tf_op jit(solution)/shard_map/ppermute | solution.py:16
  31.8 0.3 ladders.2.rest_0_
  32.1 1.4 %collective-permute-done.12.rest_1_ = bf16[384,128]{1,0:T(8,128)(2,1)S(1)} collective-permute-done((bf16[384,128]{1,0:T(8,128)(2,1)S(1)}, bf16[384,128]{1,0:T(8,128)(2,1)S(1)}, u32[]{:S(2)}, u32[]{:S(2)}) %collective-permute-start.12) | collective-permute-done | bytes 98336 | tf_op jit(solution)/shard_map/ppermute | solution.py:16
  33.5 0.8 %result_start.1.begun = f32[384,1536]{1,0:T(8,128)S(1)} custom-call(bf16[512,1536]{1,0:T(8,128)(2,1)S(1)} %get-tuple-element.45.dense, bf16[384,128]{1,0:T(8,128)(2,1)S(1)} %ladders.2.rest_0_, bf16[384,128]{1,0:T(8,128)(2,1)S(1)} %collective-permute-done.12.rest_1_), custom_call_target="tpu_custom_call" | custom-call | flops 301989888 | tf_op jit(solution)/shard_map/result_start/pallas_call | solution.py:250
  34.3 1.3 %collective-permute-done.13.rest_0_ = bf16[384,128]{1,0:T(8,128)(2,1)S(1)} collective-permute-done((bf16[384,128]{1,0:T(8,128)(2,1)S(1)}, bf16[384,128]{1,0:T(8,128)(2,1)S(1)}, u32[]{:S(2)}, u32[]{:S(2)}) %collective-permute-start.13) | collective-permute-done | bytes 98336 | tf_op jit(solution)/shard_map/ppermute | solution.py:16
  35.5 0.3 collective-permute-done.14.rest_1_
  35.9 1.9 %results.1 = f32[384,1536]{1,0:T(8,128)} custom-call(f32[384,1536]{1,0:T(8,128)S(1)} %result_start.1.begun, bf16[512,1536]{1,0:T(8,128)(2,1)S(1)} %get-tuple-element.45.dense, f32[384,1536]{1,0:T(8,128)S(1)} %get-tuple-element.56.inverse, bf16[384,128]{1,0:T(8,128)(2,1)S(1)} %collective-permute-done.13.rest_0_, ...), custom_call_target="tpu_custom_call" | custom-call | tf_op jit(solution)/shard_map/results/pallas_call | solution.py:284
  (36 shorter events, 1.3 us)
Async XLA Ops:
  0.0 5.0 %collective-permute-start = (bf16[1,16,512]{2,1,0:T(8,128)(2,1)}, bf16[1,16,512]{2,1,0:T(8,128)(2,1)S(1)}, u32[]{:S(2)}, u32[]{:S(2)}) collective-permute-start(bf16[1,16,512]{2,1,0:T(8,128)(2,1)} %bitcast.35), channel_id=1, source_target_pairs={{0,2},{1,3},{2,0},{3,1},{4,6},{5,7},{6,4},{7,5},{8,10},{9,11},{10,... | collective-permute-start | bytes 49160 | tf_op jit(solution)/shard_map/ppermute | solution.py:16
  5.0 5.0 %collective-permute-start.1 = (bf16[2,16,512]{2,1,0:T(8,128)(2,1)S(1)}, bf16[2,16,512]{2,1,0:T(8,128)(2,1)S(1)}, u32[]{:S(2)}, u32[]{:S(2)}) collective-permute-start(bf16[2,16,512]{2,1,0:T(8,128)(2,1)S(1)} %maximum_select_fusion.5), channel_id=1, source_target_pairs={{0,4},{1,5},{2,6},{3,7},{4,0},{5,1},{6,2},{7,3},{8,12},{9,13},{10,... | collective-permute-start | bytes 98312 | tf_op jit(solution)/shard_map/ppermute | solution.py:16
  10.0 6.6 %collective-permute-start.2 = (bf16[4,16,512]{2,1,0:T(8,128)(2,1)S(1)}, bf16[4,16,512]{2,1,0:T(8,128)(2,1)S(1)}, u32[]{:S(2)}, u32[]{:S(2)}) collective-permute-start(bf16[4,16,512]{2,1,0:T(8,128)(2,1)S(1)} %maximum_select_fusion.4), channel_id=1, source_target_pairs={{0,24},{8,16},{16,8},{24,0},{1,25},{9,17},{17,9},{25,1},{2,26},{10... | collective-permute-start | bytes 196616 | tf_op jit(solution)/shard_map/ppermute | solution.py:16
  12.8 4.3 %collective-permute-start.5 = (bf16[4,16,512]{2,1,0:T(8,128)(2,1)S(1)}, bf16[4,16,512]{2,1,0:T(8,128)(2,1)S(1)}, u32[]{:S(2)}, u32[]{:S(2)}) collective-permute-start(bf16[4,16,512]{2,1,0:T(8,128)(2,1)S(1)} %maximum_select_fusion.4), channel_id=1, source_target_pairs={{0,8},{8,0},{16,24},{24,16},{1,9},{9,1},{17,25},{25,17},{2,10},{10... | collective-permute-start | bytes 196616 | tf_op jit(solution)/shard_map/ppermute | solution.py:16
  13.3 4.3 %collective-permute-start.7 = (bf16[4,16,512]{2,1,0:T(8,128)(2,1)S(1)}, bf16[4,16,512]{2,1,0:T(8,128)(2,1)S(1)}, u32[]{:S(2)}, u32[]{:S(2)}) collective-permute-start(bf16[4,16,512]{2,1,0:T(8,128)(2,1)S(1)} %maximum_select_fusion.4), channel_id=1, source_target_pairs={{0,16},{8,24},{16,0},{24,8},{1,17},{9,25},{17,1},{25,9},{2,18},{10... | collective-permute-start | bytes 196616 | tf_op jit(solution)/shard_map/ppermute | solution.py:16
  13.5 1.3 %copy-start = (bf16[1,384,1536]{2,1,0:T(8,128)(2,1)S(1)}, bf16[1,384,1536]{2,1,0:T(8,128)(2,1)}, u32[]{:S(2)}) copy-start(bf16[1,384,1536]{2,1,0:T(8,128)(2,1)} %param.7) | copy-start | bytes 3538948
  14.8 0.7 %copy-start.2 = (s32[4,4]{1,0:T(4,128)S(1)}, s32[4,4]{1,0:T(4,128)}, u32[]{:S(2)}) copy-start(s32[4,4]{1,0:T(4,128)} %screen.3) | copy-start | bytes 196
  16.5 7.0 %copy-start.6 = (f32[1536]{0:T(1024)S(1)}, f32[1536]{0:T(1024)}, u32[]{:S(2)}) copy-start(f32[1536]{0:T(1024)} %param.12) | copy-start | bytes 18436
  16.5 7.2 %copy-start.1 = (bf16[512,128]{1,0:T(8,128)(2,1)S(1)}, bf16[512,128]{1,0:T(8,128)(2,1)}, u32[]{:S(2)}) copy-start(bf16[512,128]{1,0:T(8,128)(2,1)} %rest_4_.1) | copy-start | bytes 393220
  16.6 7.2 %copy-start.3 = (s32[4,4]{1,0:T(4,128)S(1)}, s32[4,4]{1,0:T(4,128)}, u32[]{:S(2)}) copy-start(s32[4,4]{1,0:T(4,128)} %screen.3) | copy-start | bytes 196
  16.6 7.2 %copy-start.4 = (f32[300]{0:T(512)S(1)}, f32[300]{0:T(512)}, u32[]{:S(2)}) copy-start(f32[300]{0:T(512)} %occ_energy.1) | copy-start | bytes 3604
  16.6 7.2 %copy-start.5 = (s32[1,2]{1,0:T(1,128)S(1)}, s32[1,2]{1,0:T(1,128)}, u32[]{:S(2)}) copy-start(s32[1,2]{1,0:T(1,128)} %pair_occ.1) | copy-start | bytes 28
  17.1 1.3 %collective-permute-start.6 = (bf16[4,16,512]{2,1,0:T(8,128)(2,1)S(1)}, bf16[4,16,512]{2,1,0:T(8,128)(2,1)S(1)}, u32[]{:S(2)}, u32[]{:S(2)}) collective-permute-start(bf16[4,16,512]{2,1,0:T(8,128)(2,1)S(1)} %collective-permute-done.5), channel_id=1, source_target_pairs={{0,1},{1,0},{2,3},{3,2},{4,5},{5,4},{6,7},{7,6},{8,9},{9,8},{10,11... | collective-permute-start | bytes 196616 | tf_op jit(solution)/shard_map/ppermute | solution.py:16
  17.1 1.4 %collective-permute-start.3 = (bf16[4,16,512]{2,1,0:T(8,128)(2,1)S(1)}, bf16[4,16,512]{2,1,0:T(8,128)(2,1)S(1)}, u32[]{:S(2)}, u32[]{:S(2)}) collective-permute-start(bf16[4,16,512]{2,1,0:T(8,128)(2,1)S(1)} %collective-permute-done.2), channel_id=1, source_target_pairs={{0,1},{1,0},{2,3},{3,2},{4,5},{5,4},{6,7},{7,6},{8,9},{9,8},{10,11... | collective-permute-start | bytes 196616 | tf_op jit(solution)/shard_map/ppermute | solution.py:16
  17.6 1.6 %collective-permute-start.8 = (bf16[4,16,512]{2,1,0:T(8,128)(2,1)S(1)}, bf16[4,16,512]{2,1,0:T(8,128)(2,1)S(1)}, u32[]{:S(2)}, u32[]{:S(2)}) collective-permute-start(bf16[4,16,512]{2,1,0:T(8,128)(2,1)S(1)} %collective-permute-done.7), channel_id=1, source_target_pairs={{0,1},{1,0},{2,3},{3,2},{4,5},{5,4},{6,7},{7,6},{8,9},{9,8},{10,11... | collective-permute-start | bytes 196616 | tf_op jit(solution)/shard_map/ppermute | solution.py:16
  18.8 4.5 %collective-permute-start.4 = (bf16[4,16,512]{2,1,0:T(8,128)(2,1)S(1)}, bf16[4,16,512]{2,1,0:T(8,128)(2,1)S(1)}, u32[]{:S(2)}, u32[]{:S(2)}) collective-permute-start(bf16[4,16,512]{2,1,0:T(8,128)(2,1)S(1)} %maximum_select_fusion.4), channel_id=1, source_target_pairs={{0,1},{1,0},{2,3},{3,2},{4,5},{5,4},{6,7},{7,6},{8,9},{9,8},{10,11... | collective-permute-start | bytes 196616 | tf_op jit(solution)/shard_map/ppermute | solution.py:16
  19.3 6.0 %collective-permute-start.9 = (bf16[384,128]{1,0:T(8,128)(2,1)S(1)}, bf16[384,128]{1,0:T(8,128)(2,1)S(1)}, u32[]{:S(2)}, u32[]{:S(2)}) collective-permute-start(bf16[384,128]{1,0:T(8,128)(2,1)S(1)} %half_products.3), channel_id=1, source_target_pairs={{0,24},{8,16},{16,8},{24,0},{1,25},{9,17},{17,9},{25,1},{2,26},{10... | collective-permute-start | bytes 294920 | tf_op jit(solution)/shard_map/ppermute | solution.py:16
  22.1 5.1 %collective-permute-start.10 = (bf16[384,128]{1,0:T(8,128)(2,1)S(1)}, bf16[384,128]{1,0:T(8,128)(2,1)S(1)}, u32[]{:S(2)}, u32[]{:S(2)}) collective-permute-start(bf16[384,128]{1,0:T(8,128)(2,1)S(1)} %get-tuple-element.52), channel_id=1, source_target_pairs={{0,16},{8,24},{16,0},{24,8},{1,17},{9,25},{17,1},{25,9},{2,18},{10... | collective-permute-start | bytes 294920 | tf_op jit(solution)/shard_map/ppermute | solution.py:16
  22.7 4.6 %collective-permute-start.11 = (bf16[384,128]{1,0:T(8,128)(2,1)S(1)}, bf16[384,128]{1,0:T(8,128)(2,1)S(1)}, u32[]{:S(2)}, u32[]{:S(2)}) collective-permute-start(bf16[384,128]{1,0:T(8,128)(2,1)S(1)} %get-tuple-element.53), channel_id=1, source_target_pairs={{0,8},{8,0},{16,24},{24,16},{1,9},{9,1},{17,25},{25,17},{2,10},{10... | collective-permute-start | bytes 294920 | tf_op jit(solution)/shard_map/ppermute | solution.py:16
  27.9 5.7 %collective-permute-start.12 = (bf16[384,128]{1,0:T(8,128)(2,1)S(1)}, bf16[384,128]{1,0:T(8,128)(2,1)S(1)}, u32[]{:S(2)}, u32[]{:S(2)}) collective-permute-start(bf16[384,128]{1,0:T(8,128)(2,1)S(1)} %get-tuple-element.55), channel_id=1, source_target_pairs={{0,24},{8,16},{16,8},{24,0},{1,25},{9,17},{17,9},{25,1},{2,26},{10... | collective-permute-start | bytes 294920 | tf_op jit(solution)/shard_map/ppermute | solution.py:16
  30.4 5.2 %collective-permute-start.13 = (bf16[384,128]{1,0:T(8,128)(2,1)S(1)}, bf16[384,128]{1,0:T(8,128)(2,1)S(1)}, u32[]{:S(2)}, u32[]{:S(2)}) collective-permute-start(bf16[384,128]{1,0:T(8,128)(2,1)S(1)} %get-tuple-element.57), channel_id=1, source_target_pairs={{0,16},{8,24},{16,0},{24,8},{1,17},{9,25},{17,1},{25,9},{2,18},{10... | collective-permute-start | bytes 294920 | tf_op jit(solution)/shard_map/ppermute | solution.py:16
  31.2 4.6 %collective-permute-start.14 = (bf16[384,128]{1,0:T(8,128)(2,1)S(1)}, bf16[384,128]{1,0:T(8,128)(2,1)S(1)}, u32[]{:S(2)}, u32[]{:S(2)}) collective-permute-start(bf16[384,128]{1,0:T(8,128)(2,1)S(1)} %get-tuple-element.58), channel_id=1, source_target_pairs={{0,8},{8,0},{16,24},{24,16},{1,9},{9,1},{17,25},{25,17},{2,10},{10... | collective-permute-start | bytes 294920 | tf_op jit(solution)/shard_map/ppermute | solution.py:16

commit v7 on v6

--- a/solution.py
+++ b/solution.py
@@ -336,6 +336,7 @@
         group = half_products([packs[k] for k in ks], [blocks[k] for k in ks])
         if not halves:
             parts[0], group = lax.optimization_barrier((parts[0], group))
+            packs[order[2]], parts[0] = lax.optimization_barrier((packs[order[2]], parts[0]))
         halves += [exchange(half, "grid", grids, k) for k, half in zip(ks, group)]
     blocks[0] = swapped(parts[0])
     halves = list(half_products([packs[0]], [blocks[0]])) + halves

time: 38 us -> 38 us (level)
  no operation moved by 1% of the time
where the time goes in v7:
time: 38 us; the launch traced here: 37.7 us
  starting transfers between devices  17.8 us (47%)
  waiting for transfers between devices  9.16 us (24%)
  Pallas kernels  8.19 us (22%)
  local copies, waits for them, and re-layouts  2.22 us (6%)
    ppermute x15, starting transfers between devices, exchange(): return lax.ppermute(value, axis, [(i, i ^ step) for i in range(size)])  17.8 us
    ppermute x15, waiting for transfers between devices, exchange(): return lax.ppermute(value, axis, [(i, i ^ step) for i in range(size)])  9.16 us
    unnamed x14, local copies, waits for them, and re-layouts  1.98 us
    pallas_call x1, Pallas kernels, results(): pl.pallas_call(functools.partial(result_kernel, order, chunks), out_shape...  1.86 us
    pallas_call x1, Pallas kernels, prepare(): pl.pallas_call(functools.partial(prepare_kernel, tile, slots, count), out...  1.39 us
    pallas_call x1, Pallas kernels, pack(): pl.pallas_call(functools.partial(pack_kernel, tile, slots, count), out_sh...  1.06 us
    pallas_call x3, Pallas kernels, half_products(): pl.pallas_call(functools.partial(half_kernel, count), out_shape=[jax.Shap...  0.87 us
  transfers between devices with their start and end apart: 15, of which 10 were waited for; matrix products, arithmetic and copies ran while one was open for 1% of the time, Pallas kernels for 15%

profile of v7, /device:TPU:0, one launch (start us, length us, event | category | flops | bytes accessed | tf_op | source)
XLA Modules:
  0.0 37.7 jit_solution(17801585124894588164)
XLA Ops:
  0.0 3.0 %collective-permute-start = (bf16[1,16,512]{2,1,0:T(8,128)(2,1)}, bf16[1,16,512]{2,1,0:T(8,128)(2,1)S(1)}, u32[]{:S(2)}, u32[]{:S(2)}) collective-permute-start(bf16[1,16,512]{2,1,0:T(8,128)(2,1)} %bitcast.35), channel_id=1, source_target_pairs={{0,2},{1,3},{2,0},{3,1},{4,6},{5,7},{6,4},{7,5},{8,10},{9,11},{10,... | collective-permute-start | bytes 49160 | tf_op jit(solution)/shard_map/ppermute | solution.py:16
  3.0 0.8 %keep.1 = bf16[16,512]{1,0:T(8,128)(2,1)S(1)} custom-call(bf16[16,512]{1,0:T(8,128)(2,1)} %value.1), custom_call_target="tpu_custom_call" | custom-call | tf_op jit(solution)/shard_map/keep/pallas_call | solution.py:25
  3.8 1.2 %collective-permute-done = bf16[1,16,512]{2,1,0:T(8,128)(2,1)S(1)} collective-permute-done((bf16[1,16,512]{2,1,0:T(8,128)(2,1)}, bf16[1,16,512]{2,1,0:T(8,128)(2,1)S(1)}, u32[]{:S(2)}, u32[]{:S(2)}) %collective-permute-start) | collective-permute-done | bytes 16416 | tf_op jit(solution)/shard_map/ppermute | solution.py:16
  5.0 3.1 %collective-permute-start.1 = (bf16[2,16,512]{2,1,0:T(8,128)(2,1)S(1)}, bf16[2,16,512]{2,1,0:T(8,128)(2,1)S(1)}, u32[]{:S(2)}, u32[]{:S(2)}) collective-permute-start(bf16[2,16,512]{2,1,0:T(8,128)(2,1)S(1)} %maximum_select_fusion.5), channel_id=1, source_target_pairs={{0,4},{1,5},{2,6},{3,7},{4,0},{5,1},{6,2},{7,3},{8,12},{9,13},{10,... | collective-permute-start | bytes 98312 | tf_op jit(solution)/shard_map/ppermute | solution.py:16
  8.1 1.9 %collective-permute-done.1 = bf16[2,16,512]{2,1,0:T(8,128)(2,1)S(1)} collective-permute-done((bf16[2,16,512]{2,1,0:T(8,128)(2,1)S(1)}, bf16[2,16,512]{2,1,0:T(8,128)(2,1)S(1)}, u32[]{:S(2)}, u32[]{:S(2)}) %collective-permute-start.1) | collective-permute-done | bytes 32800 | tf_op jit(solution)/shard_map/ppermute | solution.py:16
  10.0 2.8 %collective-permute-start.3 = (bf16[4,16,512]{2,1,0:T(8,128)(2,1)S(1)}, bf16[4,16,512]{2,1,0:T(8,128)(2,1)S(1)}, u32[]{:S(2)}, u32[]{:S(2)}) collective-permute-start(bf16[4,16,512]{2,1,0:T(8,128)(2,1)S(1)} %maximum_select_fusion.4), channel_id=1, source_target_pairs={{0,24},{8,16},{16,8},{24,0},{1,25},{9,17},{17,9},{25,1},{2,26},{10... | collective-permute-start | bytes 196616 | tf_op jit(solution)/shard_map/ppermute | solution.py:16
  12.8 0.5 %collective-permute-start.6 = (bf16[4,16,512]{2,1,0:T(8,128)(2,1)S(1)}, bf16[4,16,512]{2,1,0:T(8,128)(2,1)S(1)}, u32[]{:S(2)}, u32[]{:S(2)}) collective-permute-start(bf16[4,16,512]{2,1,0:T(8,128)(2,1)S(1)} %maximum_select_fusion.4), channel_id=1, source_target_pairs={{0,8},{8,0},{16,24},{24,16},{1,9},{9,1},{17,25},{25,17},{2,10},{10... | collective-permute-start | bytes 196616 | tf_op jit(solution)/shard_map/ppermute | solution.py:16
  13.5 1.3 %copy-done = bf16[1,384,1536]{2,1,0:T(8,128)(2,1)S(1)} copy-done((bf16[1,384,1536]{2,1,0:T(8,128)(2,1)S(1)}, bf16[1,384,1536]{2,1,0:T(8,128)(2,1)}, u32[]{:S(2)}) %copy-start) | copy-done | bytes 1179672
  14.8 0.7 %copy-done.2 = s32[4,4]{1,0:T(4,128)S(1)} copy-done((s32[4,4]{1,0:T(4,128)S(1)}, s32[4,4]{1,0:T(4,128)}, u32[]{:S(2)}) %copy-start.2) | copy-done | bytes 88
  15.5 1.1 %pack.1 = (bf16[384,512]{1,0:T(8,128)(2,1)S(1)}, bf16[384,512]{1,0:T(8,128)(2,1)S(1)}, bf16[384,512]{1,0:T(8,128)(2,1)S(1)}, bf16[384,512]{1,0:T(8,128)(2,1)S(1)}) custom-call(s32[1]{0:T(128)} %bitcast.place, s32[4,4]{1,0:T(4,128)S(1)} %copy-done.2, bf16[384,1536]{1,0:T(8,128)(2,1)S(1)} %bitcast.17), custom_call_target="tpu_custom_call" | custom-call | bytes 3145728 | tf_op jit(solution)/shard_map/pack/pallas_call | solution.py:59
  16.6 0.5 %collective-permute-done.6 = bf16[4,16,512]{2,1,0:T(8,128)(2,1)S(1)} collective-permute-done((bf16[4,16,512]{2,1,0:T(8,128)(2,1)S(1)}, bf16[4,16,512]{2,1,0:T(8,128)(2,1)S(1)}, u32[]{:S(2)}, u32[]{:S(2)}) %collective-permute-start.6) | collective-permute-done | bytes 65568 | tf_op jit(solution)/shard_map/ppermute | solution.py:16
  17.1 0.5 %collective-permute-start.4 = (bf16[4,16,512]{2,1,0:T(8,128)(2,1)S(1)}, bf16[4,16,512]{2,1,0:T(8,128)(2,1)S(1)}, u32[]{:S(2)}, u32[]{:S(2)}) collective-permute-start(bf16[4,16,512]{2,1,0:T(8,128)(2,1)S(1)} %collective-permute-done.3), channel_id=1, source_target_pairs={{0,1},{1,0},{2,3},{3,2},{4,5},{5,4},{6,7},{7,6},{8,9},{9,8},{10,11... | collective-permute-start | bytes 196616 | tf_op jit(solution)/shard_map/ppermute | solution.py:16
  17.6 0.7 %collective-permute-done.7 = bf16[4,16,512]{2,1,0:T(8,128)(2,1)S(1)} collective-permute-done((bf16[4,16,512]{2,1,0:T(8,128)(2,1)S(1)}, bf16[4,16,512]{2,1,0:T(8,128)(2,1)S(1)}, u32[]{:S(2)}, u32[]{:S(2)}) %collective-permute-start.7) | collective-permute-done | bytes 65568 | tf_op jit(solution)/shard_map/ppermute | solution.py:16
  18.8 0.4 %collective-permute-start.5 = (bf16[4,16,512]{2,1,0:T(8,128)(2,1)S(1)}, bf16[4,16,512]{2,1,0:T(8,128)(2,1)S(1)}, u32[]{:S(2)}, u32[]{:S(2)}) collective-permute-start(bf16[4,16,512]{2,1,0:T(8,128)(2,1)S(1)} %maximum_select_fusion.4), channel_id=1, source_target_pairs={{0,1},{1,0},{2,3},{3,2},{4,5},{5,4},{6,7},{7,6},{8,9},{9,8},{10,11... | collective-permute-start | bytes 196616 | tf_op jit(solution)/shard_map/ppermute | solution.py:16
  19.3 2.5 %collective-permute-start.9 = (bf16[384,128]{1,0:T(8,128)(2,1)S(1)}, bf16[384,128]{1,0:T(8,128)(2,1)S(1)}, u32[]{:S(2)}, u32[]{:S(2)}) collective-permute-start(bf16[384,128]{1,0:T(8,128)(2,1)S(1)} %half_products.3), channel_id=1, source_target_pairs={{0,24},{8,16},{16,8},{24,0},{1,25},{9,17},{17,9},{25,1},{2,26},{10... | collective-permute-start | bytes 294920 | tf_op jit(solution)/shard_map/ppermute | solution.py:16
  21.7 0.4 half_products.5
  22.1 0.6 %collective-permute-start.10 = (bf16[384,128]{1,0:T(8,128)(2,1)S(1)}, bf16[384,128]{1,0:T(8,128)(2,1)S(1)}, u32[]{:S(2)}, u32[]{:S(2)}) collective-permute-start(bf16[384,128]{1,0:T(8,128)(2,1)S(1)} %get-tuple-element.56), channel_id=1, source_target_pairs={{0,16},{8,24},{16,0},{24,8},{1,17},{9,25},{17,1},{25,9},{2,18},{10... | collective-permute-start | bytes 294920 | tf_op jit(solution)/shard_map/ppermute | solution.py:16
  22.7 0.6 %collective-permute-start.11 = (bf16[384,128]{1,0:T(8,128)(2,1)S(1)}, bf16[384,128]{1,0:T(8,128)(2,1)S(1)}, u32[]{:S(2)}, u32[]{:S(2)}) collective-permute-start(bf16[384,128]{1,0:T(8,128)(2,1)S(1)} %get-tuple-element.57), channel_id=1, source_target_pairs={{0,8},{8,0},{16,24},{24,16},{1,9},{9,1},{17,25},{25,17},{2,10},{10... | collective-permute-start | bytes 294920 | tf_op jit(solution)/shard_map/ppermute | solution.py:16
  23.8 1.4 %prepare.1 = (bf16[512,1536]{1,0:T(8,128)(2,1)S(1)}, bf16[1536,512]{1,0:T(8,128)(2,1)S(1)}, f32[128,512]{1,0:T(8,128)S(1)}, f32[384,1536]{1,0:T(8,128)S(1)}) custom-call(s32[1]{0:T(128)} %bitcast.place, s32[4,4]{1,0:T(4,128)S(1)} %copy-done.3, s32[1,2]{1,0:T(1,128)S(1)} %copy-done.5, f32[300]{0:T(512)S(1)} %copy-done.4, bf16[128,512]{1,0:T(8,128)(2,1)S(1)} %bitcast.21, ...), custom_call_target="tpu_custom_call" | custom-call | bytes 6291456 | tf_op jit(solution)/shard_map/prepare/pallas_call | solution.py:127
  25.2 0.3 mixed.1
  25.6 1.6 %collective-permute-done.10.rest_0_ = bf16[384,128]{1,0:T(8,128)(2,1)S(1)} collective-permute-done((bf16[384,128]{1,0:T(8,128)(2,1)S(1)}, bf16[384,128]{1,0:T(8,128)(2,1)S(1)}, u32[]{:S(2)}, u32[]{:S(2)}) %collective-permute-start.10) | collective-permute-done | bytes 98336 | tf_op jit(solution)/shard_map/ppermute | solution.py:16
  27.3 0.6 %weighted.1 = (bf16[128,512]{1,0:T(8,128)(2,1)S(1)}, bf16[384,128]{1,0:T(8,128)(2,1)S(1)}) custom-call(bf16[1536,512]{1,0:T(8,128)(2,1)S(1)} %get-tuple-element.50.turned, f32[128,512]{1,0:T(8,128)S(1)} %get-tuple-element.51.scale, f32[128,512]{1,0:T(8,128)S(1)} %mixed.1, bf16[384,128]{1,0:T(8,128)(2,1)S(1)} %collective-permute-done.10.rest_0_, ...), custom_call_target="tpu_custom_call" | custom-call | tf_op jit(solution)/shard_map/weighted/pallas_call | solution.py:209
  27.9 2.2 %collective-permute-start.12 = (bf16[384,128]{1,0:T(8,128)(2,1)S(1)}, bf16[384,128]{1,0:T(8,128)(2,1)S(1)}, u32[]{:S(2)}, u32[]{:S(2)}) collective-permute-start(bf16[384,128]{1,0:T(8,128)(2,1)S(1)} %get-tuple-element.59), channel_id=1, source_target_pairs={{0,24},{8,16},{16,8},{24,0},{1,25},{9,17},{17,9},{25,1},{2,26},{10... | collective-permute-start | bytes 294920 | tf_op jit(solution)/shard_map/ppermute | solution.py:16
  30.0 0.4 ladders.3
  30.4 0.9 %collective-permute-start.13 = (bf16[384,128]{1,0:T(8,128)(2,1)S(1)}, bf16[384,128]{1,0:T(8,128)(2,1)S(1)}, u32[]{:S(2)}, u32[]{:S(2)}) collective-permute-start(bf16[384,128]{1,0:T(8,128)(2,1)S(1)} %get-tuple-element.61), channel_id=1, source_target_pairs={{0,16},{8,24},{16,0},{24,8},{1,17},{9,25},{17,1},{25,9},{2,18},{10... | collective-permute-start | bytes 294920 | tf_op jit(solution)/shard_map/ppermute | solution.py:16
  31.2 0.6 %collective-permute-start.14 = (bf16[384,128]{1,0:T(8,128)(2,1)S(1)}, bf16[384,128]{1,0:T(8,128)(2,1)S(1)}, u32[]{:S(2)}, u32[]{:S(2)}) collective-permute-start(bf16[384,128]{1,0:T(8,128)(2,1)S(1)} %get-tuple-element.62), channel_id=1, source_target_pairs={{0,8},{8,0},{16,24},{24,16},{1,9},{9,1},{17,25},{25,17},{2,10},{10... | collective-permute-start | bytes 294920 | tf_op jit(solution)/shard_map/ppermute | solution.py:16
  31.8 0.3 ladders.2.rest_0_
  32.1 1.4 %collective-permute-done.12.rest_1_ = bf16[384,128]{1,0:T(8,128)(2,1)S(1)} collective-permute-done((bf16[384,128]{1,0:T(8,128)(2,1)S(1)}, bf16[384,128]{1,0:T(8,128)(2,1)S(1)}, u32[]{:S(2)}, u32[]{:S(2)}) %collective-permute-start.12) | collective-permute-done | bytes 98336 | tf_op jit(solution)/shard_map/ppermute | solution.py:16
  33.5 0.8 %result_start.1.begun = f32[384,1536]{1,0:T(8,128)S(1)} custom-call(bf16[512,1536]{1,0:T(8,128)(2,1)S(1)} %get-tuple-element.49.dense, bf16[384,128]{1,0:T(8,128)(2,1)S(1)} %ladders.2.rest_0_, bf16[384,128]{1,0:T(8,128)(2,1)S(1)} %collective-permute-done.12.rest_1_), custom_call_target="tpu_custom_call" | custom-call | flops 301989888 | tf_op jit(solution)/shard_map/result_start/pallas_call | solution.py:250
  34.3 1.3 %collective-permute-done.13.rest_0_ = bf16[384,128]{1,0:T(8,128)(2,1)S(1)} collective-permute-done((bf16[384,128]{1,0:T(8,128)(2,1)S(1)}, bf16[384,128]{1,0:T(8,128)(2,1)S(1)}, u32[]{:S(2)}, u32[]{:S(2)}) %collective-permute-start.13) | collective-permute-done | bytes 98336 | tf_op jit(solution)/shard_map/ppermute | solution.py:16
  35.5 0.3 collective-permute-done.14.rest_1_
  35.9 1.9 %results.1 = f32[384,1536]{1,0:T(8,128)} custom-call(f32[384,1536]{1,0:T(8,128)S(1)} %result_start.1.begun, bf16[512,1536]{1,0:T(8,128)(2,1)S(1)} %get-tuple-element.49.dense, f32[384,1536]{1,0:T(8,128)S(1)} %get-tuple-element.60.inverse, bf16[384,128]{1,0:T(8,128)(2,1)S(1)} %collective-permute-done.13.rest_0_, ...), custom_call_target="tpu_custom_call" | custom-call | tf_op jit(solution)/shard_map/results/pallas_call | solution.py:284
  (36 shorter events, 1.3 us)
Async XLA Ops:
  0.0 5.0 %collective-permute-start = (bf16[1,16,512]{2,1,0:T(8,128)(2,1)}, bf16[1,16,512]{2,1,0:T(8,128)(2,1)S(1)}, u32[]{:S(2)}, u32[]{:S(2)}) collective-permute-start(bf16[1,16,512]{2,1,0:T(8,128)(2,1)} %bitcast.35), channel_id=1, source_target_pairs={{0,2},{1,3},{2,0},{3,1},{4,6},{5,7},{6,4},{7,5},{8,10},{9,11},{10,... | collective-permute-start | bytes 49160 | tf_op jit(solution)/shard_map/ppermute | solution.py:16
  5.0 5.0 %collective-permute-start.1 = (bf16[2,16,512]{2,1,0:T(8,128)(2,1)S(1)}, bf16[2,16,512]{2,1,0:T(8,128)(2,1)S(1)}, u32[]{:S(2)}, u32[]{:S(2)}) collective-permute-start(bf16[2,16,512]{2,1,0:T(8,128)(2,1)S(1)} %maximum_select_fusion.5), channel_id=1, source_target_pairs={{0,4},{1,5},{2,6},{3,7},{4,0},{5,1},{6,2},{7,3},{8,12},{9,13},{10,... | collective-permute-start | bytes 98312 | tf_op jit(solution)/shard_map/ppermute | solution.py:16
  10.0 6.6 %collective-permute-start.3 = (bf16[4,16,512]{2,1,0:T(8,128)(2,1)S(1)}, bf16[4,16,512]{2,1,0:T(8,128)(2,1)S(1)}, u32[]{:S(2)}, u32[]{:S(2)}) collective-permute-start(bf16[4,16,512]{2,1,0:T(8,128)(2,1)S(1)} %maximum_select_fusion.4), channel_id=1, source_target_pairs={{0,24},{8,16},{16,8},{24,0},{1,25},{9,17},{17,9},{25,1},{2,26},{10... | collective-permute-start | bytes 196616 | tf_op jit(solution)/shard_map/ppermute | solution.py:16
  12.8 4.3 %collective-permute-start.6 = (bf16[4,16,512]{2,1,0:T(8,128)(2,1)S(1)}, bf16[4,16,512]{2,1,0:T(8,128)(2,1)S(1)}, u32[]{:S(2)}, u32[]{:S(2)}) collective-permute-start(bf16[4,16,512]{2,1,0:T(8,128)(2,1)S(1)} %maximum_select_fusion.4), channel_id=1, source_target_pairs={{0,8},{8,0},{16,24},{24,16},{1,9},{9,1},{17,25},{25,17},{2,10},{10... | collective-permute-start | bytes 196616 | tf_op jit(solution)/shard_map/ppermute | solution.py:16
  13.3 4.3 %collective-permute-start.2 = (bf16[4,16,512]{2,1,0:T(8,128)(2,1)S(1)}, bf16[4,16,512]{2,1,0:T(8,128)(2,1)S(1)}, u32[]{:S(2)}, u32[]{:S(2)}) collective-permute-start(bf16[4,16,512]{2,1,0:T(8,128)(2,1)S(1)} %maximum_select_fusion.4), channel_id=1, source_target_pairs={{0,16},{8,24},{16,0},{24,8},{1,17},{9,25},{17,1},{25,9},{2,18},{10... | collective-permute-start | bytes 196616 | tf_op jit(solution)/shard_map/ppermute | solution.py:16
  13.5 1.3 %copy-start = (bf16[1,384,1536]{2,1,0:T(8,128)(2,1)S(1)}, bf16[1,384,1536]{2,1,0:T(8,128)(2,1)}, u32[]{:S(2)}) copy-start(bf16[1,384,1536]{2,1,0:T(8,128)(2,1)} %param.7) | copy-start | bytes 3538948
  14.8 0.7 %copy-start.2 = (s32[4,4]{1,0:T(4,128)S(1)}, s32[4,4]{1,0:T(4,128)}, u32[]{:S(2)}) copy-start(s32[4,4]{1,0:T(4,128)} %screen.3) | copy-start | bytes 196
  16.5 7.0 %copy-start.6 = (f32[1536]{0:T(1024)S(1)}, f32[1536]{0:T(1024)}, u32[]{:S(2)}) copy-start(f32[1536]{0:T(1024)} %param.12) | copy-start | bytes 18436
  16.5 7.2 %copy-start.1 = (bf16[512,128]{1,0:T(8,128)(2,1)S(1)}, bf16[512,128]{1,0:T(8,128)(2,1)}, u32[]{:S(2)}) copy-start(bf16[512,128]{1,0:T(8,128)(2,1)} %rest_4_.1) | copy-start | bytes 393220
  16.6 7.2 %copy-start.3 = (s32[4,4]{1,0:T(4,128)S(1)}, s32[4,4]{1,0:T(4,128)}, u32[]{:S(2)}) copy-start(s32[4,4]{1,0:T(4,128)} %screen.3) | copy-start | bytes 196
  16.6 7.2 %copy-start.4 = (f32[300]{0:T(512)S(1)}, f32[300]{0:T(512)}, u32[]{:S(2)}) copy-start(f32[300]{0:T(512)} %occ_energy.1) | copy-start | bytes 3604
  16.6 7.2 %copy-start.5 = (s32[1,2]{1,0:T(1,128)S(1)}, s32[1,2]{1,0:T(1,128)}, u32[]{:S(2)}) copy-start(s32[1,2]{1,0:T(1,128)} %pair_occ.1) | copy-start | bytes 28
  17.1 1.3 %collective-permute-start.7 = (bf16[4,16,512]{2,1,0:T(8,128)(2,1)S(1)}, bf16[4,16,512]{2,1,0:T(8,128)(2,1)S(1)}, u32[]{:S(2)}, u32[]{:S(2)}) collective-permute-start(bf16[4,16,512]{2,1,0:T(8,128)(2,1)S(1)} %collective-permute-done.6), channel_id=1, source_target_pairs={{0,1},{1,0},{2,3},{3,2},{4,5},{5,4},{6,7},{7,6},{8,9},{9,8},{10,11... | collective-permute-start | bytes 196616 | tf_op jit(solution)/shard_map/ppermute | solution.py:16
  17.1 1.4 %collective-permute-start.4 = (bf16[4,16,512]{2,1,0:T(8,128)(2,1)S(1)}, bf16[4,16,512]{2,1,0:T(8,128)(2,1)S(1)}, u32[]{:S(2)}, u32[]{:S(2)}) collective-permute-start(bf16[4,16,512]{2,1,0:T(8,128)(2,1)S(1)} %collective-permute-done.3), channel_id=1, source_target_pairs={{0,1},{1,0},{2,3},{3,2},{4,5},{5,4},{6,7},{7,6},{8,9},{9,8},{10,11... | collective-permute-start | bytes 196616 | tf_op jit(solution)/shard_map/ppermute | solution.py:16
  17.6 1.6 %collective-permute-start.8 = (bf16[4,16,512]{2,1,0:T(8,128)(2,1)S(1)}, bf16[4,16,512]{2,1,0:T(8,128)(2,1)S(1)}, u32[]{:S(2)}, u32[]{:S(2)}) collective-permute-start(bf16[4,16,512]{2,1,0:T(8,128)(2,1)S(1)} %collective-permute-done.2), channel_id=1, source_target_pairs={{0,1},{1,0},{2,3},{3,2},{4,5},{5,4},{6,7},{7,6},{8,9},{9,8},{10,11... | collective-permute-start | bytes 196616 | tf_op jit(solution)/shard_map/ppermute | solution.py:16
  18.8 4.5 %collective-permute-start.5 = (bf16[4,16,512]{2,1,0:T(8,128)(2,1)S(1)}, bf16[4,16,512]{2,1,0:T(8,128)(2,1)S(1)}, u32[]{:S(2)}, u32[]{:S(2)}) collective-permute-start(bf16[4,16,512]{2,1,0:T(8,128)(2,1)S(1)} %maximum_select_fusion.4), channel_id=1, source_target_pairs={{0,1},{1,0},{2,3},{3,2},{4,5},{5,4},{6,7},{7,6},{8,9},{9,8},{10,11... | collective-permute-start | bytes 196616 | tf_op jit(solution)/shard_map/ppermute | solution.py:16
  19.3 6.0 %collective-permute-start.9 = (bf16[384,128]{1,0:T(8,128)(2,1)S(1)}, bf16[384,128]{1,0:T(8,128)(2,1)S(1)}, u32[]{:S(2)}, u32[]{:S(2)}) collective-permute-start(bf16[384,128]{1,0:T(8,128)(2,1)S(1)} %half_products.3), channel_id=1, source_target_pairs={{0,24},{8,16},{16,8},{24,0},{1,25},{9,17},{17,9},{25,1},{2,26},{10... | collective-permute-start | bytes 294920 | tf_op jit(solution)/shard_map/ppermute | solution.py:16
  22.1 5.1 %collective-permute-start.10 = (bf16[384,128]{1,0:T(8,128)(2,1)S(1)}, bf16[384,128]{1,0:T(8,128)(2,1)S(1)}, u32[]{:S(2)}, u32[]{:S(2)}) collective-permute-start(bf16[384,128]{1,0:T(8,128)(2,1)S(1)} %get-tuple-element.56), channel_id=1, source_target_pairs={{0,16},{8,24},{16,0},{24,8},{1,17},{9,25},{17,1},{25,9},{2,18},{10... | collective-permute-start | bytes 294920 | tf_op jit(solution)/shard_map/ppermute | solution.py:16
  22.7 4.6 %collective-permute-start.11 = (bf16[384,128]{1,0:T(8,128)(2,1)S(1)}, bf16[384,128]{1,0:T(8,128)(2,1)S(1)}, u32[]{:S(2)}, u32[]{:S(2)}) collective-permute-start(bf16[384,128]{1,0:T(8,128)(2,1)S(1)} %get-tuple-element.57), channel_id=1, source_target_pairs={{0,8},{8,0},{16,24},{24,16},{1,9},{9,1},{17,25},{25,17},{2,10},{10... | collective-permute-start | bytes 294920 | tf_op jit(solution)/shard_map/ppermute | solution.py:16
  27.9 5.7 %collective-permute-start.12 = (bf16[384,128]{1,0:T(8,128)(2,1)S(1)}, bf16[384,128]{1,0:T(8,128)(2,1)S(1)}, u32[]{:S(2)}, u32[]{:S(2)}) collective-permute-start(bf16[384,128]{1,0:T(8,128)(2,1)S(1)} %get-tuple-element.59), channel_id=1, source_target_pairs={{0,24},{8,16},{16,8},{24,0},{1,25},{9,17},{17,9},{25,1},{2,26},{10... | collective-permute-start | bytes 294920 | tf_op jit(solution)/shard_map/ppermute | solution.py:16
  30.4 5.2 %collective-permute-start.13 = (bf16[384,128]{1,0:T(8,128)(2,1)S(1)}, bf16[384,128]{1,0:T(8,128)(2,1)S(1)}, u32[]{:S(2)}, u32[]{:S(2)}) collective-permute-start(bf16[384,128]{1,0:T(8,128)(2,1)S(1)} %get-tuple-element.61), channel_id=1, source_target_pairs={{0,16},{8,24},{16,0},{24,8},{1,17},{9,25},{17,1},{25,9},{2,18},{10... | collective-permute-start | bytes 294920 | tf_op jit(solution)/shard_map/ppermute | solution.py:16
  31.2 4.6 %collective-permute-start.14 = (bf16[384,128]{1,0:T(8,128)(2,1)S(1)}, bf16[384,128]{1,0:T(8,128)(2,1)S(1)}, u32[]{:S(2)}, u32[]{:S(2)}) collective-permute-start(bf16[384,128]{1,0:T(8,128)(2,1)S(1)} %get-tuple-element.62), channel_id=1, source_target_pairs={{0,8},{8,0},{16,24},{24,16},{1,9},{9,1},{17,25},{25,17},{2,10},{10... | collective-permute-start | bytes 294920 | tf_op jit(solution)/shard_map/ppermute | solution.py:16

commit v8 on v6

--- a/solution.py
+++ b/solution.py
@@ -279,7 +279,7 @@
 
 def results(order, begun, dense, inverse, pieces):
     rows, virtuals = begun.shape
-    chunks = 6 if virtuals % 768 == 0 else 1
+    chunks = 3 if virtuals % 768 == 0 else 1
     vmem = pl.BlockSpec(memory_space=pltpu.VMEM)
     return pl.pallas_call(
         functools.partial(result_kernel, order, chunks),

time: 38 us -> 37.9 us (level)
  no operation moved by 1% of the time
where the time goes in v8:
time: 37.9 us; the launch traced here: 37.7 us
  starting transfers between devices  17.8 us (47%)
  waiting for transfers between devices  9.16 us (24%)
  Pallas kernels  8.12 us (21%)
  local copies, waits for them, and re-layouts  2.22 us (6%)
    ppermute x15, starting transfers between devices, exchange(): return lax.ppermute(value, axis, [(i, i ^ step) for i in range(size)])  17.8 us
    ppermute x15, waiting for transfers between devices, exchange(): return lax.ppermute(value, axis, [(i, i ^ step) for i in range(size)])  9.16 us
    unnamed x14, local copies, waits for them, and re-layouts  1.98 us
    pallas_call x1, Pallas kernels, results(): pl.pallas_call(functools.partial(result_kernel, order, chunks), out_shape...  1.8 us
    pallas_call x1, Pallas kernels, prepare(): pl.pallas_call(functools.partial(prepare_kernel, tile, slots, count), out...  1.39 us
    pallas_call x1, Pallas kernels, pack(): pl.pallas_call(functools.partial(pack_kernel, tile, slots, count), out_sh...  1.06 us
    pallas_call x3, Pallas kernels, half_products(): pl.pallas_call(functools.partial(half_kernel, count), out_shape=[jax.Shap...  0.87 us
  transfers between devices with their start and end apart: 15, of which 10 were waited for; matrix products, arithmetic and copies ran while one was open for 1% of the time, Pallas kernels for 15%

profile of v8, /device:TPU:0, one launch (start us, length us, event | category | flops | bytes accessed | tf_op | source)
XLA Modules:
  0.0 37.7 jit_solution(11550084542833381164)
XLA Ops:
  0.0 3.0 %collective-permute-start = (bf16[1,16,512]{2,1,0:T(8,128)(2,1)}, bf16[1,16,512]{2,1,0:T(8,128)(2,1)S(1)}, u32[]{:S(2)}, u32[]{:S(2)}) collective-permute-start(bf16[1,16,512]{2,1,0:T(8,128)(2,1)} %bitcast.35), channel_id=1, source_target_pairs={{0,2},{1,3},{2,0},{3,1},{4,6},{5,7},{6,4},{7,5},{8,10},{9,11},{10,... | collective-permute-start | bytes 49160 | tf_op jit(solution)/shard_map/ppermute | solution.py:16
  3.0 0.8 %keep.1 = bf16[16,512]{1,0:T(8,128)(2,1)S(1)} custom-call(bf16[16,512]{1,0:T(8,128)(2,1)} %value.1), custom_call_target="tpu_custom_call" | custom-call | tf_op jit(solution)/shard_map/keep/pallas_call | solution.py:25
  3.8 1.2 %collective-permute-done = bf16[1,16,512]{2,1,0:T(8,128)(2,1)S(1)} collective-permute-done((bf16[1,16,512]{2,1,0:T(8,128)(2,1)}, bf16[1,16,512]{2,1,0:T(8,128)(2,1)S(1)}, u32[]{:S(2)}, u32[]{:S(2)}) %collective-permute-start) | collective-permute-done | bytes 16416 | tf_op jit(solution)/shard_map/ppermute | solution.py:16
  5.0 3.1 %collective-permute-start.1 = (bf16[2,16,512]{2,1,0:T(8,128)(2,1)S(1)}, bf16[2,16,512]{2,1,0:T(8,128)(2,1)S(1)}, u32[]{:S(2)}, u32[]{:S(2)}) collective-permute-start(bf16[2,16,512]{2,1,0:T(8,128)(2,1)S(1)} %maximum_select_fusion.5), channel_id=1, source_target_pairs={{0,4},{1,5},{2,6},{3,7},{4,0},{5,1},{6,2},{7,3},{8,12},{9,13},{10,... | collective-permute-start | bytes 98312 | tf_op jit(solution)/shard_map/ppermute | solution.py:16
  8.1 1.9 %collective-permute-done.1 = bf16[2,16,512]{2,1,0:T(8,128)(2,1)S(1)} collective-permute-done((bf16[2,16,512]{2,1,0:T(8,128)(2,1)S(1)}, bf16[2,16,512]{2,1,0:T(8,128)(2,1)S(1)}, u32[]{:S(2)}, u32[]{:S(2)}) %collective-permute-start.1) | collective-permute-done | bytes 32800 | tf_op jit(solution)/shard_map/ppermute | solution.py:16
  10.0 2.8 %collective-permute-start.2 = (bf16[4,16,512]{2,1,0:T(8,128)(2,1)S(1)}, bf16[4,16,512]{2,1,0:T(8,128)(2,1)S(1)}, u32[]{:S(2)}, u32[]{:S(2)}) collective-permute-start(bf16[4,16,512]{2,1,0:T(8,128)(2,1)S(1)} %maximum_select_fusion.4), channel_id=1, source_target_pairs={{0,24},{8,16},{16,8},{24,0},{1,25},{9,17},{17,9},{25,1},{2,26},{10... | collective-permute-start | bytes 196616 | tf_op jit(solution)/shard_map/ppermute | solution.py:16
  12.8 0.5 %collective-permute-start.5 = (bf16[4,16,512]{2,1,0:T(8,128)(2,1)S(1)}, bf16[4,16,512]{2,1,0:T(8,128)(2,1)S(1)}, u32[]{:S(2)}, u32[]{:S(2)}) collective-permute-start(bf16[4,16,512]{2,1,0:T(8,128)(2,1)S(1)} %maximum_select_fusion.4), channel_id=1, source_target_pairs={{0,8},{8,0},{16,24},{24,16},{1,9},{9,1},{17,25},{25,17},{2,10},{10... | collective-permute-start | bytes 196616 | tf_op jit(solution)/shard_map/ppermute | solution.py:16
  13.5 1.3 %copy-done = bf16[1,384,1536]{2,1,0:T(8,128)(2,1)S(1)} copy-done((bf16[1,384,1536]{2,1,0:T(8,128)(2,1)S(1)}, bf16[1,384,1536]{2,1,0:T(8,128)(2,1)}, u32[]{:S(2)}) %copy-start) | copy-done | bytes 1179672
  14.8 0.7 %copy-done.2 = s32[4,4]{1,0:T(4,128)S(1)} copy-done((s32[4,4]{1,0:T(4,128)S(1)}, s32[4,4]{1,0:T(4,128)}, u32[]{:S(2)}) %copy-start.2) | copy-done | bytes 88
  15.5 1.1 %pack.1 = (bf16[384,512]{1,0:T(8,128)(2,1)S(1)}, bf16[384,512]{1,0:T(8,128)(2,1)S(1)}, bf16[384,512]{1,0:T(8,128)(2,1)S(1)}, bf16[384,512]{1,0:T(8,128)(2,1)S(1)}) custom-call(s32[1]{0:T(128)} %bitcast.place, s32[4,4]{1,0:T(4,128)S(1)} %copy-done.2, bf16[384,1536]{1,0:T(8,128)(2,1)S(1)} %bitcast.17), custom_call_target="tpu_custom_call" | custom-call | bytes 3145728 | tf_op jit(solution)/shard_map/pack/pallas_call | solution.py:59
  16.6 0.5 %collective-permute-done.5 = bf16[4,16,512]{2,1,0:T(8,128)(2,1)S(1)} collective-permute-done((bf16[4,16,512]{2,1,0:T(8,128)(2,1)S(1)}, bf16[4,16,512]{2,1,0:T(8,128)(2,1)S(1)}, u32[]{:S(2)}, u32[]{:S(2)}) %collective-permute-start.5) | collective-permute-done | bytes 65568 | tf_op jit(solution)/shard_map/ppermute | solution.py:16
  17.1 0.5 %collective-permute-start.3 = (bf16[4,16,512]{2,1,0:T(8,128)(2,1)S(1)}, bf16[4,16,512]{2,1,0:T(8,128)(2,1)S(1)}, u32[]{:S(2)}, u32[]{:S(2)}) collective-permute-start(bf16[4,16,512]{2,1,0:T(8,128)(2,1)S(1)} %collective-permute-done.2), channel_id=1, source_target_pairs={{0,1},{1,0},{2,3},{3,2},{4,5},{5,4},{6,7},{7,6},{8,9},{9,8},{10,11... | collective-permute-start | bytes 196616 | tf_op jit(solution)/shard_map/ppermute | solution.py:16
  17.6 0.7 %collective-permute-done.6 = bf16[4,16,512]{2,1,0:T(8,128)(2,1)S(1)} collective-permute-done((bf16[4,16,512]{2,1,0:T(8,128)(2,1)S(1)}, bf16[4,16,512]{2,1,0:T(8,128)(2,1)S(1)}, u32[]{:S(2)}, u32[]{:S(2)}) %collective-permute-start.6) | collective-permute-done | bytes 65568 | tf_op jit(solution)/shard_map/ppermute | solution.py:16
  18.8 0.4 %collective-permute-start.4 = (bf16[4,16,512]{2,1,0:T(8,128)(2,1)S(1)}, bf16[4,16,512]{2,1,0:T(8,128)(2,1)S(1)}, u32[]{:S(2)}, u32[]{:S(2)}) collective-permute-start(bf16[4,16,512]{2,1,0:T(8,128)(2,1)S(1)} %maximum_select_fusion.4), channel_id=1, source_target_pairs={{0,1},{1,0},{2,3},{3,2},{4,5},{5,4},{6,7},{7,6},{8,9},{9,8},{10,11... | collective-permute-start | bytes 196616 | tf_op jit(solution)/shard_map/ppermute | solution.py:16
  19.3 2.5 %collective-permute-start.9 = (bf16[384,128]{1,0:T(8,128)(2,1)S(1)}, bf16[384,128]{1,0:T(8,128)(2,1)S(1)}, u32[]{:S(2)}, u32[]{:S(2)}) collective-permute-start(bf16[384,128]{1,0:T(8,128)(2,1)S(1)} %half_products.3), channel_id=1, source_target_pairs={{0,24},{8,16},{16,8},{24,0},{1,25},{9,17},{17,9},{25,1},{2,26},{10... | collective-permute-start | bytes 294920 | tf_op jit(solution)/shard_map/ppermute | solution.py:16
  21.7 0.4 half_products.5
  22.1 0.6 %collective-permute-start.10 = (bf16[384,128]{1,0:T(8,128)(2,1)S(1)}, bf16[384,128]{1,0:T(8,128)(2,1)S(1)}, u32[]{:S(2)}, u32[]{:S(2)}) collective-permute-start(bf16[384,128]{1,0:T(8,128)(2,1)S(1)} %get-tuple-element.52), channel_id=1, source_target_pairs={{0,16},{8,24},{16,0},{24,8},{1,17},{9,25},{17,1},{25,9},{2,18},{10... | collective-permute-start | bytes 294920 | tf_op jit(solution)/shard_map/ppermute | solution.py:16
  22.7 0.6 %collective-permute-start.11 = (bf16[384,128]{1,0:T(8,128)(2,1)S(1)}, bf16[384,128]{1,0:T(8,128)(2,1)S(1)}, u32[]{:S(2)}, u32[]{:S(2)}) collective-permute-start(bf16[384,128]{1,0:T(8,128)(2,1)S(1)} %get-tuple-element.53), channel_id=1, source_target_pairs={{0,8},{8,0},{16,24},{24,16},{1,9},{9,1},{17,25},{25,17},{2,10},{10... | collective-permute-start | bytes 294920 | tf_op jit(solution)/shard_map/ppermute | solution.py:16
  23.8 1.4 %prepare.1 = (bf16[512,1536]{1,0:T(8,128)(2,1)S(1)}, bf16[1536,512]{1,0:T(8,128)(2,1)S(1)}, f32[128,512]{1,0:T(8,128)S(1)}, f32[384,1536]{1,0:T(8,128)S(1)}) custom-call(s32[1]{0:T(128)} %bitcast.place, s32[4,4]{1,0:T(4,128)S(1)} %copy-done.3, s32[1,2]{1,0:T(1,128)S(1)} %copy-done.5, f32[300]{0:T(512)S(1)} %copy-done.4, bf16[128,512]{1,0:T(8,128)(2,1)S(1)} %bitcast.21, ...), custom_call_target="tpu_custom_call" | custom-call | bytes 6291456 | tf_op jit(solution)/shard_map/prepare/pallas_call | solution.py:127
  25.2 0.3 mixed.1
  25.6 1.6 %collective-permute-done.10.rest_0_ = bf16[384,128]{1,0:T(8,128)(2,1)S(1)} collective-permute-done((bf16[384,128]{1,0:T(8,128)(2,1)S(1)}, bf16[384,128]{1,0:T(8,128)(2,1)S(1)}, u32[]{:S(2)}, u32[]{:S(2)}) %collective-permute-start.10) | collective-permute-done | bytes 98336 | tf_op jit(solution)/shard_map/ppermute | solution.py:16
  27.3 0.6 %weighted.1 = (bf16[128,512]{1,0:T(8,128)(2,1)S(1)}, bf16[384,128]{1,0:T(8,128)(2,1)S(1)}) custom-call(bf16[1536,512]{1,0:T(8,128)(2,1)S(1)} %get-tuple-element.46.turned, f32[128,512]{1,0:T(8,128)S(1)} %get-tuple-element.47.scale, f32[128,512]{1,0:T(8,128)S(1)} %mixed.1, bf16[384,128]{1,0:T(8,128)(2,1)S(1)} %collective-permute-done.10.rest_0_, ...), custom_call_target="tpu_custom_call" | custom-call | tf_op jit(solution)/shard_map/weighted/pallas_call | solution.py:209
  27.9 2.2 %collective-permute-start.12 = (bf16[384,128]{1,0:T(8,128)(2,1)S(1)}, bf16[384,128]{1,0:T(8,128)(2,1)S(1)}, u32[]{:S(2)}, u32[]{:S(2)}) collective-permute-start(bf16[384,128]{1,0:T(8,128)(2,1)S(1)} %get-tuple-element.55), channel_id=1, source_target_pairs={{0,24},{8,16},{16,8},{24,0},{1,25},{9,17},{17,9},{25,1},{2,26},{10... | collective-permute-start | bytes 294920 | tf_op jit(solution)/shard_map/ppermute | solution.py:16
  30.0 0.4 ladders.3
  30.4 0.9 %collective-permute-start.13 = (bf16[384,128]{1,0:T(8,128)(2,1)S(1)}, bf16[384,128]{1,0:T(8,128)(2,1)S(1)}, u32[]{:S(2)}, u32[]{:S(2)}) collective-permute-start(bf16[384,128]{1,0:T(8,128)(2,1)S(1)} %get-tuple-element.57), channel_id=1, source_target_pairs={{0,16},{8,24},{16,0},{24,8},{1,17},{9,25},{17,1},{25,9},{2,18},{10... | collective-permute-start | bytes 294920 | tf_op jit(solution)/shard_map/ppermute | solution.py:16
  31.2 0.6 %collective-permute-start.14 = (bf16[384,128]{1,0:T(8,128)(2,1)S(1)}, bf16[384,128]{1,0:T(8,128)(2,1)S(1)}, u32[]{:S(2)}, u32[]{:S(2)}) collective-permute-start(bf16[384,128]{1,0:T(8,128)(2,1)S(1)} %get-tuple-element.58), channel_id=1, source_target_pairs={{0,8},{8,0},{16,24},{24,16},{1,9},{9,1},{17,25},{25,17},{2,10},{10... | collective-permute-start | bytes 294920 | tf_op jit(solution)/shard_map/ppermute | solution.py:16
  31.8 0.3 ladders.2.rest_0_
  32.1 1.4 %collective-permute-done.12.rest_1_ = bf16[384,128]{1,0:T(8,128)(2,1)S(1)} collective-permute-done((bf16[384,128]{1,0:T(8,128)(2,1)S(1)}, bf16[384,128]{1,0:T(8,128)(2,1)S(1)}, u32[]{:S(2)}, u32[]{:S(2)}) %collective-permute-start.12) | collective-permute-done | bytes 98336 | tf_op jit(solution)/shard_map/ppermute | solution.py:16
  33.5 0.8 %result_start.1.begun = f32[384,1536]{1,0:T(8,128)S(1)} custom-call(bf16[512,1536]{1,0:T(8,128)(2,1)S(1)} %get-tuple-element.45.dense, bf16[384,128]{1,0:T(8,128)(2,1)S(1)} %ladders.2.rest_0_, bf16[384,128]{1,0:T(8,128)(2,1)S(1)} %collective-permute-done.12.rest_1_), custom_call_target="tpu_custom_call" | custom-call | flops 301989888 | tf_op jit(solution)/shard_map/result_start/pallas_call | solution.py:250
  34.3 1.3 %collective-permute-done.13.rest_0_ = bf16[384,128]{1,0:T(8,128)(2,1)S(1)} collective-permute-done((bf16[384,128]{1,0:T(8,128)(2,1)S(1)}, bf16[384,128]{1,0:T(8,128)(2,1)S(1)}, u32[]{:S(2)}, u32[]{:S(2)}) %collective-permute-start.13) | collective-permute-done | bytes 98336 | tf_op jit(solution)/shard_map/ppermute | solution.py:16
  35.5 0.3 collective-permute-done.14.rest_1_
  35.9 1.8 %results.1 = f32[384,1536]{1,0:T(8,128)} custom-call(f32[384,1536]{1,0:T(8,128)S(1)} %result_start.1.begun, bf16[512,1536]{1,0:T(8,128)(2,1)S(1)} %get-tuple-element.45.dense, f32[384,1536]{1,0:T(8,128)S(1)} %get-tuple-element.56.inverse, bf16[384,128]{1,0:T(8,128)(2,1)S(1)} %collective-permute-done.13.rest_0_, ...), custom_call_target="tpu_custom_call" | custom-call | tf_op jit(solution)/shard_map/results/pallas_call | solution.py:284
  (36 shorter events, 1.3 us)
Async XLA Ops:
  0.0 5.0 %collective-permute-start = (bf16[1,16,512]{2,1,0:T(8,128)(2,1)}, bf16[1,16,512]{2,1,0:T(8,128)(2,1)S(1)}, u32[]{:S(2)}, u32[]{:S(2)}) collective-permute-start(bf16[1,16,512]{2,1,0:T(8,128)(2,1)} %bitcast.35), channel_id=1, source_target_pairs={{0,2},{1,3},{2,0},{3,1},{4,6},{5,7},{6,4},{7,5},{8,10},{9,11},{10,... | collective-permute-start | bytes 49160 | tf_op jit(solution)/shard_map/ppermute | solution.py:16
  5.0 5.0 %collective-permute-start.1 = (bf16[2,16,512]{2,1,0:T(8,128)(2,1)S(1)}, bf16[2,16,512]{2,1,0:T(8,128)(2,1)S(1)}, u32[]{:S(2)}, u32[]{:S(2)}) collective-permute-start(bf16[2,16,512]{2,1,0:T(8,128)(2,1)S(1)} %maximum_select_fusion.5), channel_id=1, source_target_pairs={{0,4},{1,5},{2,6},{3,7},{4,0},{5,1},{6,2},{7,3},{8,12},{9,13},{10,... | collective-permute-start | bytes 98312 | tf_op jit(solution)/shard_map/ppermute | solution.py:16
  10.0 6.6 %collective-permute-start.2 = (bf16[4,16,512]{2,1,0:T(8,128)(2,1)S(1)}, bf16[4,16,512]{2,1,0:T(8,128)(2,1)S(1)}, u32[]{:S(2)}, u32[]{:S(2)}) collective-permute-start(bf16[4,16,512]{2,1,0:T(8,128)(2,1)S(1)} %maximum_select_fusion.4), channel_id=1, source_target_pairs={{0,24},{8,16},{16,8},{24,0},{1,25},{9,17},{17,9},{25,1},{2,26},{10... | collective-permute-start | bytes 196616 | tf_op jit(solution)/shard_map/ppermute | solution.py:16
  12.8 4.3 %collective-permute-start.5 = (bf16[4,16,512]{2,1,0:T(8,128)(2,1)S(1)}, bf16[4,16,512]{2,1,0:T(8,128)(2,1)S(1)}, u32[]{:S(2)}, u32[]{:S(2)}) collective-permute-start(bf16[4,16,512]{2,1,0:T(8,128)(2,1)S(1)} %maximum_select_fusion.4), channel_id=1, source_target_pairs={{0,8},{8,0},{16,24},{24,16},{1,9},{9,1},{17,25},{25,17},{2,10},{10... | collective-permute-start | bytes 196616 | tf_op jit(solution)/shard_map/ppermute | solution.py:16
  13.3 4.3 %collective-permute-start.7 = (bf16[4,16,512]{2,1,0:T(8,128)(2,1)S(1)}, bf16[4,16,512]{2,1,0:T(8,128)(2,1)S(1)}, u32[]{:S(2)}, u32[]{:S(2)}) collective-permute-start(bf16[4,16,512]{2,1,0:T(8,128)(2,1)S(1)} %maximum_select_fusion.4), channel_id=1, source_target_pairs={{0,16},{8,24},{16,0},{24,8},{1,17},{9,25},{17,1},{25,9},{2,18},{10... | collective-permute-start | bytes 196616 | tf_op jit(solution)/shard_map/ppermute | solution.py:16
  13.5 1.3 %copy-start = (bf16[1,384,1536]{2,1,0:T(8,128)(2,1)S(1)}, bf16[1,384,1536]{2,1,0:T(8,128)(2,1)}, u32[]{:S(2)}) copy-start(bf16[1,384,1536]{2,1,0:T(8,128)(2,1)} %param.7) | copy-start | bytes 3538948
  14.8 0.7 %copy-start.2 = (s32[4,4]{1,0:T(4,128)S(1)}, s32[4,4]{1,0:T(4,128)}, u32[]{:S(2)}) copy-start(s32[4,4]{1,0:T(4,128)} %screen.3) | copy-start | bytes 196
  16.5 7.0 %copy-start.6 = (f32[1536]{0:T(1024)S(1)}, f32[1536]{0:T(1024)}, u32[]{:S(2)}) copy-start(f32[1536]{0:T(1024)} %param.12) | copy-start | bytes 18436
  16.5 7.2 %copy-start.1 = (bf16[512,128]{1,0:T(8,128)(2,1)S(1)}, bf16[512,128]{1,0:T(8,128)(2,1)}, u32[]{:S(2)}) copy-start(bf16[512,128]{1,0:T(8,128)(2,1)} %rest_4_.1) | copy-start | bytes 393220
  16.6 7.2 %copy-start.3 = (s32[4,4]{1,0:T(4,128)S(1)}, s32[4,4]{1,0:T(4,128)}, u32[]{:S(2)}) copy-start(s32[4,4]{1,0:T(4,128)} %screen.3) | copy-start | bytes 196
  16.6 7.2 %copy-start.4 = (f32[300]{0:T(512)S(1)}, f32[300]{0:T(512)}, u32[]{:S(2)}) copy-start(f32[300]{0:T(512)} %occ_energy.1) | copy-start | bytes 3604
  16.6 7.2 %copy-start.5 = (s32[1,2]{1,0:T(1,128)S(1)}, s32[1,2]{1,0:T(1,128)}, u32[]{:S(2)}) copy-start(s32[1,2]{1,0:T(1,128)} %pair_occ.1) | copy-start | bytes 28
  17.1 1.3 %collective-permute-start.6 = (bf16[4,16,512]{2,1,0:T(8,128)(2,1)S(1)}, bf16[4,16,512]{2,1,0:T(8,128)(2,1)S(1)}, u32[]{:S(2)}, u32[]{:S(2)}) collective-permute-start(bf16[4,16,512]{2,1,0:T(8,128)(2,1)S(1)} %collective-permute-done.5), channel_id=1, source_target_pairs={{0,1},{1,0},{2,3},{3,2},{4,5},{5,4},{6,7},{7,6},{8,9},{9,8},{10,11... | collective-permute-start | bytes 196616 | tf_op jit(solution)/shard_map/ppermute | solution.py:16
  17.1 1.4 %collective-permute-start.3 = (bf16[4,16,512]{2,1,0:T(8,128)(2,1)S(1)}, bf16[4,16,512]{2,1,0:T(8,128)(2,1)S(1)}, u32[]{:S(2)}, u32[]{:S(2)}) collective-permute-start(bf16[4,16,512]{2,1,0:T(8,128)(2,1)S(1)} %collective-permute-done.2), channel_id=1, source_target_pairs={{0,1},{1,0},{2,3},{3,2},{4,5},{5,4},{6,7},{7,6},{8,9},{9,8},{10,11... | collective-permute-start | bytes 196616 | tf_op jit(solution)/shard_map/ppermute | solution.py:16
  17.6 1.6 %collective-permute-start.8 = (bf16[4,16,512]{2,1,0:T(8,128)(2,1)S(1)}, bf16[4,16,512]{2,1,0:T(8,128)(2,1)S(1)}, u32[]{:S(2)}, u32[]{:S(2)}) collective-permute-start(bf16[4,16,512]{2,1,0:T(8,128)(2,1)S(1)} %collective-permute-done.7), channel_id=1, source_target_pairs={{0,1},{1,0},{2,3},{3,2},{4,5},{5,4},{6,7},{7,6},{8,9},{9,8},{10,11... | collective-permute-start | bytes 196616 | tf_op jit(solution)/shard_map/ppermute | solution.py:16
  18.8 4.5 %collective-permute-start.4 = (bf16[4,16,512]{2,1,0:T(8,128)(2,1)S(1)}, bf16[4,16,512]{2,1,0:T(8,128)(2,1)S(1)}, u32[]{:S(2)}, u32[]{:S(2)}) collective-permute-start(bf16[4,16,512]{2,1,0:T(8,128)(2,1)S(1)} %maximum_select_fusion.4), channel_id=1, source_target_pairs={{0,1},{1,0},{2,3},{3,2},{4,5},{5,4},{6,7},{7,6},{8,9},{9,8},{10,11... | collective-permute-start | bytes 196616 | tf_op jit(solution)/shard_map/ppermute | solution.py:16
  19.3 6.0 %collective-permute-start.9 = (bf16[384,128]{1,0:T(8,128)(2,1)S(1)}, bf16[384,128]{1,0:T(8,128)(2,1)S(1)}, u32[]{:S(2)}, u32[]{:S(2)}) collective-permute-start(bf16[384,128]{1,0:T(8,128)(2,1)S(1)} %half_products.3), channel_id=1, source_target_pairs={{0,24},{8,16},{16,8},{24,0},{1,25},{9,17},{17,9},{25,1},{2,26},{10... | collective-permute-start | bytes 294920 | tf_op jit(solution)/shard_map/ppermute | solution.py:16
  22.1 5.1 %collective-permute-start.10 = (bf16[384,128]{1,0:T(8,128)(2,1)S(1)}, bf16[384,128]{1,0:T(8,128)(2,1)S(1)}, u32[]{:S(2)}, u32[]{:S(2)}) collective-permute-start(bf16[384,128]{1,0:T(8,128)(2,1)S(1)} %get-tuple-element.52), channel_id=1, source_target_pairs={{0,16},{8,24},{16,0},{24,8},{1,17},{9,25},{17,1},{25,9},{2,18},{10... | collective-permute-start | bytes 294920 | tf_op jit(solution)/shard_map/ppermute | solution.py:16
  22.7 4.6 %collective-permute-start.11 = (bf16[384,128]{1,0:T(8,128)(2,1)S(1)}, bf16[384,128]{1,0:T(8,128)(2,1)S(1)}, u32[]{:S(2)}, u32[]{:S(2)}) collective-permute-start(bf16[384,128]{1,0:T(8,128)(2,1)S(1)} %get-tuple-element.53), channel_id=1, source_target_pairs={{0,8},{8,0},{16,24},{24,16},{1,9},{9,1},{17,25},{25,17},{2,10},{10... | collective-permute-start | bytes 294920 | tf_op jit(solution)/shard_map/ppermute | solution.py:16
  27.9 5.7 %collective-permute-start.12 = (bf16[384,128]{1,0:T(8,128)(2,1)S(1)}, bf16[384,128]{1,0:T(8,128)(2,1)S(1)}, u32[]{:S(2)}, u32[]{:S(2)}) collective-permute-start(bf16[384,128]{1,0:T(8,128)(2,1)S(1)} %get-tuple-element.55), channel_id=1, source_target_pairs={{0,24},{8,16},{16,8},{24,0},{1,25},{9,17},{17,9},{25,1},{2,26},{10... | collective-permute-start | bytes 294920 | tf_op jit(solution)/shard_map/ppermute | solution.py:16
  30.4 5.2 %collective-permute-start.13 = (bf16[384,128]{1,0:T(8,128)(2,1)S(1)}, bf16[384,128]{1,0:T(8,128)(2,1)S(1)}, u32[]{:S(2)}, u32[]{:S(2)}) collective-permute-start(bf16[384,128]{1,0:T(8,128)(2,1)S(1)} %get-tuple-element.57), channel_id=1, source_target_pairs={{0,16},{8,24},{16,0},{24,8},{1,17},{9,25},{17,1},{25,9},{2,18},{10... | collective-permute-start | bytes 294920 | tf_op jit(solution)/shard_map/ppermute | solution.py:16
  31.2 4.6 %collective-permute-start.14 = (bf16[384,128]{1,0:T(8,128)(2,1)S(1)}, bf16[384,128]{1,0:T(8,128)(2,1)S(1)}, u32[]{:S(2)}, u32[]{:S(2)}) collective-permute-start(bf16[384,128]{1,0:T(8,128)(2,1)S(1)} %get-tuple-element.58), channel_id=1, source_target_pairs={{0,8},{8,0},{16,24},{24,16},{1,9},{9,1},{17,25},{25,17},{2,10},{10... | collective-permute-start | bytes 294920 | tf_op jit(solution)/shard_map/ppermute | solution.py:16

commit v9 on v8

--- a/solution.py
+++ b/solution.py
@@ -73,8 +73,8 @@
 def half_kernel(count, *refs):
     for k in range(count):
         refs[2 * count + k][...] = lax.dot_general(
+            refs[count + k][...],
             refs[k][...],
-            refs[count + k][...],
             (((1,), (1,)), ((), ())),
             preferred_element_type=F32,
         ).astype(BF16)
@@ -87,7 +87,7 @@
     vmem = pl.BlockSpec(memory_space=pltpu.VMEM)
     return pl.pallas_call(
         functools.partial(half_kernel, count),
-        out_shape=[jax.ShapeDtypeStruct((rows, width), BF16)] * count,
+        out_shape=[jax.ShapeDtypeStruct((width, rows), BF16)] * count,
         in_specs=[vmem] * (2 * count),
         out_specs=[vmem] * count,
         cost_estimate=pl.CostEstimate(
@@ -143,12 +143,12 @@
 
 
 def mixed_part(half, factor):
-    return lax.dot_general(half, factor, (((0,), (0,)), ((), ())), preferred_element_type=F32)
+    return jnp.dot(half, factor, preferred_element_type=F32)
 
 
 def mixed_kernel(order, place, turned, *rest):
     halves, out = rest[:-1], rest[-1]
-    rows = halves[0].shape[0]
+    rows = halves[0].shape[1]
     total = None
     for k, half in zip(order, halves):
         start = pl.multiple_of((place[0] ^ k) * rows, rows)
@@ -159,7 +159,7 @@
 
 def mixed_sum(order, place, turned, halves):
     known = len(halves)
-    width, points = halves[0].shape[1], turned.shape[1]
+    width, points = halves[0].shape[0], turned.shape[1]
     vmem = pl.BlockSpec(memory_space=pltpu.VMEM)
     return pl.pallas_call(
         functools.partial(mixed_kernel, order),
@@ -187,7 +187,7 @@
 
 def weighted_kernel(first, late, turned, scale, mixed, *rest):
     halves, (weighted, out) = rest[: len(late)], rest[len(late) :]
-    rows = halves[0].shape[0]
+    rows = halves[0].shape[1]
     total = mixed[...]
     for k, half in zip(late, halves):
         total = total + mixed_part(half[...], own_rows(turned, k, rows))
@@ -201,7 +201,7 @@
 
 
 def ladders(order, late, turned, scale, mixed, halves):
-    rows, width = halves[0].shape
+    width, rows = halves[0].shape
     vmem = pl.BlockSpec(memory_space=pltpu.VMEM)
     piece = jax.ShapeDtypeStruct((rows, width), BF16)
     limit = pltpu.CompilerParams(vmem_limit_bytes=VMEM_LIMIT)

time: 37.9 us -> 37.9 us (level)
  no operation moved by 1% of the time
where the time goes in v9:
time: 37.9 us; the launch traced here: 37.7 us
  starting transfers between devices  17.8 us (47%)
  waiting for transfers between devices  9.16 us (24%)
  Pallas kernels  8.14 us (21%)
  local copies, waits for them, and re-layouts  2.22 us (6%)
    ppermute x15, starting transfers between devices, exchange(): return lax.ppermute(value, axis, [(i, i ^ step) for i in range(size)])  17.8 us
    ppermute x15, waiting for transfers between devices, exchange(): return lax.ppermute(value, axis, [(i, i ^ step) for i in range(size)])  9.16 us
    unnamed x14, local copies, waits for them, and re-layouts  1.98 us
    pallas_call x1, Pallas kernels, results(): pl.pallas_call(functools.partial(result_kernel, order, chunks), out_shape...  1.8 us
    pallas_call x1, Pallas kernels, prepare(): pl.pallas_call(functools.partial(prepare_kernel, tile, slots, count), out...  1.39 us
    pallas_call x1, Pallas kernels, pack(): pl.pallas_call(functools.partial(pack_kernel, tile, slots, count), out_sh...  1.06 us
    pallas_call x3, Pallas kernels, half_products(): pl.pallas_call(functools.partial(half_kernel, count), out_shape=[jax.Shap...  0.94 us
  transfers between devices with their start and end apart: 15, of which 10 were waited for; matrix products, arithmetic and copies ran while one was open for 1% of the time, Pallas kernels for 15%

profile of v9, /device:TPU:0, one launch (start us, length us, event | category | flops | bytes accessed | tf_op | source)
XLA Modules:
  0.0 37.7 jit_solution(5060846707991663371)
XLA Ops:
  0.0 3.0 %collective-permute-start = (bf16[1,16,512]{2,1,0:T(8,128)(2,1)}, bf16[1,16,512]{2,1,0:T(8,128)(2,1)S(1)}, u32[]{:S(2)}, u32[]{:S(2)}) collective-permute-start(bf16[1,16,512]{2,1,0:T(8,128)(2,1)} %bitcast.35), channel_id=1, source_target_pairs={{0,2},{1,3},{2,0},{3,1},{4,6},{5,7},{6,4},{7,5},{8,10},{9,11},{10,... | collective-permute-start | bytes 49160 | tf_op jit(solution)/shard_map/ppermute | solution.py:16
  3.0 0.8 %keep.1 = bf16[16,512]{1,0:T(8,128)(2,1)S(1)} custom-call(bf16[16,512]{1,0:T(8,128)(2,1)} %value.1), custom_call_target="tpu_custom_call" | custom-call | tf_op jit(solution)/shard_map/keep/pallas_call | solution.py:25
  3.8 1.2 %collective-permute-done = bf16[1,16,512]{2,1,0:T(8,128)(2,1)S(1)} collective-permute-done((bf16[1,16,512]{2,1,0:T(8,128)(2,1)}, bf16[1,16,512]{2,1,0:T(8,128)(2,1)S(1)}, u32[]{:S(2)}, u32[]{:S(2)}) %collective-permute-start) | collective-permute-done | bytes 16416 | tf_op jit(solution)/shard_map/ppermute | solution.py:16
  5.0 3.1 %collective-permute-start.1 = (bf16[2,16,512]{2,1,0:T(8,128)(2,1)S(1)}, bf16[2,16,512]{2,1,0:T(8,128)(2,1)S(1)}, u32[]{:S(2)}, u32[]{:S(2)}) collective-permute-start(bf16[2,16,512]{2,1,0:T(8,128)(2,1)S(1)} %maximum_select_fusion.5), channel_id=1, source_target_pairs={{0,4},{1,5},{2,6},{3,7},{4,0},{5,1},{6,2},{7,3},{8,12},{9,13},{10,... | collective-permute-start | bytes 98312 | tf_op jit(solution)/shard_map/ppermute | solution.py:16
  8.1 1.9 %collective-permute-done.1 = bf16[2,16,512]{2,1,0:T(8,128)(2,1)S(1)} collective-permute-done((bf16[2,16,512]{2,1,0:T(8,128)(2,1)S(1)}, bf16[2,16,512]{2,1,0:T(8,128)(2,1)S(1)}, u32[]{:S(2)}, u32[]{:S(2)}) %collective-permute-start.1) | collective-permute-done | bytes 32800 | tf_op jit(solution)/shard_map/ppermute | solution.py:16
  10.0 2.8 %collective-permute-start.2 = (bf16[4,16,512]{2,1,0:T(8,128)(2,1)S(1)}, bf16[4,16,512]{2,1,0:T(8,128)(2,1)S(1)}, u32[]{:S(2)}, u32[]{:S(2)}) collective-permute-start(bf16[4,16,512]{2,1,0:T(8,128)(2,1)S(1)} %maximum_select_fusion.4), channel_id=1, source_target_pairs={{0,24},{8,16},{16,8},{24,0},{1,25},{9,17},{17,9},{25,1},{2,26},{10... | collective-permute-start | bytes 196616 | tf_op jit(solution)/shard_map/ppermute | solution.py:16
  12.8 0.5 %collective-permute-start.5 = (bf16[4,16,512]{2,1,0:T(8,128)(2,1)S(1)}, bf16[4,16,512]{2,1,0:T(8,128)(2,1)S(1)}, u32[]{:S(2)}, u32[]{:S(2)}) collective-permute-start(bf16[4,16,512]{2,1,0:T(8,128)(2,1)S(1)} %maximum_select_fusion.4), channel_id=1, source_target_pairs={{0,8},{8,0},{16,24},{24,16},{1,9},{9,1},{17,25},{25,17},{2,10},{10... | collective-permute-start | bytes 196616 | tf_op jit(solution)/shard_map/ppermute | solution.py:16
  13.5 1.3 %copy-done = bf16[1,384,1536]{2,1,0:T(8,128)(2,1)S(1)} copy-done((bf16[1,384,1536]{2,1,0:T(8,128)(2,1)S(1)}, bf16[1,384,1536]{2,1,0:T(8,128)(2,1)}, u32[]{:S(2)}) %copy-start) | copy-done | bytes 1179672
  14.8 0.7 %copy-done.2 = s32[4,4]{1,0:T(4,128)S(1)} copy-done((s32[4,4]{1,0:T(4,128)S(1)}, s32[4,4]{1,0:T(4,128)}, u32[]{:S(2)}) %copy-start.2) | copy-done | bytes 88
  15.5 1.1 %pack.1 = (bf16[384,512]{1,0:T(8,128)(2,1)S(1)}, bf16[384,512]{1,0:T(8,128)(2,1)S(1)}, bf16[384,512]{1,0:T(8,128)(2,1)S(1)}, bf16[384,512]{1,0:T(8,128)(2,1)S(1)}) custom-call(s32[1]{0:T(128)} %bitcast.place, s32[4,4]{1,0:T(4,128)S(1)} %copy-done.2, bf16[384,1536]{1,0:T(8,128)(2,1)S(1)} %bitcast.17), custom_call_target="tpu_custom_call" | custom-call | bytes 3145728 | tf_op jit(solution)/shard_map/pack/pallas_call | solution.py:59
  16.6 0.5 %collective-permute-done.5 = bf16[4,16,512]{2,1,0:T(8,128)(2,1)S(1)} collective-permute-done((bf16[4,16,512]{2,1,0:T(8,128)(2,1)S(1)}, bf16[4,16,512]{2,1,0:T(8,128)(2,1)S(1)}, u32[]{:S(2)}, u32[]{:S(2)}) %collective-permute-start.5) | collective-permute-done | bytes 65568 | tf_op jit(solution)/shard_map/ppermute | solution.py:16
  17.1 0.5 %collective-permute-start.3 = (bf16[4,16,512]{2,1,0:T(8,128)(2,1)S(1)}, bf16[4,16,512]{2,1,0:T(8,128)(2,1)S(1)}, u32[]{:S(2)}, u32[]{:S(2)}) collective-permute-start(bf16[4,16,512]{2,1,0:T(8,128)(2,1)S(1)} %collective-permute-done.2), channel_id=1, source_target_pairs={{0,1},{1,0},{2,3},{3,2},{4,5},{5,4},{6,7},{7,6},{8,9},{9,8},{10,11... | collective-permute-start | bytes 196616 | tf_op jit(solution)/shard_map/ppermute | solution.py:16
  17.6 0.7 %collective-permute-done.6 = bf16[4,16,512]{2,1,0:T(8,128)(2,1)S(1)} collective-permute-done((bf16[4,16,512]{2,1,0:T(8,128)(2,1)S(1)}, bf16[4,16,512]{2,1,0:T(8,128)(2,1)S(1)}, u32[]{:S(2)}, u32[]{:S(2)}) %collective-permute-start.6) | collective-permute-done | bytes 65568 | tf_op jit(solution)/shard_map/ppermute | solution.py:16
  18.5 0.3 half_products.3
  18.8 0.4 %collective-permute-start.4 = (bf16[4,16,512]{2,1,0:T(8,128)(2,1)S(1)}, bf16[4,16,512]{2,1,0:T(8,128)(2,1)S(1)}, u32[]{:S(2)}, u32[]{:S(2)}) collective-permute-start(bf16[4,16,512]{2,1,0:T(8,128)(2,1)S(1)} %maximum_select_fusion.4), channel_id=1, source_target_pairs={{0,1},{1,0},{2,3},{3,2},{4,5},{5,4},{6,7},{7,6},{8,9},{9,8},{10,11... | collective-permute-start | bytes 196616 | tf_op jit(solution)/shard_map/ppermute | solution.py:16
  19.3 2.5 %collective-permute-start.9 = (bf16[128,384]{1,0:T(8,128)(2,1)S(1)}, bf16[128,384]{1,0:T(8,128)(2,1)S(1)}, u32[]{:S(2)}, u32[]{:S(2)}) collective-permute-start(bf16[128,384]{1,0:T(8,128)(2,1)S(1)} %half_products.3), channel_id=1, source_target_pairs={{0,24},{8,16},{16,8},{24,0},{1,25},{9,17},{17,9},{25,1},{2,26},{10... | collective-permute-start | bytes 294920 | tf_op jit(solution)/shard_map/ppermute | solution.py:16
  21.7 0.4 half_products.5
  22.1 0.6 %collective-permute-start.10 = (bf16[128,384]{1,0:T(8,128)(2,1)S(1)}, bf16[128,384]{1,0:T(8,128)(2,1)S(1)}, u32[]{:S(2)}, u32[]{:S(2)}) collective-permute-start(bf16[128,384]{1,0:T(8,128)(2,1)S(1)} %get-tuple-element.52), channel_id=1, source_target_pairs={{0,16},{8,24},{16,0},{24,8},{1,17},{9,25},{17,1},{25,9},{2,18},{10... | collective-permute-start | bytes 294920 | tf_op jit(solution)/shard_map/ppermute | solution.py:16
  22.7 0.6 %collective-permute-start.11 = (bf16[128,384]{1,0:T(8,128)(2,1)S(1)}, bf16[128,384]{1,0:T(8,128)(2,1)S(1)}, u32[]{:S(2)}, u32[]{:S(2)}) collective-permute-start(bf16[128,384]{1,0:T(8,128)(2,1)S(1)} %get-tuple-element.53), channel_id=1, source_target_pairs={{0,8},{8,0},{16,24},{24,16},{1,9},{9,1},{17,25},{25,17},{2,10},{10... | collective-permute-start | bytes 294920 | tf_op jit(solution)/shard_map/ppermute | solution.py:16
  23.9 1.4 %prepare.1 = (bf16[512,1536]{1,0:T(8,128)(2,1)S(1)}, bf16[1536,512]{1,0:T(8,128)(2,1)S(1)}, f32[128,512]{1,0:T(8,128)S(1)}, f32[384,1536]{1,0:T(8,128)S(1)}) custom-call(s32[1]{0:T(128)} %bitcast.place, s32[4,4]{1,0:T(4,128)S(1)} %copy-done.3, s32[1,2]{1,0:T(1,128)S(1)} %copy-done.5, f32[300]{0:T(512)S(1)} %copy-done.4, bf16[128,512]{1,0:T(8,128)(2,1)S(1)} %bitcast.21, ...), custom_call_target="tpu_custom_call" | custom-call | bytes 6291456 | tf_op jit(solution)/shard_map/prepare/pallas_call | solution.py:127
  25.3 0.3 mixed.1
  25.6 1.6 %collective-permute-done.10.rest_0_ = bf16[128,384]{1,0:T(8,128)(2,1)S(1)} collective-permute-done((bf16[128,384]{1,0:T(8,128)(2,1)S(1)}, bf16[128,384]{1,0:T(8,128)(2,1)S(1)}, u32[]{:S(2)}, u32[]{:S(2)}) %collective-permute-start.10) | collective-permute-done | bytes 98336 | tf_op jit(solution)/shard_map/ppermute | solution.py:16
  27.3 0.5 %weighted.1 = (bf16[128,512]{1,0:T(8,128)(2,1)S(1)}, bf16[384,128]{1,0:T(8,128)(2,1)S(1)}) custom-call(bf16[1536,512]{1,0:T(8,128)(2,1)S(1)} %get-tuple-element.46.turned, f32[128,512]{1,0:T(8,128)S(1)} %get-tuple-element.47.scale, f32[128,512]{1,0:T(8,128)S(1)} %mixed.1, bf16[128,384]{1,0:T(8,128)(2,1)S(1)} %collective-permute-done.10.rest_0_, ...), custom_call_target="tpu_custom_call" | custom-call | tf_op jit(solution)/shard_map/weighted/pallas_call | solution.py:209
  27.9 2.2 %collective-permute-start.12 = (bf16[384,128]{1,0:T(8,128)(2,1)S(1)}, bf16[384,128]{1,0:T(8,128)(2,1)S(1)}, u32[]{:S(2)}, u32[]{:S(2)}) collective-permute-start(bf16[384,128]{1,0:T(8,128)(2,1)S(1)} %get-tuple-element.55), channel_id=1, source_target_pairs={{0,24},{8,16},{16,8},{24,0},{1,25},{9,17},{17,9},{25,1},{2,26},{10... | collective-permute-start | bytes 294920 | tf_op jit(solution)/shard_map/ppermute | solution.py:16
  30.0 0.4 ladders.3
  30.4 0.9 %collective-permute-start.13 = (bf16[384,128]{1,0:T(8,128)(2,1)S(1)}, bf16[384,128]{1,0:T(8,128)(2,1)S(1)}, u32[]{:S(2)}, u32[]{:S(2)}) collective-permute-start(bf16[384,128]{1,0:T(8,128)(2,1)S(1)} %get-tuple-element.57), channel_id=1, source_target_pairs={{0,16},{8,24},{16,0},{24,8},{1,17},{9,25},{17,1},{25,9},{2,18},{10... | collective-permute-start | bytes 294920 | tf_op jit(solution)/shard_map/ppermute | solution.py:16
  31.3 0.6 %collective-permute-start.14 = (bf16[384,128]{1,0:T(8,128)(2,1)S(1)}, bf16[384,128]{1,0:T(8,128)(2,1)S(1)}, u32[]{:S(2)}, u32[]{:S(2)}) collective-permute-start(bf16[384,128]{1,0:T(8,128)(2,1)S(1)} %get-tuple-element.58), channel_id=1, source_target_pairs={{0,8},{8,0},{16,24},{24,16},{1,9},{9,1},{17,25},{25,17},{2,10},{10... | collective-permute-start | bytes 294920 | tf_op jit(solution)/shard_map/ppermute | solution.py:16
  32.1 1.4 %collective-permute-done.12.rest_1_ = bf16[384,128]{1,0:T(8,128)(2,1)S(1)} collective-permute-done((bf16[384,128]{1,0:T(8,128)(2,1)S(1)}, bf16[384,128]{1,0:T(8,128)(2,1)S(1)}, u32[]{:S(2)}, u32[]{:S(2)}) %collective-permute-start.12) | collective-permute-done | bytes 98336 | tf_op jit(solution)/shard_map/ppermute | solution.py:16
  33.5 0.8 %result_start.1.begun = f32[384,1536]{1,0:T(8,128)S(1)} custom-call(bf16[512,1536]{1,0:T(8,128)(2,1)S(1)} %get-tuple-element.45.dense, bf16[384,128]{1,0:T(8,128)(2,1)S(1)} %ladders.2.rest_0_, bf16[384,128]{1,0:T(8,128)(2,1)S(1)} %collective-permute-done.12.rest_1_), custom_call_target="tpu_custom_call" | custom-call | flops 301989888 | tf_op jit(solution)/shard_map/result_start/pallas_call | solution.py:250
  34.3 1.3 %collective-permute-done.13.rest_0_ = bf16[384,128]{1,0:T(8,128)(2,1)S(1)} collective-permute-done((bf16[384,128]{1,0:T(8,128)(2,1)S(1)}, bf16[384,128]{1,0:T(8,128)(2,1)S(1)}, u32[]{:S(2)}, u32[]{:S(2)}) %collective-permute-start.13) | collective-permute-done | bytes 98336 | tf_op jit(solution)/shard_map/ppermute | solution.py:16
  35.5 0.3 collective-permute-done.14.rest_1_
  35.9 1.8 %results.1 = f32[384,1536]{1,0:T(8,128)} custom-call(f32[384,1536]{1,0:T(8,128)S(1)} %result_start.1.begun, bf16[512,1536]{1,0:T(8,128)(2,1)S(1)} %get-tuple-element.45.dense, f32[384,1536]{1,0:T(8,128)S(1)} %get-tuple-element.56.inverse, bf16[384,128]{1,0:T(8,128)(2,1)S(1)} %collective-permute-done.13.rest_0_, ...), custom_call_target="tpu_custom_call" | custom-call | tf_op jit(solution)/shard_map/results/pallas_call | solution.py:284
  (36 shorter events, 1.4 us)
Async XLA Ops:
  0.0 5.0 %collective-permute-start = (bf16[1,16,512]{2,1,0:T(8,128)(2,1)}, bf16[1,16,512]{2,1,0:T(8,128)(2,1)S(1)}, u32[]{:S(2)}, u32[]{:S(2)}) collective-permute-start(bf16[1,16,512]{2,1,0:T(8,128)(2,1)} %bitcast.35), channel_id=1, source_target_pairs={{0,2},{1,3},{2,0},{3,1},{4,6},{5,7},{6,4},{7,5},{8,10},{9,11},{10,... | collective-permute-start | bytes 49160 | tf_op jit(solution)/shard_map/ppermute | solution.py:16
  5.0 5.0 %collective-permute-start.1 = (bf16[2,16,512]{2,1,0:T(8,128)(2,1)S(1)}, bf16[2,16,512]{2,1,0:T(8,128)(2,1)S(1)}, u32[]{:S(2)}, u32[]{:S(2)}) collective-permute-start(bf16[2,16,512]{2,1,0:T(8,128)(2,1)S(1)} %maximum_select_fusion.5), channel_id=1, source_target_pairs={{0,4},{1,5},{2,6},{3,7},{4,0},{5,1},{6,2},{7,3},{8,12},{9,13},{10,... | collective-permute-start | bytes 98312 | tf_op jit(solution)/shard_map/ppermute | solution.py:16
  10.0 6.6 %collective-permute-start.2 = (bf16[4,16,512]{2,1,0:T(8,128)(2,1)S(1)}, bf16[4,16,512]{2,1,0:T(8,128)(2,1)S(1)}, u32[]{:S(2)}, u32[]{:S(2)}) collective-permute-start(bf16[4,16,512]{2,1,0:T(8,128)(2,1)S(1)} %maximum_select_fusion.4), channel_id=1, source_target_pairs={{0,24},{8,16},{16,8},{24,0},{1,25},{9,17},{17,9},{25,1},{2,26},{10... | collective-permute-start | bytes 196616 | tf_op jit(solution)/shard_map/ppermute | solution.py:16
  12.8 4.3 %collective-permute-start.5 = (bf16[4,16,512]{2,1,0:T(8,128)(2,1)S(1)}, bf16[4,16,512]{2,1,0:T(8,128)(2,1)S(1)}, u32[]{:S(2)}, u32[]{:S(2)}) collective-permute-start(bf16[4,16,512]{2,1,0:T(8,128)(2,1)S(1)} %maximum_select_fusion.4), channel_id=1, source_target_pairs={{0,8},{8,0},{16,24},{24,16},{1,9},{9,1},{17,25},{25,17},{2,10},{10... | collective-permute-start | bytes 196616 | tf_op jit(solution)/shard_map/ppermute | solution.py:16
  13.3 4.3 %collective-permute-start.7 = (bf16[4,16,512]{2,1,0:T(8,128)(2,1)S(1)}, bf16[4,16,512]{2,1,0:T(8,128)(2,1)S(1)}, u32[]{:S(2)}, u32[]{:S(2)}) collective-permute-start(bf16[4,16,512]{2,1,0:T(8,128)(2,1)S(1)} %maximum_select_fusion.4), channel_id=1, source_target_pairs={{0,16},{8,24},{16,0},{24,8},{1,17},{9,25},{17,1},{25,9},{2,18},{10... | collective-permute-start | bytes 196616 | tf_op jit(solution)/shard_map/ppermute | solution.py:16
  13.5 1.3 %copy-start = (bf16[1,384,1536]{2,1,0:T(8,128)(2,1)S(1)}, bf16[1,384,1536]{2,1,0:T(8,128)(2,1)}, u32[]{:S(2)}) copy-start(bf16[1,384,1536]{2,1,0:T(8,128)(2,1)} %param.7) | copy-start | bytes 3538948
  14.8 0.7 %copy-start.2 = (s32[4,4]{1,0:T(4,128)S(1)}, s32[4,4]{1,0:T(4,128)}, u32[]{:S(2)}) copy-start(s32[4,4]{1,0:T(4,128)} %screen.3) | copy-start | bytes 196
  16.5 7.1 %copy-start.6 = (f32[1536]{0:T(1024)S(1)}, f32[1536]{0:T(1024)}, u32[]{:S(2)}) copy-start(f32[1536]{0:T(1024)} %param.12) | copy-start | bytes 18436
  16.5 7.3 %copy-start.1 = (bf16[512,128]{1,0:T(8,128)(2,1)S(1)}, bf16[512,128]{1,0:T(8,128)(2,1)}, u32[]{:S(2)}) copy-start(bf16[512,128]{1,0:T(8,128)(2,1)} %rest_4_.1) | copy-start | bytes 393220
  16.6 7.3 %copy-start.3 = (s32[4,4]{1,0:T(4,128)S(1)}, s32[4,4]{1,0:T(4,128)}, u32[]{:S(2)}) copy-start(s32[4,4]{1,0:T(4,128)} %screen.3) | copy-start | bytes 196
  16.6 7.3 %copy-start.4 = (f32[300]{0:T(512)S(1)}, f32[300]{0:T(512)}, u32[]{:S(2)}) copy-start(f32[300]{0:T(512)} %occ_energy.1) | copy-start | bytes 3604
  16.6 7.3 %copy-start.5 = (s32[1,2]{1,0:T(1,128)S(1)}, s32[1,2]{1,0:T(1,128)}, u32[]{:S(2)}) copy-start(s32[1,2]{1,0:T(1,128)} %pair_occ.1) | copy-start | bytes 28
  17.1 1.3 %collective-permute-start.6 = (bf16[4,16,512]{2,1,0:T(8,128)(2,1)S(1)}, bf16[4,16,512]{2,1,0:T(8,128)(2,1)S(1)}, u32[]{:S(2)}, u32[]{:S(2)}) collective-permute-start(bf16[4,16,512]{2,1,0:T(8,128)(2,1)S(1)} %collective-permute-done.5), channel_id=1, source_target_pairs={{0,1},{1,0},{2,3},{3,2},{4,5},{5,4},{6,7},{7,6},{8,9},{9,8},{10,11... | collective-permute-start | bytes 196616 | tf_op jit(solution)/shard_map/ppermute | solution.py:16
  17.1 1.4 %collective-permute-start.3 = (bf16[4,16,512]{2,1,0:T(8,128)(2,1)S(1)}, bf16[4,16,512]{2,1,0:T(8,128)(2,1)S(1)}, u32[]{:S(2)}, u32[]{:S(2)}) collective-permute-start(bf16[4,16,512]{2,1,0:T(8,128)(2,1)S(1)} %collective-permute-done.2), channel_id=1, source_target_pairs={{0,1},{1,0},{2,3},{3,2},{4,5},{5,4},{6,7},{7,6},{8,9},{9,8},{10,11... | collective-permute-start | bytes 196616 | tf_op jit(solution)/shard_map/ppermute | solution.py:16
  17.6 1.6 %collective-permute-start.8 = (bf16[4,16,512]{2,1,0:T(8,128)(2,1)S(1)}, bf16[4,16,512]{2,1,0:T(8,128)(2,1)S(1)}, u32[]{:S(2)}, u32[]{:S(2)}) collective-permute-start(bf16[4,16,512]{2,1,0:T(8,128)(2,1)S(1)} %collective-permute-done.7), channel_id=1, source_target_pairs={{0,1},{1,0},{2,3},{3,2},{4,5},{5,4},{6,7},{7,6},{8,9},{9,8},{10,11... | collective-permute-start | bytes 196616 | tf_op jit(solution)/shard_map/ppermute | solution.py:16
  18.8 4.5 %collective-permute-start.4 = (bf16[4,16,512]{2,1,0:T(8,128)(2,1)S(1)}, bf16[4,16,512]{2,1,0:T(8,128)(2,1)S(1)}, u32[]{:S(2)}, u32[]{:S(2)}) collective-permute-start(bf16[4,16,512]{2,1,0:T(8,128)(2,1)S(1)} %maximum_select_fusion.4), channel_id=1, source_target_pairs={{0,1},{1,0},{2,3},{3,2},{4,5},{5,4},{6,7},{7,6},{8,9},{9,8},{10,11... | collective-permute-start | bytes 196616 | tf_op jit(solution)/shard_map/ppermute | solution.py:16
  19.3 6.0 %collective-permute-start.9 = (bf16[128,384]{1,0:T(8,128)(2,1)S(1)}, bf16[128,384]{1,0:T(8,128)(2,1)S(1)}, u32[]{:S(2)}, u32[]{:S(2)}) collective-permute-start(bf16[128,384]{1,0:T(8,128)(2,1)S(1)} %half_products.3), channel_id=1, source_target_pairs={{0,24},{8,16},{16,8},{24,0},{1,25},{9,17},{17,9},{25,1},{2,26},{10... | collective-permute-start | bytes 294920 | tf_op jit(solution)/shard_map/ppermute | solution.py:16
  22.1 5.1 %collective-permute-start.10 = (bf16[128,384]{1,0:T(8,128)(2,1)S(1)}, bf16[128,384]{1,0:T(8,128)(2,1)S(1)}, u32[]{:S(2)}, u32[]{:S(2)}) collective-permute-start(bf16[128,384]{1,0:T(8,128)(2,1)S(1)} %get-tuple-element.52), channel_id=1, source_target_pairs={{0,16},{8,24},{16,0},{24,8},{1,17},{9,25},{17,1},{25,9},{2,18},{10... | collective-permute-start | bytes 294920 | tf_op jit(solution)/shard_map/ppermute | solution.py:16
  22.7 4.6 %collective-permute-start.11 = (bf16[128,384]{1,0:T(8,128)(2,1)S(1)}, bf16[128,384]{1,0:T(8,128)(2,1)S(1)}, u32[]{:S(2)}, u32[]{:S(2)}) collective-permute-start(bf16[128,384]{1,0:T(8,128)(2,1)S(1)} %get-tuple-element.53), channel_id=1, source_target_pairs={{0,8},{8,0},{16,24},{24,16},{1,9},{9,1},{17,25},{25,17},{2,10},{10... | collective-permute-start | bytes 294920 | tf_op jit(solution)/shard_map/ppermute | solution.py:16
  27.9 5.7 %collective-permute-start.12 = (bf16[384,128]{1,0:T(8,128)(2,1)S(1)}, bf16[384,128]{1,0:T(8,128)(2,1)S(1)}, u32[]{:S(2)}, u32[]{:S(2)}) collective-permute-start(bf16[384,128]{1,0:T(8,128)(2,1)S(1)} %get-tuple-element.55), channel_id=1, source_target_pairs={{0,24},{8,16},{16,8},{24,0},{1,25},{9,17},{17,9},{25,1},{2,26},{10... | collective-permute-start | bytes 294920 | tf_op jit(solution)/shard_map/ppermute | solution.py:16
  30.4 5.2 %collective-permute-start.13 = (bf16[384,128]{1,0:T(8,128)(2,1)S(1)}, bf16[384,128]{1,0:T(8,128)(2,1)S(1)}, u32[]{:S(2)}, u32[]{:S(2)}) collective-permute-start(bf16[384,128]{1,0:T(8,128)(2,1)S(1)} %get-tuple-element.57), channel_id=1, source_target_pairs={{0,16},{8,24},{16,0},{24,8},{1,17},{9,25},{17,1},{25,9},{2,18},{10... | collective-permute-start | bytes 294920 | tf_op jit(solution)/shard_map/ppermute | solution.py:16
  31.3 4.6 %collective-permute-start.14 = (bf16[384,128]{1,0:T(8,128)(2,1)S(1)}, bf16[384,128]{1,0:T(8,128)(2,1)S(1)}, u32[]{:S(2)}, u32[]{:S(2)}) collective-permute-start(bf16[384,128]{1,0:T(8,128)(2,1)S(1)} %get-tuple-element.58), channel_id=1, source_target_pairs={{0,8},{8,0},{16,24},{24,16},{1,9},{9,1},{17,25},{25,17},{2,10},{10... | collective-permute-start | bytes 294920 | tf_op jit(solution)/shard_map/ppermute | solution.py:16

commit v10 on v9

--- a/solution.py
+++ b/solution.py
@@ -336,6 +336,7 @@
         group = half_products([packs[k] for k in ks], [blocks[k] for k in ks])
         if not halves:
             parts[0], group = lax.optimization_barrier((parts[0], group))
+            packs[order[2]], parts[0] = lax.optimization_barrier((packs[order[2]], parts[0]))
         halves += [exchange(half, "grid", grids, k) for k, half in zip(ks, group)]
     blocks[0] = swapped(parts[0])
     halves = list(half_products([packs[0]], [blocks[0]])) + halves

time: 37.9 us -> 37.9 us (level)
  no operation moved by 1% of the time
where the time goes in v10:
time: 37.9 us; the launch traced here: 37.7 us
  starting transfers between devices  17.8 us (47%)
  waiting for transfers between devices  9.16 us (24%)
  Pallas kernels  8.14 us (21%)
  local copies, waits for them, and re-layouts  2.22 us (6%)
    ppermute x15, starting transfers between devices, exchange(): return lax.ppermute(value, axis, [(i, i ^ step) for i in range(size)])  17.8 us
    ppermute x15, waiting for transfers between devices, exchange(): return lax.ppermute(value, axis, [(i, i ^ step) for i in range(size)])  9.16 us
    unnamed x14, local copies, waits for them, and re-layouts  1.98 us
    pallas_call x1, Pallas kernels, results(): pl.pallas_call(functools.partial(result_kernel, order, chunks), out_shape...  1.8 us
    pallas_call x1, Pallas kernels, prepare(): pl.pallas_call(functools.partial(prepare_kernel, tile, slots, count), out...  1.39 us
    pallas_call x1, Pallas kernels, pack(): pl.pallas_call(functools.partial(pack_kernel, tile, slots, count), out_sh...  1.06 us
    pallas_call x3, Pallas kernels, half_products(): pl.pallas_call(functools.partial(half_kernel, count), out_shape=[jax.Shap...  0.94 us
  transfers between devices with their start and end apart: 15, of which 10 were waited for; matrix products, arithmetic and copies ran while one was open for 1% of the time, Pallas kernels for 15%

profile of v10, /device:TPU:0, one launch (start us, length us, event | category | flops | bytes accessed | tf_op | source)
XLA Modules:
  0.0 37.7 jit_solution(5060846707991663371)
XLA Ops:
  0.0 3.0 %collective-permute-start = (bf16[1,16,512]{2,1,0:T(8,128)(2,1)}, bf16[1,16,512]{2,1,0:T(8,128)(2,1)S(1)}, u32[]{:S(2)}, u32[]{:S(2)}) collective-permute-start(bf16[1,16,512]{2,1,0:T(8,128)(2,1)} %bitcast.35), channel_id=1, source_target_pairs={{0,2},{1,3},{2,0},{3,1},{4,6},{5,7},{6,4},{7,5},{8,10},{9,11},{10,... | collective-permute-start | bytes 49160 | tf_op jit(solution)/shard_map/ppermute | solution.py:16
  3.0 0.8 %keep.1 = bf16[16,512]{1,0:T(8,128)(2,1)S(1)} custom-call(bf16[16,512]{1,0:T(8,128)(2,1)} %value.1), custom_call_target="tpu_custom_call" | custom-call | tf_op jit(solution)/shard_map/keep/pallas_call | solution.py:25
  3.8 1.2 %collective-permute-done = bf16[1,16,512]{2,1,0:T(8,128)(2,1)S(1)} collective-permute-done((bf16[1,16,512]{2,1,0:T(8,128)(2,1)}, bf16[1,16,512]{2,1,0:T(8,128)(2,1)S(1)}, u32[]{:S(2)}, u32[]{:S(2)}) %collective-permute-start) | collective-permute-done | bytes 16416 | tf_op jit(solution)/shard_map/ppermute | solution.py:16
  5.0 3.1 %collective-permute-start.1 = (bf16[2,16,512]{2,1,0:T(8,128)(2,1)S(1)}, bf16[2,16,512]{2,1,0:T(8,128)(2,1)S(1)}, u32[]{:S(2)}, u32[]{:S(2)}) collective-permute-start(bf16[2,16,512]{2,1,0:T(8,128)(2,1)S(1)} %maximum_select_fusion.5), channel_id=1, source_target_pairs={{0,4},{1,5},{2,6},{3,7},{4,0},{5,1},{6,2},{7,3},{8,12},{9,13},{10,... | collective-permute-start | bytes 98312 | tf_op jit(solution)/shard_map/ppermute | solution.py:16
  8.1 1.9 %collective-permute-done.1 = bf16[2,16,512]{2,1,0:T(8,128)(2,1)S(1)} collective-permute-done((bf16[2,16,512]{2,1,0:T(8,128)(2,1)S(1)}, bf16[2,16,512]{2,1,0:T(8,128)(2,1)S(1)}, u32[]{:S(2)}, u32[]{:S(2)}) %collective-permute-start.1) | collective-permute-done | bytes 32800 | tf_op jit(solution)/shard_map/ppermute | solution.py:16
  10.0 2.8 %collective-permute-start.3 = (bf16[4,16,512]{2,1,0:T(8,128)(2,1)S(1)}, bf16[4,16,512]{2,1,0:T(8,128)(2,1)S(1)}, u32[]{:S(2)}, u32[]{:S(2)}) collective-permute-start(bf16[4,16,512]{2,1,0:T(8,128)(2,1)S(1)} %maximum_select_fusion.4), channel_id=1, source_target_pairs={{0,24},{8,16},{16,8},{24,0},{1,25},{9,17},{17,9},{25,1},{2,26},{10... | collective-permute-start | bytes 196616 | tf_op jit(solution)/shard_map/ppermute | solution.py:16
  12.8 0.5 %collective-permute-start.6 = (bf16[4,16,512]{2,1,0:T(8,128)(2,1)S(1)}, bf16[4,16,512]{2,1,0:T(8,128)(2,1)S(1)}, u32[]{:S(2)}, u32[]{:S(2)}) collective-permute-start(bf16[4,16,512]{2,1,0:T(8,128)(2,1)S(1)} %maximum_select_fusion.4), channel_id=1, source_target_pairs={{0,8},{8,0},{16,24},{24,16},{1,9},{9,1},{17,25},{25,17},{2,10},{10... | collective-permute-start | bytes 196616 | tf_op jit(solution)/shard_map/ppermute | solution.py:16
  13.5 1.3 %copy-done = bf16[1,384,1536]{2,1,0:T(8,128)(2,1)S(1)} copy-done((bf16[1,384,1536]{2,1,0:T(8,128)(2,1)S(1)}, bf16[1,384,1536]{2,1,0:T(8,128)(2,1)}, u32[]{:S(2)}) %copy-start) | copy-done | bytes 1179672
  14.8 0.7 %copy-done.2 = s32[4,4]{1,0:T(4,128)S(1)} copy-done((s32[4,4]{1,0:T(4,128)S(1)}, s32[4,4]{1,0:T(4,128)}, u32[]{:S(2)}) %copy-start.2) | copy-done | bytes 88
  15.5 1.1 %pack.1 = (bf16[384,512]{1,0:T(8,128)(2,1)S(1)}, bf16[384,512]{1,0:T(8,128)(2,1)S(1)}, bf16[384,512]{1,0:T(8,128)(2,1)S(1)}, bf16[384,512]{1,0:T(8,128)(2,1)S(1)}) custom-call(s32[1]{0:T(128)} %bitcast.place, s32[4,4]{1,0:T(4,128)S(1)} %copy-done.2, bf16[384,1536]{1,0:T(8,128)(2,1)S(1)} %bitcast.17), custom_call_target="tpu_custom_call" | custom-call | bytes 3145728 | tf_op jit(solution)/shard_map/pack/pallas_call | solution.py:59
  16.6 0.5 %collective-permute-done.6 = bf16[4,16,512]{2,1,0:T(8,128)(2,1)S(1)} collective-permute-done((bf16[4,16,512]{2,1,0:T(8,128)(2,1)S(1)}, bf16[4,16,512]{2,1,0:T(8,128)(2,1)S(1)}, u32[]{:S(2)}, u32[]{:S(2)}) %collective-permute-start.6) | collective-permute-done | bytes 65568 | tf_op jit(solution)/shard_map/ppermute | solution.py:16
  17.1 0.5 %collective-permute-start.4 = (bf16[4,16,512]{2,1,0:T(8,128)(2,1)S(1)}, bf16[4,16,512]{2,1,0:T(8,128)(2,1)S(1)}, u32[]{:S(2)}, u32[]{:S(2)}) collective-permute-start(bf16[4,16,512]{2,1,0:T(8,128)(2,1)S(1)} %collective-permute-done.3), channel_id=1, source_target_pairs={{0,1},{1,0},{2,3},{3,2},{4,5},{5,4},{6,7},{7,6},{8,9},{9,8},{10,11... | collective-permute-start | bytes 196616 | tf_op jit(solution)/shard_map/ppermute | solution.py:16
  17.6 0.7 %collective-permute-done.7 = bf16[4,16,512]{2,1,0:T(8,128)(2,1)S(1)} collective-permute-done((bf16[4,16,512]{2,1,0:T(8,128)(2,1)S(1)}, bf16[4,16,512]{2,1,0:T(8,128)(2,1)S(1)}, u32[]{:S(2)}, u32[]{:S(2)}) %collective-permute-start.7) | collective-permute-done | bytes 65568 | tf_op jit(solution)/shard_map/ppermute | solution.py:16
  18.5 0.3 half_products.3
  18.8 0.4 %collective-permute-start.5 = (bf16[4,16,512]{2,1,0:T(8,128)(2,1)S(1)}, bf16[4,16,512]{2,1,0:T(8,128)(2,1)S(1)}, u32[]{:S(2)}, u32[]{:S(2)}) collective-permute-start(bf16[4,16,512]{2,1,0:T(8,128)(2,1)S(1)} %maximum_select_fusion.4), channel_id=1, source_target_pairs={{0,1},{1,0},{2,3},{3,2},{4,5},{5,4},{6,7},{7,6},{8,9},{9,8},{10,11... | collective-permute-start | bytes 196616 | tf_op jit(solution)/shard_map/ppermute | solution.py:16
  19.3 2.5 %collective-permute-start.9 = (bf16[128,384]{1,0:T(8,128)(2,1)S(1)}, bf16[128,384]{1,0:T(8,128)(2,1)S(1)}, u32[]{:S(2)}, u32[]{:S(2)}) collective-permute-start(bf16[128,384]{1,0:T(8,128)(2,1)S(1)} %half_products.3), channel_id=1, source_target_pairs={{0,24},{8,16},{16,8},{24,0},{1,25},{9,17},{17,9},{25,1},{2,26},{10... | collective-permute-start | bytes 294920 | tf_op jit(solution)/shard_map/ppermute | solution.py:16
  21.7 0.4 half_products.5
  22.1 0.6 %collective-permute-start.10 = (bf16[128,384]{1,0:T(8,128)(2,1)S(1)}, bf16[128,384]{1,0:T(8,128)(2,1)S(1)}, u32[]{:S(2)}, u32[]{:S(2)}) collective-permute-start(bf16[128,384]{1,0:T(8,128)(2,1)S(1)} %get-tuple-element.56), channel_id=1, source_target_pairs={{0,16},{8,24},{16,0},{24,8},{1,17},{9,25},{17,1},{25,9},{2,18},{10... | collective-permute-start | bytes 294920 | tf_op jit(solution)/shard_map/ppermute | solution.py:16
  22.7 0.6 %collective-permute-start.11 = (bf16[128,384]{1,0:T(8,128)(2,1)S(1)}, bf16[128,384]{1,0:T(8,128)(2,1)S(1)}, u32[]{:S(2)}, u32[]{:S(2)}) collective-permute-start(bf16[128,384]{1,0:T(8,128)(2,1)S(1)} %get-tuple-element.57), channel_id=1, source_target_pairs={{0,8},{8,0},{16,24},{24,16},{1,9},{9,1},{17,25},{25,17},{2,10},{10... | collective-permute-start | bytes 294920 | tf_op jit(solution)/shard_map/ppermute | solution.py:16
  23.9 1.4 %prepare.1 = (bf16[512,1536]{1,0:T(8,128)(2,1)S(1)}, bf16[1536,512]{1,0:T(8,128)(2,1)S(1)}, f32[128,512]{1,0:T(8,128)S(1)}, f32[384,1536]{1,0:T(8,128)S(1)}) custom-call(s32[1]{0:T(128)} %bitcast.place, s32[4,4]{1,0:T(4,128)S(1)} %copy-done.3, s32[1,2]{1,0:T(1,128)S(1)} %copy-done.5, f32[300]{0:T(512)S(1)} %copy-done.4, bf16[128,512]{1,0:T(8,128)(2,1)S(1)} %bitcast.21, ...), custom_call_target="tpu_custom_call" | custom-call | bytes 6291456 | tf_op jit(solution)/shard_map/prepare/pallas_call | solution.py:127
  25.3 0.3 mixed.1
  25.6 1.6 %collective-permute-done.10.rest_0_ = bf16[128,384]{1,0:T(8,128)(2,1)S(1)} collective-permute-done((bf16[128,384]{1,0:T(8,128)(2,1)S(1)}, bf16[128,384]{1,0:T(8,128)(2,1)S(1)}, u32[]{:S(2)}, u32[]{:S(2)}) %collective-permute-start.10) | collective-permute-done | bytes 98336 | tf_op jit(solution)/shard_map/ppermute | solution.py:16
  27.3 0.5 %weighted.1 = (bf16[128,512]{1,0:T(8,128)(2,1)S(1)}, bf16[384,128]{1,0:T(8,128)(2,1)S(1)}) custom-call(bf16[1536,512]{1,0:T(8,128)(2,1)S(1)} %get-tuple-element.50.turned, f32[128,512]{1,0:T(8,128)S(1)} %get-tuple-element.51.scale, f32[128,512]{1,0:T(8,128)S(1)} %mixed.1, bf16[128,384]{1,0:T(8,128)(2,1)S(1)} %collective-permute-done.10.rest_0_, ...), custom_call_target="tpu_custom_call" | custom-call | tf_op jit(solution)/shard_map/weighted/pallas_call | solution.py:209
  27.9 2.2 %collective-permute-start.12 = (bf16[384,128]{1,0:T(8,128)(2,1)S(1)}, bf16[384,128]{1,0:T(8,128)(2,1)S(1)}, u32[]{:S(2)}, u32[]{:S(2)}) collective-permute-start(bf16[384,128]{1,0:T(8,128)(2,1)S(1)} %get-tuple-element.59), channel_id=1, source_target_pairs={{0,24},{8,16},{16,8},{24,0},{1,25},{9,17},{17,9},{25,1},{2,26},{10... | collective-permute-start | bytes 294920 | tf_op jit(solution)/shard_map/ppermute | solution.py:16
  30.0 0.4 ladders.3
  30.4 0.9 %collective-permute-start.13 = (bf16[384,128]{1,0:T(8,128)(2,1)S(1)}, bf16[384,128]{1,0:T(8,128)(2,1)S(1)}, u32[]{:S(2)}, u32[]{:S(2)}) collective-permute-start(bf16[384,128]{1,0:T(8,128)(2,1)S(1)} %get-tuple-element.61), channel_id=1, source_target_pairs={{0,16},{8,24},{16,0},{24,8},{1,17},{9,25},{17,1},{25,9},{2,18},{10... | collective-permute-start | bytes 294920 | tf_op jit(solution)/shard_map/ppermute | solution.py:16
  31.3 0.6 %collective-permute-start.14 = (bf16[384,128]{1,0:T(8,128)(2,1)S(1)}, bf16[384,128]{1,0:T(8,128)(2,1)S(1)}, u32[]{:S(2)}, u32[]{:S(2)}) collective-permute-start(bf16[384,128]{1,0:T(8,128)(2,1)S(1)} %get-tuple-element.62), channel_id=1, source_target_pairs={{0,8},{8,0},{16,24},{24,16},{1,9},{9,1},{17,25},{25,17},{2,10},{10... | collective-permute-start | bytes 294920 | tf_op jit(solution)/shard_map/ppermute | solution.py:16
  32.1 1.4 %collective-permute-done.12.rest_1_ = bf16[384,128]{1,0:T(8,128)(2,1)S(1)} collective-permute-done((bf16[384,128]{1,0:T(8,128)(2,1)S(1)}, bf16[384,128]{1,0:T(8,128)(2,1)S(1)}, u32[]{:S(2)}, u32[]{:S(2)}) %collective-permute-start.12) | collective-permute-done | bytes 98336 | tf_op jit(solution)/shard_map/ppermute | solution.py:16
  33.5 0.8 %result_start.1.begun = f32[384,1536]{1,0:T(8,128)S(1)} custom-call(bf16[512,1536]{1,0:T(8,128)(2,1)S(1)} %get-tuple-element.49.dense, bf16[384,128]{1,0:T(8,128)(2,1)S(1)} %ladders.2.rest_0_, bf16[384,128]{1,0:T(8,128)(2,1)S(1)} %collective-permute-done.12.rest_1_), custom_call_target="tpu_custom_call" | custom-call | flops 301989888 | tf_op jit(solution)/shard_map/result_start/pallas_call | solution.py:250
  34.3 1.3 %collective-permute-done.13.rest_0_ = bf16[384,128]{1,0:T(8,128)(2,1)S(1)} collective-permute-done((bf16[384,128]{1,0:T(8,128)(2,1)S(1)}, bf16[384,128]{1,0:T(8,128)(2,1)S(1)}, u32[]{:S(2)}, u32[]{:S(2)}) %collective-permute-start.13) | collective-permute-done | bytes 98336 | tf_op jit(solution)/shard_map/ppermute | solution.py:16
  35.5 0.3 collective-permute-done.14.rest_1_
  35.9 1.8 %results.1 = f32[384,1536]{1,0:T(8,128)} custom-call(f32[384,1536]{1,0:T(8,128)S(1)} %result_start.1.begun, bf16[512,1536]{1,0:T(8,128)(2,1)S(1)} %get-tuple-element.49.dense, f32[384,1536]{1,0:T(8,128)S(1)} %get-tuple-element.60.inverse, bf16[384,128]{1,0:T(8,128)(2,1)S(1)} %collective-permute-done.13.rest_0_, ...), custom_call_target="tpu_custom_call" | custom-call | tf_op jit(solution)/shard_map/results/pallas_call | solution.py:284
  (36 shorter events, 1.4 us)
Async XLA Ops:
  0.0 5.0 %collective-permute-start = (bf16[1,16,512]{2,1,0:T(8,128)(2,1)}, bf16[1,16,512]{2,1,0:T(8,128)(2,1)S(1)}, u32[]{:S(2)}, u32[]{:S(2)}) collective-permute-start(bf16[1,16,512]{2,1,0:T(8,128)(2,1)} %bitcast.35), channel_id=1, source_target_pairs={{0,2},{1,3},{2,0},{3,1},{4,6},{5,7},{6,4},{7,5},{8,10},{9,11},{10,... | collective-permute-start | bytes 49160 | tf_op jit(solution)/shard_map/ppermute | solution.py:16
  5.0 5.0 %collective-permute-start.1 = (bf16[2,16,512]{2,1,0:T(8,128)(2,1)S(1)}, bf16[2,16,512]{2,1,0:T(8,128)(2,1)S(1)}, u32[]{:S(2)}, u32[]{:S(2)}) collective-permute-start(bf16[2,16,512]{2,1,0:T(8,128)(2,1)S(1)} %maximum_select_fusion.5), channel_id=1, source_target_pairs={{0,4},{1,5},{2,6},{3,7},{4,0},{5,1},{6,2},{7,3},{8,12},{9,13},{10,... | collective-permute-start | bytes 98312 | tf_op jit(solution)/shard_map/ppermute | solution.py:16
  10.0 6.6 %collective-permute-start.3 = (bf16[4,16,512]{2,1,0:T(8,128)(2,1)S(1)}, bf16[4,16,512]{2,1,0:T(8,128)(2,1)S(1)}, u32[]{:S(2)}, u32[]{:S(2)}) collective-permute-start(bf16[4,16,512]{2,1,0:T(8,128)(2,1)S(1)} %maximum_select_fusion.4), channel_id=1, source_target_pairs={{0,24},{8,16},{16,8},{24,0},{1,25},{9,17},{17,9},{25,1},{2,26},{10... | collective-permute-start | bytes 196616 | tf_op jit(solution)/shard_map/ppermute | solution.py:16
  12.8 4.3 %collective-permute-start.6 = (bf16[4,16,512]{2,1,0:T(8,128)(2,1)S(1)}, bf16[4,16,512]{2,1,0:T(8,128)(2,1)S(1)}, u32[]{:S(2)}, u32[]{:S(2)}) collective-permute-start(bf16[4,16,512]{2,1,0:T(8,128)(2,1)S(1)} %maximum_select_fusion.4), channel_id=1, source_target_pairs={{0,8},{8,0},{16,24},{24,16},{1,9},{9,1},{17,25},{25,17},{2,10},{10... | collective-permute-start | bytes 196616 | tf_op jit(solution)/shard_map/ppermute | solution.py:16
  13.3 4.3 %collective-permute-start.2 = (bf16[4,16,512]{2,1,0:T(8,128)(2,1)S(1)}, bf16[4,16,512]{2,1,0:T(8,128)(2,1)S(1)}, u32[]{:S(2)}, u32[]{:S(2)}) collective-permute-start(bf16[4,16,512]{2,1,0:T(8,128)(2,1)S(1)} %maximum_select_fusion.4), channel_id=1, source_target_pairs={{0,16},{8,24},{16,0},{24,8},{1,17},{9,25},{17,1},{25,9},{2,18},{10... | collective-permute-start | bytes 196616 | tf_op jit(solution)/shard_map/ppermute | solution.py:16
  13.5 1.3 %copy-start = (bf16[1,384,1536]{2,1,0:T(8,128)(2,1)S(1)}, bf16[1,384,1536]{2,1,0:T(8,128)(2,1)}, u32[]{:S(2)}) copy-start(bf16[1,384,1536]{2,1,0:T(8,128)(2,1)} %param.7) | copy-start | bytes 3538948
  14.8 0.7 %copy-start.2 = (s32[4,4]{1,0:T(4,128)S(1)}, s32[4,4]{1,0:T(4,128)}, u32[]{:S(2)}) copy-start(s32[4,4]{1,0:T(4,128)} %screen.3) | copy-start | bytes 196
  16.5 7.1 %copy-start.6 = (f32[1536]{0:T(1024)S(1)}, f32[1536]{0:T(1024)}, u32[]{:S(2)}) copy-start(f32[1536]{0:T(1024)} %param.12) | copy-start | bytes 18436
  16.5 7.3 %copy-start.1 = (bf16[512,128]{1,0:T(8,128)(2,1)S(1)}, bf16[512,128]{1,0:T(8,128)(2,1)}, u32[]{:S(2)}) copy-start(bf16[512,128]{1,0:T(8,128)(2,1)} %rest_4_.1) | copy-start | bytes 393220
  16.6 7.3 %copy-start.3 = (s32[4,4]{1,0:T(4,128)S(1)}, s32[4,4]{1,0:T(4,128)}, u32[]{:S(2)}) copy-start(s32[4,4]{1,0:T(4,128)} %screen.3) | copy-start | bytes 196
  16.6 7.3 %copy-start.4 = (f32[300]{0:T(512)S(1)}, f32[300]{0:T(512)}, u32[]{:S(2)}) copy-start(f32[300]{0:T(512)} %occ_energy.1) | copy-start | bytes 3604
  16.6 7.3 %copy-start.5 = (s32[1,2]{1,0:T(1,128)S(1)}, s32[1,2]{1,0:T(1,128)}, u32[]{:S(2)}) copy-start(s32[1,2]{1,0:T(1,128)} %pair_occ.1) | copy-start | bytes 28
  17.1 1.3 %collective-permute-start.7 = (bf16[4,16,512]{2,1,0:T(8,128)(2,1)S(1)}, bf16[4,16,512]{2,1,0:T(8,128)(2,1)S(1)}, u32[]{:S(2)}, u32[]{:S(2)}) collective-permute-start(bf16[4,16,512]{2,1,0:T(8,128)(2,1)S(1)} %collective-permute-done.6), channel_id=1, source_target_pairs={{0,1},{1,0},{2,3},{3,2},{4,5},{5,4},{6,7},{7,6},{8,9},{9,8},{10,11... | collective-permute-start | bytes 196616 | tf_op jit(solution)/shard_map/ppermute | solution.py:16
  17.1 1.4 %collective-permute-start.4 = (bf16[4,16,512]{2,1,0:T(8,128)(2,1)S(1)}, bf16[4,16,512]{2,1,0:T(8,128)(2,1)S(1)}, u32[]{:S(2)}, u32[]{:S(2)}) collective-permute-start(bf16[4,16,512]{2,1,0:T(8,128)(2,1)S(1)} %collective-permute-done.3), channel_id=1, source_target_pairs={{0,1},{1,0},{2,3},{3,2},{4,5},{5,4},{6,7},{7,6},{8,9},{9,8},{10,11... | collective-permute-start | bytes 196616 | tf_op jit(solution)/shard_map/ppermute | solution.py:16
  17.6 1.6 %collective-permute-start.8 = (bf16[4,16,512]{2,1,0:T(8,128)(2,1)S(1)}, bf16[4,16,512]{2,1,0:T(8,128)(2,1)S(1)}, u32[]{:S(2)}, u32[]{:S(2)}) collective-permute-start(bf16[4,16,512]{2,1,0:T(8,128)(2,1)S(1)} %collective-permute-done.2), channel_id=1, source_target_pairs={{0,1},{1,0},{2,3},{3,2},{4,5},{5,4},{6,7},{7,6},{8,9},{9,8},{10,11... | collective-permute-start | bytes 196616 | tf_op jit(solution)/shard_map/ppermute | solution.py:16
  18.8 4.5 %collective-permute-start.5 = (bf16[4,16,512]{2,1,0:T(8,128)(2,1)S(1)}, bf16[4,16,512]{2,1,0:T(8,128)(2,1)S(1)}, u32[]{:S(2)}, u32[]{:S(2)}) collective-permute-start(bf16[4,16,512]{2,1,0:T(8,128)(2,1)S(1)} %maximum_select_fusion.4), channel_id=1, source_target_pairs={{0,1},{1,0},{2,3},{3,2},{4,5},{5,4},{6,7},{7,6},{8,9},{9,8},{10,11... | collective-permute-start | bytes 196616 | tf_op jit(solution)/shard_map/ppermute | solution.py:16
  19.3 6.0 %collective-permute-start.9 = (bf16[128,384]{1,0:T(8,128)(2,1)S(1)}, bf16[128,384]{1,0:T(8,128)(2,1)S(1)}, u32[]{:S(2)}, u32[]{:S(2)}) collective-permute-start(bf16[128,384]{1,0:T(8,128)(2,1)S(1)} %half_products.3), channel_id=1, source_target_pairs={{0,24},{8,16},{16,8},{24,0},{1,25},{9,17},{17,9},{25,1},{2,26},{10... | collective-permute-start | bytes 294920 | tf_op jit(solution)/shard_map/ppermute | solution.py:16
  22.1 5.1 %collective-permute-start.10 = (bf16[128,384]{1,0:T(8,128)(2,1)S(1)}, bf16[128,384]{1,0:T(8,128)(2,1)S(1)}, u32[]{:S(2)}, u32[]{:S(2)}) collective-permute-start(bf16[128,384]{1,0:T(8,128)(2,1)S(1)} %get-tuple-element.56), channel_id=1, source_target_pairs={{0,16},{8,24},{16,0},{24,8},{1,17},{9,25},{17,1},{25,9},{2,18},{10... | collective-permute-start | bytes 294920 | tf_op jit(solution)/shard_map/ppermute | solution.py:16
  22.7 4.6 %collective-permute-start.11 = (bf16[128,384]{1,0:T(8,128)(2,1)S(1)}, bf16[128,384]{1,0:T(8,128)(2,1)S(1)}, u32[]{:S(2)}, u32[]{:S(2)}) collective-permute-start(bf16[128,384]{1,0:T(8,128)(2,1)S(1)} %get-tuple-element.57), channel_id=1, source_target_pairs={{0,8},{8,0},{16,24},{24,16},{1,9},{9,1},{17,25},{25,17},{2,10},{10... | collective-permute-start | bytes 294920 | tf_op jit(solution)/shard_map/ppermute | solution.py:16
  27.9 5.7 %collective-permute-start.12 = (bf16[384,128]{1,0:T(8,128)(2,1)S(1)}, bf16[384,128]{1,0:T(8,128)(2,1)S(1)}, u32[]{:S(2)}, u32[]{:S(2)}) collective-permute-start(bf16[384,128]{1,0:T(8,128)(2,1)S(1)} %get-tuple-element.59), channel_id=1, source_target_pairs={{0,24},{8,16},{16,8},{24,0},{1,25},{9,17},{17,9},{25,1},{2,26},{10... | collective-permute-start | bytes 294920 | tf_op jit(solution)/shard_map/ppermute | solution.py:16
  30.4 5.2 %collective-permute-start.13 = (bf16[384,128]{1,0:T(8,128)(2,1)S(1)}, bf16[384,128]{1,0:T(8,128)(2,1)S(1)}, u32[]{:S(2)}, u32[]{:S(2)}) collective-permute-start(bf16[384,128]{1,0:T(8,128)(2,1)S(1)} %get-tuple-element.61), channel_id=1, source_target_pairs={{0,16},{8,24},{16,0},{24,8},{1,17},{9,25},{17,1},{25,9},{2,18},{10... | collective-permute-start | bytes 294920 | tf_op jit(solution)/shard_map/ppermute | solution.py:16
  31.3 4.6 %collective-permute-start.14 = (bf16[384,128]{1,0:T(8,128)(2,1)S(1)}, bf16[384,128]{1,0:T(8,128)(2,1)S(1)}, u32[]{:S(2)}, u32[]{:S(2)}) collective-permute-start(bf16[384,128]{1,0:T(8,128)(2,1)S(1)} %get-tuple-element.62), channel_id=1, source_target_pairs={{0,8},{8,0},{16,24},{24,16},{1,9},{9,1},{17,25},{25,17},{2,10},{10... | collective-permute-start | bytes 294920 | tf_op jit(solution)/shard_map/ppermute | solution.py:16
